TPU v7x, 32 devices: a whole 2x2x4 slice. The times are simulated.
32 devices in a mesh: seq: 16 (over z, x, core), batch: 2 (over y).
Axes of the slice: x: 2, y: 2, z: 4, core: 2. Of those that a mesh axis runs over, the one named last changes fastest.
Arguments:
- inputs: bfloat16 [2, 2048, 1024], P('batch', 'seq'), may hold values from -6 to 6
- lengths: int32 [2, 8], P('batch'), may hold values from 64 to 1599, as said below
- proj_query: bfloat16 [1024, 1024], replicated, may hold values from -0.1875 to 0.1875
- proj_latent: bfloat16 [1024, 512], replicated, may hold values from -0.1875 to 0.1875
- proj_expand: bfloat16 [256, 256], replicated, may hold values from -0.375 to 0.375
- proj_output: bfloat16 [1024, 1024], replicated, may hold values from -1.5 to 1.5
- ffn_gate: bfloat16 [1024, 2816], replicated, may hold values from -0.1875 to 0.1875
- ffn_up: bfloat16 [1024, 2816], replicated, may hold values from -0.1875 to 0.1875
- ffn_down: bfloat16 [2816, 1024], replicated, may hold values from -0.109375 to 0.109375
- norm_attn: bfloat16 [1024], replicated, may hold values from 0.099609375 to 1.8984375
- norm_ffn: bfloat16 [1024], replicated, may hold values from 0.099609375 to 1.8984375
- cotangent: bfloat16 [2, 2048, 1024], P('batch', 'seq'), may hold values from -6 to 6
Outputs:
- output: bfloat16 [2, 2048, 1024], P('batch', 'seq')
- input_grad: bfloat16 [2, 2048, 1024], P('batch', 'seq')
- grad_query: float32 [1024, 1024], P('seq')
- grad_latent: float32 [1024, 512], P('seq')
- grad_expand: float32 [256, 256], P(None, 'seq')
- grad_output: float32 [1024, 1024], P('seq')
- grad_gate: float32 [1024, 2816], P('seq')
- grad_up: float32 [1024, 2816], P('seq')
- grad_down: float32 [2816, 1024], P(None, 'seq')
- grad_norm_attn: float32 [1024], P('seq')
- grad_norm_ffn: float32 [1024], P('seq')
Inputs may be any that keep to these rules, and one draw needn't show every extreme that they name: `lengths`: in each bucket the first document is the longest; the other 7 documents have 128 // 2 to 73 positions; 1 to 16 positions at the end of a bucket are padding.
All inputs are finite; a program needn't handle non-finite values.
Results may differ from a plain program's by a relative error of at most 0.015.
Values may be sent and summed in bfloat16 or wider, within the bound.
No kernel may reach another device: no remote copies, remote signals or barrier semaphores. Data moves between devices by JAX's collectives and lax.ppermute only.
A program may use at most 192 MiB of HBM per device.

v0:
```python
import jax
import jax.numpy as jnp
from jax import lax
from jax.sharding import PartitionSpec as P

HEADS = 16
HD = 64
GROUPS = 2
LAT = 256
DOCS = 8


eps = 1e-05
scale = 0.125
masked = -1e30


def doc_numbers(lengths_row, count):
    ends = jnp.cumsum(lengths_row)
    places = jnp.arange(count, dtype=jnp.int32)
    return jnp.sum((places[:, None] >= ends[None, :]).astype(jnp.int32), axis=1)


def inner(left, right):
    return jnp.dot(left, right, preferred_element_type=jnp.float32)


def outer(left, right):
    return lax.dot_general(
        left, right, (((0,), (0,)), ((), ())), preferred_element_type=jnp.float32
    )


def across(left, right):
    return lax.dot_general(
        left, right, (((1,), (1,)), ((), ())), preferred_element_type=jnp.float32
    )


def expand(latent, proj_expand):
    width = 2 * HD
    pieces = [
        inner(latent[:, g * LAT : (g + 1) * LAT], proj_expand[:, g * width : (g + 1) * width])
        for g in range(GROUPS)
    ]
    return jnp.concatenate(pieces, axis=1).astype(jnp.bfloat16)


def norm_forward(hidden, gain):
    inverse = lax.rsqrt(jnp.mean(hidden * hidden, axis=-1, keepdims=True) + eps)
    return (hidden * inverse * gain, inverse)


def norm_backward(hidden, gain, inverse, grad):
    scaled = grad * gain
    gain_grad = jnp.sum(grad * hidden * inverse, axis=0)
    cubed = inverse * inverse * inverse
    hidden_grad = inverse * scaled - hidden * cubed * jnp.mean(
        scaled * hidden, axis=-1, keepdims=True
    )
    return (hidden_grad, gain_grad)


def allowed_mask(query_docs, query_places, key_docs, key_places):
    same = (
        (query_docs[:, None] == key_docs[None, :])
        & (key_places[None, :] <= query_places[:, None])
        & (query_docs[:, None] < DOCS)
    )
    return same | (key_places[None, :] == query_places[:, None])


def shards(
    inputs,
    lengths,
    proj_query,
    proj_latent,
    proj_expand,
    proj_output,
    ffn_gate,
    ffn_up,
    ffn_down,
    norm_attn,
    norm_ffn,
    cotangent,
):
    tok = inputs.shape[1]
    seq_len = tok * lax.axis_size("seq")
    per_group = HEADS // GROUPS
    hidden = inputs[0].astype(jnp.float32)
    gain_attn = norm_attn.astype(jnp.float32)
    gain_ffn = norm_ffn.astype(jnp.float32)
    all_docs = doc_numbers(lengths[0], seq_len)
    first = lax.axis_index("seq") * tok
    query_places = first + jnp.arange(tok, dtype=jnp.int32)
    query_docs = lax.dynamic_slice_in_dim(all_docs, first, tok)
    block = 1024
    count = seq_len // block
    doc_blocks = all_docs.reshape(count, block)
    place_blocks = jnp.arange(seq_len, dtype=jnp.int32).reshape(count, block)
    normed, inverse_attn = norm_forward(hidden, gain_attn)
    normed_low = normed.astype(jnp.bfloat16)
    queries = inner(normed_low, proj_query).astype(jnp.bfloat16)
    latent = inner(normed_low, proj_latent).astype(jnp.bfloat16)
    query_heads = queries.reshape(tok, GROUPS, per_group, HD)
    kv_all = expand(lax.all_gather(latent, "seq", axis=0, tiled=True), proj_expand)

    def scores(kv_block, doc_block, place_block):
        split = kv_block.reshape(block, GROUPS, 2, HD)
        keys = split[:, :, 0]
        values = split[:, :, 1]
        raw = (
            jnp.einsum("bghd,kgd->ghbk", query_heads, keys, preferred_element_type=jnp.float32)
            * scale
        )
        allowed = allowed_mask(query_docs, query_places, doc_block, place_block)[None, None]
        return (raw, allowed, keys, values)

    def top_step(carry, blocks):
        top, total = carry
        raw, allowed, keys, values = scores(blocks[0], blocks[1], blocks[2])
        held = jnp.where(allowed, raw, masked)
        new_top = jnp.maximum(top, jnp.max(held, axis=-1))
        expo = jnp.where(allowed, jnp.exp(held - new_top[..., None]), 0.0)
        total = total * jnp.exp(top - new_top) + jnp.sum(expo, axis=-1)
        return ((new_top, total), None)

    kv_blocks = kv_all.reshape(count, block, GROUPS * 2 * HD)
    start = (
        jnp.full((GROUPS, per_group, tok), masked, jnp.float32),
        jnp.zeros((GROUPS, per_group, tok), jnp.float32),
    )
    (top, total), unused = lax.scan(top_step, start, (kv_blocks, doc_blocks, place_blocks))
    log_total = top + jnp.log(total)

    def out_step(acc, blocks):
        raw, allowed, keys, values = scores(blocks[0], blocks[1], blocks[2])
        probs = jnp.where(allowed, jnp.exp(raw - log_total[..., None]), 0.0).astype(jnp.bfloat16)
        return (
            acc + jnp.einsum("ghbk,kgd->bghd", probs, values, preferred_element_type=jnp.float32),
            None,
        )

    attended, unused = lax.scan(
        out_step,
        jnp.zeros((tok, GROUPS, per_group, HD), jnp.float32),
        (kv_blocks, doc_blocks, place_blocks),
    )
    attended_low = attended.reshape(tok, HEADS * HD).astype(jnp.bfloat16)
    middle = hidden + inner(attended_low, proj_output)
    normed_two, inverse_ffn = norm_forward(middle, gain_ffn)
    normed_two_low = normed_two.astype(jnp.bfloat16)
    gate = inner(normed_two_low, ffn_gate)
    upper = inner(normed_two_low, ffn_up)
    sigma = jax.nn.sigmoid(gate)
    swish = gate * sigma
    activ_low = (swish * upper).astype(jnp.bfloat16)
    output = (middle + inner(activ_low, ffn_down)).astype(jnp.bfloat16)
    grad_out = cotangent[0].astype(jnp.float32)
    grad_out_low = grad_out.astype(jnp.bfloat16)
    grad_down = outer(activ_low, grad_out_low)
    d_activ = across(grad_out_low, ffn_down)
    d_gate = (d_activ * upper * sigma * (1.0 + gate * (1.0 - sigma))).astype(jnp.bfloat16)
    d_upper = (d_activ * swish).astype(jnp.bfloat16)
    grad_gate = outer(normed_two_low, d_gate)
    grad_up = outer(normed_two_low, d_upper)
    d_normed_two = across(d_gate, ffn_gate) + across(d_upper, ffn_up)
    d_middle, grad_norm_ffn = norm_backward(middle, gain_ffn, inverse_ffn, d_normed_two)
    d_middle = d_middle + grad_out
    d_middle_low = d_middle.astype(jnp.bfloat16)
    grad_output = outer(attended_low, d_middle_low)
    d_attended = across(d_middle_low, proj_output).astype(jnp.bfloat16)
    d_heads = d_attended.reshape(tok, GROUPS, per_group, HD)
    row_dots = jnp.einsum("bghd,bghd->ghb", d_heads.astype(jnp.float32), attended)
    kv_back = lax.all_gather(expand(latent, proj_expand), "seq", axis=0, tiled=True).reshape(
        count, block, GROUPS * 2 * HD
    )

    def back_step(d_query, blocks):
        raw, allowed, keys, values = scores(blocks[0], blocks[1], blocks[2])
        probs = jnp.where(allowed, jnp.exp(raw - log_total[..., None]), 0.0)
        probs_low = probs.astype(jnp.bfloat16)
        d_probs = jnp.einsum("bghd,kgd->ghbk", d_heads, values, preferred_element_type=jnp.float32)
        d_raw = (probs * (d_probs - row_dots[..., None])).astype(jnp.bfloat16)
        d_query = (
            d_query
            + jnp.einsum("ghbk,kgd->bghd", d_raw, keys, preferred_element_type=jnp.float32) * scale
        )
        d_keys = (
            jnp.einsum("ghbk,bghd->kgd", d_raw, query_heads, preferred_element_type=jnp.float32)
            * scale
        )
        d_values = jnp.einsum(
            "ghbk,bghd->kgd", probs_low, d_heads, preferred_element_type=jnp.float32
        )
        return (d_query, jnp.stack([d_keys, d_values], axis=2).reshape(block, GROUPS * 2 * HD))

    d_query, kv_terms = lax.scan(
        back_step,
        jnp.zeros((tok, GROUPS, per_group, HD), jnp.float32),
        (kv_back, doc_blocks, place_blocks),
    )
    width = 2 * HD
    kv_flat = kv_terms.reshape(seq_len, GROUPS * width)
    arrived = lax.all_to_all(
        kv_flat.astype(jnp.bfloat16), "seq", split_axis=0, concat_axis=0, tiled=True
    ).astype(kv_flat.dtype)
    kv_grads = jnp.sum(arrived.reshape(-1, tok, GROUPS * width), axis=0).astype(jnp.bfloat16)
    d_query_low = d_query.reshape(tok, HEADS * HD).astype(jnp.bfloat16)
    grad_query = outer(normed_low, d_query_low)
    grad_expand = jnp.concatenate(
        [
            outer(latent[:, g * LAT : (g + 1) * LAT], kv_grads[:, g * width : (g + 1) * width])
            for g in range(GROUPS)
        ],
        axis=1,
    )
    d_latent = jnp.concatenate(
        [
            across(
                kv_grads[:, g * width : (g + 1) * width],
                proj_expand[:, g * width : (g + 1) * width],
            )
            for g in range(GROUPS)
        ],
        axis=1,
    )
    d_latent_low = d_latent.astype(jnp.bfloat16)
    grad_latent = outer(normed_low, d_latent_low)
    d_normed = across(d_query_low, proj_query) + across(d_latent_low, proj_latent)
    d_hidden, grad_norm_attn = norm_backward(hidden, gain_attn, inverse_attn, d_normed)
    input_grad = (d_hidden + d_middle).astype(jnp.bfloat16)
    shares = (
        lax.psum_scatter(grad_query, "seq", scatter_dimension=0, tiled=True),
        lax.psum_scatter(grad_latent, "seq", scatter_dimension=0, tiled=True),
        lax.psum_scatter(grad_expand, "seq", scatter_dimension=1, tiled=True),
        lax.psum_scatter(grad_output, "seq", scatter_dimension=0, tiled=True),
        lax.psum_scatter(grad_gate, "seq", scatter_dimension=0, tiled=True),
        lax.psum_scatter(grad_up, "seq", scatter_dimension=0, tiled=True),
        lax.psum_scatter(grad_down, "seq", scatter_dimension=1, tiled=True),
        lax.psum_scatter(grad_norm_attn, "seq", scatter_dimension=0, tiled=True),
        lax.psum_scatter(grad_norm_ffn, "seq", scatter_dimension=0, tiled=True),
    )
    sums = (
        lax.psum(shares[0].astype(jnp.bfloat16), "batch").astype(jnp.float32),
        lax.psum(shares[1].astype(jnp.bfloat16), "batch").astype(jnp.float32),
        lax.psum(shares[2].astype(jnp.bfloat16), "batch").astype(jnp.float32),
        lax.psum(shares[3].astype(jnp.bfloat16), "batch").astype(jnp.float32),
        lax.psum(shares[4].astype(jnp.bfloat16), "batch").astype(jnp.float32),
        lax.psum(shares[5].astype(jnp.bfloat16), "batch").astype(jnp.float32),
        lax.psum(shares[6].astype(jnp.bfloat16), "batch").astype(jnp.float32),
        lax.psum(shares[7].astype(jnp.bfloat16), "batch").astype(jnp.float32),
        lax.psum(shares[8].astype(jnp.bfloat16), "batch").astype(jnp.float32),
    )
    return (
        output[None],
        input_grad[None],
        sums[0],
        sums[1],
        sums[2],
        sums[3],
        sums[4],
        sums[5],
        sums[6],
        sums[7],
        sums[8],
    )


def solution(mesh):
    return jax.shard_map(
        shards,
        mesh=mesh,
        in_specs=(
            P("batch", "seq", None),
            P("batch", None),
            P(),
            P(),
            P(),
            P(),
            P(),
            P(),
            P(),
            P(),
            P(),
            P("batch", "seq", None),
        ),
        out_specs=(
            P("batch", "seq", None),
            P("batch", "seq", None),
            P("seq", None),
            P("seq", None),
            P(None, "seq"),
            P("seq", None),
            P("seq", None),
            P("seq", None),
            P(None, "seq"),
            P("seq"),
            P("seq"),
        ),
        check_vma=False,
    )
```

profile of v0, /device:TPU:0, one launch (start us, length us, event | category | flops | bytes accessed | tf_op | source)
XLA Modules:
  0.0 934.9 jit_solution(5289468852770768460)
XLA Ops:
  17.9 2.2 convolution_convert_fusion.3
  20.3 33.6 %all-gather.5.cloned.1.call-done = bf16[2048,256]{0,1:T(8,128)(2,1)} async-done(((bf16[128,256]{0,1:T(8,128)(2,1)}), bf16[2048,256]{0,1:T(8,128)(2,1)}) %all-gather.5.cloned.1.call-update) | async-done | bytes 1048592 | tf_op jit(solution)/shard_map/all_gather | solution.py:175
  53.9 2.3 copy.127
  56.2 41.4 %all-gather.3.cloned.1.call-done = bf16[2048,512]{1,0:T(8,128)(2,1)} async-done(((bf16[128,512]{1,0:T(8,128)(2,1)}), bf16[2048,512]{1,0:T(8,128)(2,1)}) %all-gather.3.cloned.1.call-update) | async-done | bytes 2097168 | tf_op jit(solution)/shard_map/all_gather | solution.py:106
  104.2 10.2 %while.37 = (s32[]{:T(128)}, f32[2,8,128]{2,1,0:T(8,128)S(1)}, f32[2,8,128]{2,1,0:T(8,128)S(1)}, s32[128]{0:T(128)}, s32[2,1024]{1,0:T(2,128)S(1)}, /*index=5*/s...) while((s32[]{:T(128)}, f32[2,8,128]{2,1,0:T(8,128)S(1)}, ...), condition=%wide.region_6.7_spmd.clone, body=%wide.region_3.6_spmd.clone.sunk | while | flops 286009600 | bytes 18876812 | solution.py:133
  107.3 2.0 select_reduce_fusion.2
  115.1 13.5 %while.38 = (s32[]{:T(128)}, f32[128,2,8,64]{0,3,2,1:T(8,128)}, bf16[2,1024,256]{1,2,0:T(8,128)(2,1)S(1)}, s32[128]{0:T(128)}, s32[2,1024]{1,0:T(2,128)S(1)}, /*...) while((s32[]{:T(128)}, f32[128,2,8,64]{0,3,2,1:T(8,128)}, ...), condition=%wide.region_8.9_spmd.clone, body=%wide.region_7.8_spmd.clone.sunk | while | flops 546308352 | bytes 3180939 | solution.py:144
  117.6 4.1 fusion.164
  124.2 4.3 fusion.164
  133.1 3.7 fusion.102
  137.9 3.2 multiply_convert_fusion
  143.1 2.6 multiply_reduce_fusion
  148.9 24.2 %while.39 = (s32[]{:T(128)}, f32[128,2,8,64]{0,3,2,1:T(8,128)S(1)}, bf16[2,1024,256]{2,1,0:T(8,128)(2,1)}, bf16[2,1024,256]{1,2,0:T(8,128)(2,1)}, s32[128]{0:T(1...) while((s32[]{:T(128)}, f32[128,2,8,64]{0,3,2,1:T(8,128)S(1)}, ...), condition=%wide.region_12.13_spmd.clone, body=%wide.region_11.12_spmd.clone.sunk | while | flops 1364852992 | bytes 46844324 | solution.py:198
  154.9 2.8 fusion.173
  166.9 2.8 fusion.173
  173.1 28.5 %all_to_all.6 = bf16[16,128,256]{2,1,0:T(8,128)(2,1)S(1)} all-to-all(bf16[16,128,256]{2,1,0:T(8,128)(2,1)} %bitcast.316), channel_id=1, replica_groups=mesh['seq'=16,'batch'=2] {'seq'}, dimensions={0} | all-to-all | bytes 2097152 | tf_op jit(solution)/shard_map/all_to_all | solution.py:205
  204.1 2.7 fusion.76
  206.9 2.8 fusion.67
  209.8 5.9 fusion.106
  216.8 6.0 fusion.105
  224.0 5.9 fusion.70
  233.2 32.7 %reduce-scatter.10.cloned.1.call-done = f32[64,512]{1,0:T(8,128)} async-done(((f32[1024,512]{1,0:T(8,128)}), f32[64,512]{1,0:T(8,128)}) %reduce-scatter.10.cloned.1.call-update) | async-done | bytes 131088 | tf_op jit(solution)/shard_map/reduce_scatter | solution.py:235
  267.5 74.2 %reduce-scatter.14.cloned.1.call-done = f32[64,1024]{1,0:T(8,128)} async-done(((f32[1024,1024]{1,0:T(8,128)}), f32[64,1024]{1,0:T(8,128)}) %reduce-scatter.14.cloned.1.call-update) | async-done | bytes 262160 | tf_op jit(solution)/shard_map/reduce_scatter | solution.py:237
  343.3 73.5 %reduce-scatter.8.cloned.1.call-done = f32[64,1024]{1,0:T(8,128)} async-done(((f32[1024,1024]{1,0:T(8,128)}), f32[64,1024]{1,0:T(8,128)}) %reduce-scatter.8.cloned.1.call-update) | async-done | bytes 262160 | tf_op jit(solution)/shard_map/reduce_scatter | solution.py:234
  418.3 128.3 %reduce-scatter.18.cloned.1.call-done = f32[64,2816]{1,0:T(8,128)} async-done(((f32[1024,2816]{1,0:T(8,128)}), f32[64,2816]{1,0:T(8,128)}) %reduce-scatter.18.cloned.1.call-update) | async-done | bytes 720912 | tf_op jit(solution)/shard_map/reduce_scatter | solution.py:239
  548.5 128.3 %reduce-scatter.16.cloned.1.call-done = f32[64,2816]{1,0:T(8,128)} async-done(((f32[1024,2816]{1,0:T(8,128)}), f32[64,2816]{1,0:T(8,128)}) %reduce-scatter.16.cloned.1.call-update) | async-done | bytes 720912 | tf_op jit(solution)/shard_map/reduce_scatter | solution.py:238
  678.7 128.8 %reduce-scatter.20.cloned.1.call-done = f32[2816,64]{0,1:T(8,128)} async-done(((f32[2816,1024]{0,1:T(8,128)}), f32[2816,64]{0,1:T(8,128)}) %reduce-scatter.20.cloned.1.call-update) | async-done | bytes 720912 | tf_op jit(solution)/shard_map/reduce_scatter | solution.py:240
  810.3 4.6 fusion.45
  815.5 32.9 %all-reduce.2 = (bf16[1024]{0:T(1024)(128)(2,1)S(1)}, bf16[1024]{0:T(1024)(128)(2,1)S(1)}) all-reduce(f32[1024]{0:T(1024)S(1)} %get-tuple-element.362, f32[1024]{0:T(1024)S(1)} %copy-done.32), channel_id=9, replica_groups=mesh['seq'=16,'batch'=2] {'seq'}, use_global_device_ids=true, to_apply=%region_30.31.clone | all-reduce | flops 2048 | bytes 12288
  850.5 16.1 %reduce-scatter.12.cloned.1.call-done = f32[256,16]{0,1:T(8,128)} async-done(((f32[256,256]{0,1:T(8,128)}), f32[256,16]{0,1:T(8,128)}) %reduce-scatter.12.cloned.1.call-update) | async-done | bytes 16400 | tf_op jit(solution)/shard_map/reduce_scatter | solution.py:236
  867.4 5.0 all-reduce.3
  874.1 43.6 %all-reduce.7.cloned.1.call-done = (bf16[64,1024]{1,0:T(8,128)(2,1)}, bf16[64,512]{1,0:T(8,128)(2,1)}, bf16[64,1024]{1,0:T(8,128)(2,1)}, bf16[64,2816]{1,0:T(8,1...) async-done(((bf16[64,1024]{1,0:T(8,128)(2,1)}, bf16[64,512]{1,0:T(8,128)(2,1)}, bf16[64,1024]{1,0:T(8,128)(2,1)}, bf16[64,2816]{1,0:T(8,128)(2,1)}, ...) | async-done | bytes 1409040 | tf_op jit(solution)/shard_map/psum | solution.py:245
  (229 shorter events, 94.1 us)
Async XLA Ops:
  7.2 122.5 %copy-start = (bf16[1024,1024]{1,0:T(8,128)(2,1)S(1)}, bf16[1024,1024]{1,0:T(8,128)(2,1)}, u32[]{:S(2)}) copy-start(bf16[1024,1024]{1,0:T(8,128)(2,1)} %param.23) | copy-start | bytes 6291460
  7.2 90.4 %copy-start.23 = (bf16[256,256]{1,0:T(8,128)(2,1)S(1)}, bf16[256,256]{1,0:T(8,128)(2,1)}, u32[]{:S(2)}) copy-start(bf16[256,256]{1,0:T(8,128)(2,1)} %param.22) | copy-start | bytes 393220
  7.2 46.7 %all-gather.5.cloned.1.call-start = ((), (), s32[]{:S(2)}) async-start(), calls=%async_computation.9 | async-start | bytes 1114112 | tf_op jit(solution)/shard_map/all_gather | solution.py:175
  9.0 92.9 %copy-start.29 = (f32[128]{0:T(128)}, f32[128]{0:T(128)S(1)}, u32[]{:S(2)}) copy-start(f32[128]{0:T(128)S(1)} %get-tuple-element.447) | copy-start | bytes 1540
  9.7 92.2 %copy-start.25 = (f32[1024]{0:T(1024)}, f32[1024]{0:T(1024)S(1)}, u32[]{:S(2)}) copy-start(f32[1024]{0:T(1024)S(1)} %convert_element_type.153) | copy-start | bytes 12292
  14.2 83.3 %all-gather.3.cloned.1.call-start = ((), (), s32[]{:S(2)}) async-start(), calls=%async_computation.8 | async-start | bytes 2228224 | tf_op jit(solution)/shard_map/all_gather | solution.py:106
  15.0 250.9 %reduce-scatter.10.cloned.1.call-start = ((), (), s32[]{:S(2)}) async-start(), calls=%async_computation.11 | async-start | bytes 2228224 | tf_op jit(solution)/shard_map/reduce_scatter | solution.py:235
  129.7 7.2 slice-start
  129.7 8.2 slice-start.4
  131.3 14.4 %copy-start.4 = (f32[128,1024]{1,0:T(8,128)}, f32[128,1024]{1,0:T(8,128)S(1)}, u32[]{:S(2)}) copy-start(f32[128,1024]{1,0:T(8,128)S(1)} %get-tuple-element.451) | copy-start | bytes 1572868
  136.9 6.2 slice-start.2
  143.1 5.8 copy-start.2
  143.1 5.8 copy-start.33
  148.9 52.9 %copy-start.24 = (bf16[256,256]{1,0:T(8,128)(2,1)S(1)}, bf16[256,256]{1,0:T(8,128)(2,1)}, u32[]{:S(2)}) copy-start(bf16[256,256]{1,0:T(8,128)(2,1)} %param.22) | copy-start | bytes 393220
  148.9 53.2 %copy-start.3 = (bf16[1,128,1024]{2,1,0:T(8,128)(2,1)S(1)}, bf16[1,128,1024]{2,1,0:T(8,128)(2,1)}, u32[]{:S(2)}) copy-start(bf16[1,128,1024]{2,1,0:T(8,128)(2,1)} %param.18) | copy-start | bytes 786436
  148.9 53.2 %copy-start.26 = (f32[1024]{0:T(1024)S(1)}, f32[1024]{0:T(1024)}, u32[]{:S(2)}) copy-start(f32[1024]{0:T(1024)} %copy-done.25) | copy-start | bytes 12292
  148.9 53.2 %copy-start.30 = (f32[128]{0:T(128)S(1)}, f32[128]{0:T(128)}, u32[]{:S(2)}) copy-start(f32[128]{0:T(128)} %copy-done.29) | copy-start | bytes 1540
  173.1 31.0 %copy-start.8 = (f32[128,1024]{1,0:T(8,128)S(1)}, f32[128,1024]{1,0:T(8,128)}, u32[]{:S(2)}) copy-start(f32[128,1024]{1,0:T(8,128)} %copy-done.7) | copy-start | bytes 1572868
  173.1 31.0 %copy-start.16 = (bf16[128,2,8,64]{0,3,2,1:T(8,128)(2,1)S(1)}, bf16[128,2,8,64]{0,3,2,1:T(8,128)(2,1)}, u32[]{:S(2)}) copy-start(bf16[128,2,8,64]{0,3,2,1:T(8,128)(2,1)} %copy-done.15) | copy-start | bytes 786436
  204.0 137.6 %reduce-scatter.14.cloned.1.call-start = ((), (), s32[]{:S(2)}) async-start(), calls=%async_computation.13 | async-start | bytes 4456448 | tf_op jit(solution)/shard_map/reduce_scatter | solution.py:237
  206.8 209.9 %reduce-scatter.8.cloned.1.call-start = ((), (), s32[]{:S(2)}) async-start(), calls=%async_computation.10 | async-start | bytes 4456448 | tf_op jit(solution)/shard_map/reduce_scatter | solution.py:234
  209.7 336.9 %reduce-scatter.18.cloned.1.call-start = ((), (), s32[]{:S(2)}) async-start(), calls=%async_computation.15 | async-start | bytes 12255232 | tf_op jit(solution)/shard_map/reduce_scatter | solution.py:239
  215.7 461.1 %reduce-scatter.16.cloned.1.call-start = ((), (), s32[]{:S(2)}) async-start(), calls=%async_computation.14 | async-start | bytes 12255232 | tf_op jit(solution)/shard_map/reduce_scatter | solution.py:238
  222.8 584.7 %reduce-scatter.20.cloned.1.call-start = ((), (), s32[]{:S(2)}) async-start(), calls=%async_computation.16 | async-start | bytes 12255232 | tf_op jit(solution)/shard_map/reduce_scatter | solution.py:240
  229.9 579.5 %copy-start.6 = (bf16[1024,1024]{1,0:T(8,128)(2,1)S(1)}, bf16[1024,1024]{1,0:T(8,128)(2,1)}, u32[]{:S(2)}) copy-start(bf16[1024,1024]{1,0:T(8,128)(2,1)} %param.20) | copy-start | bytes 6291460
  229.9 580.4 %copy-start.5 = (f32[128,1024]{1,0:T(8,128)S(1)}, f32[128,1024]{1,0:T(8,128)}, u32[]{:S(2)}) copy-start(f32[128,1024]{1,0:T(8,128)} %copy-done.4) | copy-start | bytes 1572868
  229.9 636.8 %reduce-scatter.12.cloned.1.call-start = ((), (), s32[]{:S(2)}) async-start(), calls=%async_computation.12 | async-start | bytes 278528 | tf_op jit(solution)/shard_map/reduce_scatter | solution.py:236
  231.9 685.7 %all-reduce.7.cloned.1.call-start = ((), (), s32[]{:S(2)}) async-start(), calls=%async_computation.17 | async-start | bytes 2818048 | tf_op jit(solution)/shard_map/psum | solution.py:245
  809.4 5.6 copy-start.31
  809.4 6.1 copy-start.32
  809.4 39.2 %copy-start.34 = (f32[128]{0:T(128)S(1)}, f32[128]{0:T(128)}, u32[]{:S(2)}) copy-start(f32[128]{0:T(128)} %get-tuple-element.446) | copy-start | bytes 1540
  810.3 117.8 %copy-start.1 = (bf16[1024,1024]{1,0:T(8,128)(2,1)S(1)}, bf16[1024,1024]{1,0:T(8,128)(2,1)}, u32[]{:S(2)}) copy-start(bf16[1024,1024]{1,0:T(8,128)(2,1)} %param.23) | copy-start | bytes 6291460
  (20 other events, 62.0 us)
Sparse Core Ops, SparseCore 0:
  14.3 39.4 all-gather.4
  56.6 40.8 all-gather.2
  204.1 61.7 reduce-scatter.9
  270.1 71.4 reduce-scatter.13
  345.3 71.3 reduce-scatter.7
  421.2 125.3 reduce-scatter.17
  550.7 126.0 reduce-scatter.15
  681.4 125.9 reduce-scatter.19
  811.6 55.0 reduce-scatter.11
  869.8 47.8 all-reduce.6
where the time goes:
time: 937 us; the launch traced here: 935 us
  waiting for transfers between devices  701 us (75%)
  matrix products  83.2 us (9%)
  blocking collectives  66.4 us (7%)
  other arithmetic  51.5 us (5%)
  local copies, waits for them, and re-layouts  15.8 us (2%)
  between operations  15.6 us (2%)
    reduce_scatter x1, waiting for transfers between devices, shards(): lax.psum_scatter(grad_down, 'seq', scatter_dimension=1, tiled=True)  129 us
    reduce_scatter x1, waiting for transfers between devices, shards(): lax.psum_scatter(grad_gate, 'seq', scatter_dimension=0, tiled=True)  128 us
    reduce_scatter x1, waiting for transfers between devices, shards(): lax.psum_scatter(grad_up, 'seq', scatter_dimension=0, tiled=True)  128 us
    reduce_scatter x1, waiting for transfers between devices, shards(): lax.psum_scatter(grad_output, 'seq', scatter_dimension=0, tiled=True)  74.2 us
    reduce_scatter x1, waiting for transfers between devices, shards(): lax.psum_scatter(grad_query, 'seq', scatter_dimension=0, tiled=True)  73.5 us
    psum x1, waiting for transfers between devices, shards(): lax.psum(shares[0].astype(jnp.bfloat16), 'batch').astype(jnp.float32)  43.6 us
    all_gather x1, waiting for transfers between devices, shards(): lax.all_gather(latent, 'seq', axis=0, tiled=True)  41.4 us
    all_gather x1, waiting for transfers between devices, shards(): lax.all_gather(expand(latent, proj_expand), 'seq', axis=0, tiled=True)  33.6 us
  transfers between devices with their start and end apart: 10, of which 10 were waited for; matrix products, arithmetic and copies ran while one was open for 6% of the time, Pallas kernels for 0%

commit v1 on v0

v1 whole, which is shorter than its diff:
```python
import functools

import jax
import jax.numpy as jnp
from jax import lax
from jax.experimental import pallas as pl
from jax.experimental.pallas import tpu as pltpu
from jax.sharding import Mesh
from jax.sharding import PartitionSpec as P

HEADS = 16
HD = 64
GROUPS = 2
PER = HEADS // GROUPS
LAT = 256
DOCS = 8
LANE = 128
CHUNK = 256

F32 = jnp.float32
BF16 = jnp.bfloat16
eps = 1e-05
scale = 0.125
masked = -1e30

SEQ = ("z", "x", "core")
PLANE = ("x", "core", "batch")
WIDE = 3 * LANE

VM = pl.BlockSpec(memory_space=pltpu.VMEM)
SM = pl.BlockSpec(memory_space=pltpu.SMEM)
ANY = pl.BlockSpec(memory_space=pl.ANY)
LIMIT = 60 * 1024 * 1024


def nn(left, right):
    return jnp.dot(left, right, preferred_element_type=F32)


def tn(left, right):
    return lax.dot_general(left, right, (((0,), (0,)), ((), ())), preferred_element_type=F32)


def nt(left, right):
    return lax.dot_general(left, right, (((1,), (1,)), ((), ())), preferred_element_type=F32)


def shape(dims, dtype):
    return jax.ShapeDtypeStruct(dims, dtype)


def norm_forward(hidden, gain):
    inverse = lax.rsqrt(jnp.mean(hidden * hidden, axis=-1, keepdims=True) + eps)
    return (hidden * inverse * gain, inverse)


def norm_backward(hidden, gain, inverse, grad):
    scaled = grad * gain
    gain_grad = jnp.sum(grad * hidden * inverse, axis=0, keepdims=True)
    cubed = inverse * inverse * inverse
    hidden_grad = inverse * scaled - hidden * cubed * jnp.mean(
        scaled * hidden, axis=-1, keepdims=True
    )
    return (hidden_grad, gain_grad)


def doc_bounds(sc, tok):
    first = sc[0]
    query = first + lax.broadcasted_iota(jnp.int32, (1, tok), 1)
    begin = jnp.zeros((1, tok), jnp.int32)
    low = jnp.int32(0)
    end = jnp.int32(0)
    for d in range(DOCS):
        end = end + sc[8 + d]
        begin = jnp.where(query >= end, end, begin)
        low = jnp.where(first >= end, end, low)
    begin = jnp.where(query >= end, query, begin)
    low = jnp.where(first >= end, first, low)
    return query, begin, low // CHUNK, (first + tok - 1) // CHUNK + 1


def chunk_bias(chunk, query, begin):
    key = chunk * CHUNK + lax.broadcasted_iota(jnp.int32, (CHUNK, LANE), 0)
    bias = jnp.where((key >= begin) & (key <= query), 0.0, masked)
    return jnp.concatenate([bias] * PER, axis=1)


def attend_kernel(
    nz, relative, sc, k00, k01, k10, k11, qp, hidden, wo, gain,
    kvs, ot, logs, left, mid, normed, top, total, acc,
):
    tok = hidden.shape[0]
    z, x, core = sc[1], sc[2], sc[3]
    for rc, rx, ref in ((0, 0, k00), (0, 1, k01), (1, 0, k10), (1, 1, k11)):
        for k in range(nz):
            where_z = z - k if relative else k
            slot = (where_z * 2 + (rx ^ x)) * 2 + (rc ^ core)

            @pl.when(where_z >= 0)
            def _():
                kvs[pl.ds(pl.multiple_of(slot * tok, tok), tok), :] = ref[k]

    query, begin, low, high = doc_bounds(sc, tok)
    top[...] = jnp.full(top.shape, masked, F32)
    total[...] = jnp.zeros(total.shape, F32)
    acc[...] = jnp.zeros(acc.shape, F32)

    @pl.loop(low, high)
    def _(chunk):
        kv = kvs[pl.ds(pl.multiple_of(chunk * CHUNK, CHUNK), CHUNK), :]
        bias = chunk_bias(chunk, query, begin)
        for g in range(GROUPS):
            part = kv[:, g * LANE : (g + 1) * LANE]
            raw = nn(part, qp[g]) + bias
            old = top[g]
            new = jnp.maximum(old, jnp.max(raw, axis=0, keepdims=True))
            prob = jnp.exp(raw - new)
            fade = jnp.exp(old - new)
            top[g] = new
            total[g] = total[g] * fade + jnp.sum(prob, axis=0, keepdims=True)
            acc[g] = acc[g] * fade + tn(part, prob.astype(BF16))

    for g in range(GROUPS):
        mixed = acc[g, HD : 2 * HD, :] * (1.0 / total[g])
        ot[g] = mixed
        logs[g] = top[g] + jnp.log(total[g])
        for h in range(PER):
            row = (g * PER + h) * HD
            left[0, row : row + HD, :] = mixed[:, h * LANE : (h + 1) * LANE].astype(BF16)
    middle = hidden[...].astype(F32) + tn(left[0], wo[...])
    mid[...] = middle
    value, unused = norm_forward(middle, gain[...])
    normed[...] = value.astype(BF16)
    left[1] = value.T.astype(BF16)


def attend(sc, kv_parts, qp, hidden, wo, gain, nz, relative):
    tok, width = hidden.shape
    seq_len = nz * 4 * tok
    return pl.pallas_call(
        functools.partial(attend_kernel, nz, relative),
        out_shape=(
            shape((seq_len, 2 * LANE), BF16),
            shape((GROUPS, HD, PER * tok), F32),
            shape((GROUPS, 1, PER * tok), F32),
            shape((2, width, tok), BF16),
            shape((tok, width), F32),
            shape((tok, width), BF16),
        ),
        in_specs=[SM] + [VM] * 8,
        out_specs=(VM,) * 6,
        scratch_shapes=[
            pltpu.VMEM((GROUPS, 1, PER * tok), F32),
            pltpu.VMEM((GROUPS, 1, PER * tok), F32),
            pltpu.VMEM((GROUPS, 2 * HD, PER * tok), F32),
        ],
        compiler_params=pltpu.CompilerParams(vmem_limit_bytes=LIMIT),
        name="attend",
    )(sc, *kv_parts, qp, hidden, wo, gain)


def start_tile(place):
    return (place * 11) // 4


def feed_kernel(
    steps, sc, normed, grad_out, mid, gain, wo, wg, wu, wd, *rest
):
    sends = rest[:8]
    output, dmid, dop, gain_grad = rest[8:12]
    acc, back, dgate_s, dup_s, act_s = rest[12:]
    step = pl.program_id(0)

    @pl.when(step == 0)
    def _():
        acc[...] = jnp.zeros(acc.shape, F32)
        back[...] = jnp.zeros(back.shape, F32)

    n2 = normed[...]
    dy = grad_out[...]
    gate = nn(n2, wg[...])
    upper = nn(n2, wu[...])
    d_act = nt(dy, wd[...])
    sigma = jax.nn.sigmoid(gate)
    swish = gate * sigma
    act = (swish * upper).astype(BF16)
    dgate = (d_act * upper * sigma * (1.0 + gate * (1.0 - sigma))).astype(BF16)
    dup = (d_act * swish).astype(BF16)
    acc[...] += nn(act, wd[...])
    back[...] += nt(dgate, wg[...]) + nt(dup, wu[...])
    tile = wg.shape[1]
    cols = pl.ds(pl.multiple_of(step * tile, tile), tile)
    dgate_s[:, cols] = dgate
    dup_s[:, cols] = dup
    act_s[:, cols] = act

    @pl.when(step == steps - 1)
    def _():
        middle = mid[...]
        output[...] = (middle + acc[...]).astype(BF16)
        inverse = lax.rsqrt(jnp.mean(middle * middle, axis=-1, keepdims=True) + eps)
        grad, gains = norm_backward(middle, gain[...], inverse, back[...])
        grad = grad + dy.astype(F32)
        dmid[...] = grad
        gain_grad[...] = gains
        low = grad.astype(BF16)
        back[...] = low.astype(F32)
        for k in range(8):
            place = sc[4] ^ k
            cols = pl.ds(pl.multiple_of(start_tile(place) * LANE, LANE), WIDE)
            sends[k][:, 0:WIDE] = dgate_s[:, cols]
            sends[k][:, WIDE : 2 * WIDE] = dup_s[:, cols]
            sends[k][:, 2 * WIDE : 3 * WIDE] = act_s[:, cols]
            cols = pl.ds(pl.multiple_of(place * LANE, LANE), LANE)
            sends[k][:, 3 * WIDE :] = back[:, cols].astype(BF16)
        turned = nt(wo[...], low).astype(BF16)
        dop[:, 0:HD, :] = jnp.zeros((GROUPS, HD, dop.shape[2]), BF16)
        for g in range(GROUPS):
            for h in range(PER):
                row = (g * PER + h) * HD
                dop[g, HD:, h * LANE : (h + 1) * LANE] = turned[row : row + HD, :]


def feed(sc, normed, grad_out, mid, gain, wo, wg, wu, wd):
    tok, width = normed.shape
    hidden = wg.shape[1]
    tile = 2 * LANE
    steps = hidden // tile
    fixed = lambda *dims: pl.BlockSpec(dims, lambda i: (0,) * len(dims))
    send = shape((tok, 3 * WIDE + LANE), BF16)
    return pl.pallas_call(
        functools.partial(feed_kernel, steps),
        grid=(steps,),
        out_shape=(send,) * 8
        + (
            shape((tok, width), BF16),
            shape((tok, width), F32),
            shape((GROUPS, 2 * HD, PER * tok), BF16),
            shape((1, width), F32),
        ),
        in_specs=[
            SM,
            fixed(tok, width),
            fixed(tok, width),
            fixed(tok, width),
            fixed(1, width),
            fixed(width, width),
            pl.BlockSpec((width, tile), lambda i: (0, i)),
            pl.BlockSpec((width, tile), lambda i: (0, i)),
            pl.BlockSpec((tile, width), lambda i: (i, 0)),
        ],
        out_specs=(fixed(*send.shape),) * 8
        + (
            fixed(tok, width),
            fixed(tok, width),
            fixed(GROUPS, 2 * HD, PER * tok),
            fixed(1, width),
        ),
        scratch_shapes=[
            pltpu.VMEM((tok, width), F32),
            pltpu.VMEM((tok, width), F32),
            pltpu.VMEM((tok, hidden), BF16),
            pltpu.VMEM((tok, hidden), BF16),
            pltpu.VMEM((tok, hidden), BF16),
        ],
        compiler_params=pltpu.CompilerParams(vmem_limit_bytes=LIMIT),
        name="feed",
    )(sc, normed, grad_out, mid, gain, wo, wg, wu, wd)


def back_kernel(nz, sc, kvs, qp, dop, ot, logs, *rest):
    sends = rest[:8]
    dq, keep, send = rest[8:11]
    acc, rows, block = rest[11:]
    tok = dq.shape[0]
    x, core = sc[2], sc[3]

    @pl.loop(0, nz)
    def _(i):
        keep[:, i] = jnp.zeros((2,) + keep.shape[2:], BF16)
        send[:, i] = jnp.zeros((2,) + send.shape[2:], BF16)

    query, begin, low, high = doc_bounds(sc, tok)
    acc[...] = jnp.zeros(acc.shape, F32)
    for g in range(GROUPS):
        rows[g] = jnp.sum(dop[g, HD:, :].astype(F32) * ot[g], axis=0, keepdims=True)

    @pl.loop(low, high)
    def _(chunk):
        kv = kvs[pl.ds(pl.multiple_of(chunk * CHUNK, CHUNK), CHUNK), :]
        bias = chunk_bias(chunk, query, begin)
        for g in range(GROUPS):
            part = kv[:, g * LANE : (g + 1) * LANE]
            prob = jnp.exp(nn(part, qp[g]) + bias - logs[g])
            slope = (prob * (nn(part, dop[g]) - rows[g])).astype(BF16)
            block[:, g * LANE : (g + 1) * LANE] = nt(slope, qp[g]) + nt(prob.astype(BF16), dop[g])
            acc[g] += tn(part, slope)
        where_z = chunk // 2
        rel = (chunk % 2) ^ x
        keep[rel, where_z] = block[pl.ds(pl.multiple_of(core * tok, tok), tok), :].astype(BF16)
        send[rel, where_z] = block[pl.ds(pl.multiple_of((1 - core) * tok, tok), tok), :].astype(BF16)

    for g in range(GROUPS):
        for h in range(0, PER, 2):
            pair = [acc[g, 0:HD, (h + i) * LANE : (h + i + 1) * LANE] for i in range(2)]
            col = (g * PER + h) * HD
            dq[:, col : col + LANE] = (jnp.concatenate(pair, axis=0).T * scale).astype(BF16)
    for k in range(8):
        place = sc[4] ^ k
        sends[k][...] = dq[:, pl.ds(pl.multiple_of(place * LANE, LANE), LANE)]


def attend_back(sc, kvs, qp, dop, ot, logs, nz, tok):
    width = HEADS * HD
    part = shape((2, nz, tok, 2 * LANE), BF16)
    return pl.pallas_call(
        functools.partial(back_kernel, nz),
        out_shape=(shape((tok, LANE), BF16),) * 8 + (shape((tok, width), BF16), part, part),
        in_specs=[SM] + [VM] * 5,
        out_specs=(VM,) * 11,
        scratch_shapes=[
            pltpu.VMEM((GROUPS, 2 * HD, PER * tok), F32),
            pltpu.VMEM((GROUPS, 1, PER * tok), F32),
            pltpu.VMEM((CHUNK, 2 * LANE), F32),
        ],
        compiler_params=pltpu.CompilerParams(vmem_limit_bytes=LIMIT),
        name="attend_back",
    )(sc, kvs, qp, dop, ot, logs)


def weight_kernel(plan, nz, sc, *refs):
    count = max(index for index, unused, unused in plan) + 1
    lefts = refs[:count]
    rights = refs[count : count + 8]
    keep, send = refs[count + 8 : count + 10]
    wide, tall, sems = refs[count + 10 :]
    tok = rights[0].shape[0]
    copies = []
    for k in range(8):
        place = sc[4] ^ k
        copies.append(
            pltpu.make_async_copy(rights[k], tall.at[pl.ds(k * tok, tok), :], sems.at[count, k])
        )
        for i in range(count):
            copies.append(
                pltpu.make_async_copy(
                    lefts[i].at[place], wide.at[i, :, pl.ds(k * tok, tok)], sems.at[i, k]
                )
            )
    for copy in copies:
        copy.start()
    for copy in copies:
        copy.wait()
    bit = sc[1] % 2
    size = keep.shape[1]

    @pl.loop(0, nz // 2)
    def _(i):
        for ref, half in ((keep, bit), (send, 1 - bit)):
            rows = pl.ds(pl.multiple_of((2 * i + half) * size, size), size)
            for index, begin, stop in plan:
                ref[i, :, begin:stop] = nn(wide[index, rows, :], tall[:, begin:stop]).astype(BF16)


def weight_terms(sc, lefts, rights, plan, nz):
    tok, width = rights[0].shape
    rows = lefts[0].shape[1]
    half = shape((nz // 2, rows // nz, width), BF16)
    return pl.pallas_call(
        functools.partial(weight_kernel, plan, nz),
        out_shape=(half, half),
        in_specs=[SM] + [ANY] * (len(lefts) + 8),
        out_specs=(VM, VM),
        scratch_shapes=[
            pltpu.VMEM((len(lefts), rows, 8 * tok), BF16),
            pltpu.VMEM((8 * tok, width), BF16),
            pltpu.SemaphoreType.DMA((len(lefts) + 1, 8)),
        ],
        compiler_params=pltpu.CompilerParams(vmem_limit_bytes=LIMIT),
        name="weight_terms",
    )(sc, *lefts, *rights)


def swap(value, axis):
    return lax.ppermute(value, axis, [(0, 1), (1, 0)])


def plane_swap(parts):
    moved = [parts[0]]
    for k in range(1, 8):
        moved.append(lax.ppermute(parts[k], PLANE, [(d, d ^ k) for d in range(8)]))
    return moved


def z_halve(value, z, nz, step):
    bit = (z >> step) & 1
    pairs = value.reshape((value.shape[0] // 2, 2) + value.shape[1:])
    keep = lax.dynamic_index_in_dim(pairs, bit, 1, keepdims=False)
    send = lax.dynamic_index_in_dim(pairs, 1 - bit, 1, keepdims=False)
    return keep, send


def z_finish(keep, send, z, nz):
    flip = lambda step: [(i, i ^ (1 << step)) for i in range(nz)]
    total = keep.astype(F32) + lax.ppermute(send, "z", flip(0)).astype(F32)
    step = 1
    while (1 << step) < nz:
        keep, send = z_halve(total, z, nz, step)
        total = keep + lax.ppermute(send.astype(BF16), "z", flip(step)).astype(F32)
        step += 1
    return total[0]


def rows_out(block, place):
    parts = block.astype(BF16).reshape(4, block.shape[0] // 4, block.shape[1])
    rows = [lax.dynamic_index_in_dim(parts, (place ^ k) >> 1, 0, keepdims=False) for k in range(8)]
    return plane_swap(rows)


def place_kernel(rows, hidden, sc, *refs):
    parts = refs[:8]
    gate, up, down, outp = refs[8:]
    for k in range(8):
        place = sc[4] ^ k
        start = start_tile(place)
        part = parts[k][...].astype(F32)
        twice = (place > 0) & (start < start_tile(place - 1) + 3)
        for index, ref in ((0, gate), (1, up), (2, down)):
            for i in range(3):

                @pl.when(jnp.logical_not(twice) if i == 0 else start >= 0)
                def _():
                    cols = pl.ds(pl.multiple_of((start + i) * LANE, LANE), LANE)
                    col = index * WIDE + i * LANE
                    ref[:, cols] = part[:, col : col + LANE]

        outp[:, pl.ds(pl.multiple_of(place * LANE, LANE), LANE)] = part[:, 3 * WIDE :]


def place_wide(sc, parts, hidden, width):
    rows = parts[0].shape[0]
    wide = shape((rows, hidden), F32)
    return pl.pallas_call(
        functools.partial(place_kernel, rows, hidden),
        out_shape=(wide, wide, wide, shape((rows, width), F32)),
        in_specs=[SM] + [VM] * 8,
        out_specs=(VM,) * 4,
        compiler_params=pltpu.CompilerParams(vmem_limit_bytes=LIMIT),
        name="place_wide",
    )(sc, *parts)


def in_place(parts, place):
    stacked = jnp.stack(parts)
    order = place ^ jnp.arange(8, dtype=jnp.int32)
    stacked = jnp.take(stacked, order, axis=0)
    return stacked.transpose(1, 0, 2).reshape(parts[0].shape[0], -1).astype(F32)


def shards(
    inputs, lengths, proj_query, proj_latent, proj_expand, proj_output,
    ffn_gate, ffn_up, ffn_down, norm_attn, norm_ffn, cotangent,
):
    tok, width = inputs.shape[1:]
    nz = lax.axis_size("z")
    z, x, core, batch = [lax.axis_index(a) for a in ("z", "x", "core", "batch")]
    place = (x * 2 + core) * 2 + batch
    hidden_size = ffn_gate.shape[1]
    first = ((z * 2 + x) * 2 + core) * tok
    sc = jnp.stack([first, z, x, core, place, place, place, place]).astype(jnp.int32)
    sc = jnp.concatenate([sc, lengths[0]])

    hidden_low = inputs[0]
    hidden = hidden_low.astype(F32)
    dy = cotangent[0]
    gain_attn = norm_attn.astype(F32)[None]
    gain_ffn = norm_ffn.astype(F32)[None]

    normed, inverse = norm_forward(hidden, gain_attn)
    normed_low = normed.astype(BF16)
    latent = nn(normed_low, proj_latent).astype(BF16)
    kv = jnp.concatenate(
        [
            nn(latent[:, g * LAT : (g + 1) * LAT], proj_expand[:, g * LANE : (g + 1) * LANE])
            for g in range(GROUPS)
        ],
        axis=1,
    ).astype(BF16)

    relative = nz <= 4
    if relative:
        moved = [kv]
        for k in range(1, nz):
            moved.append(lax.ppermute(kv, "z", [(i, i + k) for i in range(nz - k)]))
        k00 = jnp.stack(moved)
    else:
        k00 = lax.all_gather(kv, "z", axis=0)
    k01 = swap(k00, "x")
    k10 = swap(k00, "core")
    k11 = swap(k01, "core")

    queries = nn(normed_low, proj_query).astype(BF16) * scale
    turned = queries.T.reshape(GROUPS, PER, HD, tok).transpose(0, 2, 1, 3)
    qp = jnp.pad(turned.reshape(GROUPS, HD, PER * tok), ((0, 0), (0, HD), (0, 0)))
    early = lax.all_gather(jnp.stack([dy.T, normed_low.T]), PLANE, axis=1)

    kvs, ot, logs, left, mid, normed_two = attend(
        sc, (k00, k01, k10, k11), qp, hidden_low, proj_output, gain_ffn, nz, relative
    )
    later = lax.all_gather(left, PLANE, axis=1)
    fed = feed(
        sc, normed_two, dy, mid, gain_ffn, proj_output, ffn_gate, ffn_up, ffn_down
    )
    output, dmid, dop, gain_two = fed[8:]
    wide_parts = plane_swap(fed[:8])

    backed = attend_back(sc, kvs, qp, dop, ot, logs, nz, tok)
    dq, keep, send = backed[8:]
    came = swap(send, "core")
    side = (keep[1].astype(F32) + came[1].astype(F32)).astype(BF16)
    side = swap(side, "x").astype(F32)
    term = keep[0].astype(F32) + came[0].astype(F32) + side
    if relative:
        kv_grad = lax.dynamic_index_in_dim(term, z, 0, keepdims=False)
        term_low = term.astype(BF16)
        for k in range(1, nz):
            block = lax.dynamic_index_in_dim(term_low, jnp.maximum(z - k, 0), 0, keepdims=False)
            block = lax.ppermute(block, "z", [(i, i - k) for i in range(k, nz)])
            kv_grad = kv_grad + block.astype(F32)
    else:
        kv_grad = lax.psum_scatter(term, "z", scatter_dimension=0, tiled=False)
    kv_grad = kv_grad.astype(BF16)
    query_parts = plane_swap(backed[:8])

    d_latent = jnp.concatenate(
        [
            nt(kv_grad[:, g * LANE : (g + 1) * LANE], proj_expand[:, g * LANE : (g + 1) * LANE])
            for g in range(GROUPS)
        ],
        axis=1,
    ).astype(BF16)
    lat_cols = d_latent.shape[1] // 8
    lat_split = d_latent.reshape(tok, 8, lat_cols).transpose(1, 0, 2)
    lat_parts = plane_swap(
        [lax.dynamic_index_in_dim(lat_split, place ^ k, 0, keepdims=False) for k in range(8)]
    )
    d_normed = nt(dq, proj_query) + nt(d_latent, proj_latent)
    d_hidden, gain_one = norm_backward(hidden, gain_attn, inverse, d_normed)
    input_grad = (d_hidden + dmid).astype(BF16)

    seq = nz * 4
    expand_t = jnp.concatenate(
        [
            lax.dot_general(
                kv_grad[:, g * LANE : (g + 1) * LANE],
                latent[:, g * LAT : (g + 1) * LAT],
                (((0,), (0,)), ((), ())),
                preferred_element_type=F32,
            )
            for g in range(GROUPS)
        ],
        axis=0,
    )
    small = jnp.concatenate(
        [
            expand_t.reshape(seq, -1),
            gain_one.reshape(seq, -1),
            gain_two.reshape(seq, -1),
        ],
        axis=1,
    )
    small = small.reshape(nz, 2, 2, -1)
    for axis, where, dim in (("core", core, 2), ("x", x, 1)):
        mine = lax.dynamic_index_in_dim(small, where, dim, keepdims=False)
        other = lax.dynamic_index_in_dim(small, 1 - where, dim, keepdims=False)
        small = mine + swap(other.astype(BF16), axis).astype(F32)
    step = 0
    while (1 << step) < nz:
        mine, other = z_halve(small, z, nz, step)
        flips = [(i, i ^ (1 << step)) for i in range(nz)]
        small = mine + lax.ppermute(other.astype(BF16), "z", flips).astype(F32)
        step += 1
    small_low = small[0].astype(BF16)
    small = small_low.astype(F32) + swap(small_low, "batch").astype(F32)
    cut = expand_t.size // seq
    gains = (small.shape[0] - cut) // 2
    grad_expand = small[:cut].reshape(-1, expand_t.shape[1]).T
    grad_norm_attn = small[cut : cut + gains]
    grad_norm_ffn = small[cut + gains :]

    dys, n1s = early[0], early[1]
    os, n2s = later[0], later[1]
    plan = ((0, 0, 2 * WIDE), (1, 2 * WIDE, 3 * WIDE), (2, 3 * WIDE, 3 * WIDE + LANE))
    keep, send = weight_terms(sc, (n2s, dys, os), wide_parts, plan, nz)
    wide = z_finish(keep, send, z, nz)
    grad_gate, grad_up, grad_down_t, grad_output = place_wide(
        sc, rows_out(wide, place), hidden_size, width
    )
    keep, send = weight_terms(sc, (n1s,), query_parts, ((0, 0, LANE),), nz)
    grad_query = in_place(rows_out(z_finish(keep, send, z, nz), place), place)
    keep, send = weight_terms(sc, (n1s,), lat_parts, ((0, 0, lat_cols),), nz)
    grad_latent = in_place(rows_out(z_finish(keep, send, z, nz), place), place)
    return (
        output[None],
        input_grad[None],
        grad_query,
        grad_latent,
        grad_expand,
        grad_output,
        grad_gate,
        grad_up,
        grad_down_t.T,
        grad_norm_attn,
        grad_norm_ffn,
    )


def solution(mesh):
    seq, batch = mesh.shape["seq"], mesh.shape["batch"]
    fine = Mesh(mesh.devices.reshape(seq // 4, 2, 2, batch), SEQ + ("batch",))
    return jax.shard_map(
        shards,
        mesh=fine,
        in_specs=(P("batch", SEQ, None), P("batch", None))
        + (P(),) * 9
        + (P("batch", SEQ, None),),
        out_specs=(
            P("batch", SEQ, None),
            P("batch", SEQ, None),
            P(SEQ, None),
            P(SEQ, None),
            P(None, SEQ),
            P(SEQ, None),
            P(SEQ, None),
            P(SEQ, None),
            P(None, SEQ),
            P(SEQ),
            P(SEQ),
        ),
        check_vma=False,
    )
```

time: 937 us -> 339 us (0.36)
  waiting for transfers between devices: 701 us -> 141 us
  starting transfers between devices: 0.67 us -> 79.9 us
  matrix products: 83.2 us -> 8.02 us
  blocking collectives: 66.4 us -> 0 us
  Pallas kernels: 0 us -> 49.5 us
  other arithmetic: 51.5 us -> 14.1 us
  local copies, waits for them, and re-layouts: 15.8 us -> 29.2 us
    reduce_scatter x7 -> x0, waiting for transfers between devices: 582 us -> none  [the longest x1 129 us: shards(): lax.psum_scatter(grad_down, 'seq', scatter_dimension=1, tiled=True)]
    ppermute x0 -> x64, waiting for transfers between devices: none -> 131 us  [the longest x3 47.9 us: z_finish(): total = keep + lax.ppermute(send.astype(BF16), 'z', flip(step)).astype(F32)]
    ppermute x0 -> x64, starting transfers between devices: none -> 79.7 us  [the longest x42 41 us: plane_swap(): moved.append(lax.ppermute(parts[k], PLANE, [(d, d ^ k) for d in range(8)]))]
    dot_general x40 -> x10, matrix products: 83.2 us -> 8.02 us  [the longest x4 4.12 us: nn(): return jnp.dot(left, right, preferred_element_type=F32)]
    all_gather x2, waiting for transfers between devices: 75 us -> 10.6 us  [the longest x1 10.6 us: shards(): early = lax.all_gather(jnp.stack([dy.T, normed_low.T]), PLANE, axis=1)]
    pallas_call x0 -> x7, Pallas kernels: none -> 49.5 us  [the longest x1 19.3 us: feed(): pl.pallas_call(functools.partial(feed_kernel, steps), grid=(steps,), out_...]
    psum x1 -> x0, waiting for transfers between devices: 43.6 us -> none  [shards(): lax.psum(shares[0].astype(jnp.bfloat16), 'batch').astype(jnp.float32)]
    unnamed x1 -> x0, blocking collectives: 32.9 us -> none
  transfers between devices with their start and end apart: 10 -> 66, of which waited for: 10 -> 25; matrix products, arithmetic and copies ran while one was open for 6% -> 9% of each run, Pallas kernels for 0% -> 5%
where the time goes in v1:
time: 339 us; the launch traced here: 337 us
  waiting for transfers between devices  141 us (42%)
  starting transfers between devices  79.9 us (24%)
  Pallas kernels  49.5 us (15%)
  local copies, waits for them, and re-layouts  29.2 us (9%)
  between operations  15.2 us (4%)
  other arithmetic  14.1 us (4%)
  matrix products  8.02 us (2%)
    ppermute x3, waiting for transfers between devices, z_finish(): total = keep + lax.ppermute(send.astype(BF16), 'z', flip(step)).astype(F32)  47.9 us
    ppermute x42, starting transfers between devices, plane_swap(): moved.append(lax.ppermute(parts[k], PLANE, [(d, d ^ k) for d in range(8)]))  41 us
    ppermute x42, waiting for transfers between devices, plane_swap(): moved.append(lax.ppermute(parts[k], PLANE, [(d, d ^ k) for d in range(8)]))  35.9 us
    pallas_call x1, Pallas kernels, feed(): pl.pallas_call(functools.partial(feed_kernel, steps), grid=(steps,), out_...  19.3 us
    ppermute x3, waiting for transfers between devices, shards(): block = lax.ppermute(block, 'z', [(i, i - k) for i in range(k, nz)])  19.2 us
    ppermute x8, waiting for transfers between devices, swap(): return lax.ppermute(value, axis, [(0, 1), (1, 0)])  18.2 us
    pallas_call x3, Pallas kernels, weight_terms(): pl.pallas_call(functools.partial(weight_kernel, plan, nz), out_shape=(hal...  17.1 us
    ppermute x3, starting transfers between devices, shards(): moved.append(lax.ppermute(kv, 'z', [(i, i + k) for i in range(nz - k)]))  10.7 us
  transfers between devices with their start and end apart: 66, of which 25 were waited for; matrix products, arithmetic and copies ran while one was open for 9% of the time, Pallas kernels for 5%

profile of v1, /device:TPU:0, one launch (start us, length us, event | category | flops | bytes accessed | tf_op | source)
XLA Modules:
  0.0 337.3 jit_solution(17723155181985305919)
XLA Ops:
  13.4 7.0 %collective-permute-start.2 = (bf16[128,256]{1,0:T(8,128)(2,1)S(1)}, bf16[128,256]{1,0:T(8,128)(2,1)S(1)}, u32[]{:S(2)}, u32[]{:S(2)}) collective-permute-start(bf16[128,256]{1,0:T(8,128)(2,1)S(1)} %pad_maximum_fusion.3), channel_id=1, source_target_pairs={{0,24},{1,25},{2,26},{3,27},{4,28},{5,29},{6,30},{7,31}} | collective-permute-start | bytes 196616 | tf_op jit(solution)/shard_map/ppermute | solution.py:494
  21.7 2.5 collective-permute-start
  27.6 5.4 %collective-permute-done.3.k01 = bf16[4,128,256]{2,1,0:T(8,128)(2,1)S(1)} collective-permute-done((bf16[4,128,256]{2,1,0:T(8,128)(2,1)S(1)}, bf16[4,128,256]{2,1,0:T(8,128)(2,1)S(1)}, u32[]{:S(2)}, u32[]{:S(2)}) %collective-permute-start.3) | collective-permute-done | bytes 262176 | tf_op jit(solution)/shard_map/ppermute | solution.py:385
  35.8 5.3 %attend.1 = (bf16[2048,256]{1,0:T(8,128)(2,1)}, f32[2,64,1024]{2,1,0:T(8,128)}, f32[2,1,1024]{2,1,0:T(1,128)}, bf16[2,1024,128]{2,1,0:T(8,128)(2,1)}, f32[128,1024]{1,0:T(8,128)}, /*index=5*/bf16[128,1024]{1,0:T(8,128)(2,1)}) custom-call(s32[16]{0:T(128)} %concatenate.46.sc, bf16[4,128,256]{2,1,0:T(8,128)(2,1)} %copy-done.7, ...), custom_call_target="tpu_custom_call" | custom-call | tf_op jit(solution)/shard_map/attend/pallas_call | solution.py:140
  41.2 19.3 %feed.1 = (bf16[128,1280]{1,0:T(8,128)(2,1)}, bf16[128,1280]{1,0:T(8,128)(2,1)}, bf16[128,1280]{1,0:T(8,128)(2,1)}, bf16[128,1280]{1,0:T(8,128)(2,1)}, bf16[128,...) custom-call(s32[16]{0:T(128)} %concatenate.46.sc, ...), custom_call_target="tpu_custom_call" | custom-call | tf_op jit(solution)/shard_map/feed/pallas_call | solution.py:231
  60.5 4.5 %attend_back.1 = (bf16[128,128]{1,0:T(8,128)(2,1)}, bf16[128,128]{1,0:T(8,128)(2,1)}, bf16[128,128]{1,0:T(8,128)(2,1)}, bf16[128,128]{1,0:T(8,128)(2,1)}, bf16[1...) custom-call(s32[16]{0:T(128)} %concatenate.46.sc, ...), custom_call_target="tpu_custom_call" | custom-call | tf_op jit(solution)/shard_map/attend_back/pallas_call | solution.py:316
  69.9 4.3 %collective-permute-start.7 = (bf16[4,128,256]{2,1,0:T(8,128)(2,1)}, bf16[4,128,256]{2,1,0:T(8,128)(2,1)}, u32[]{:S(2)}, u32[]{:S(2)}) collective-permute-start(bf16[4,128,256]{2,1,0:T(8,128)(2,1)} %fusion.12), channel_id=1, source_target_pairs={{0,4},{4,0},{1,5},{5,1},{2,6},{6,2},{3,7},{7,3},{8,12},{12,8},{9,1... | collective-permute-start | bytes 786440 | tf_op jit(solution)/shard_map/ppermute | solution.py:385
  74.1 7.1 %collective-permute-done.7 = bf16[4,128,256]{2,1,0:T(8,128)(2,1)} collective-permute-done((bf16[4,128,256]{2,1,0:T(8,128)(2,1)}, bf16[4,128,256]{2,1,0:T(8,128)(2,1)}, u32[]{:S(2)}, u32[]{:S(2)}) %collective-permute-start.7) | collective-permute-done | bytes 262176 | tf_op jit(solution)/shard_map/ppermute | solution.py:385
  87.9 17.7 %collective-permute-done.10 = bf16[128,256]{1,0:T(8,128)(2,1)} collective-permute-done((bf16[128,256]{1,0:T(8,128)(2,1)}, bf16[128,256]{1,0:T(8,128)(2,1)}, u32[]{:S(2)}, u32[]{:S(2)}) %collective-permute-start.10) | collective-permute-done | bytes 65568 | tf_op jit(solution)/shard_map/ppermute | solution.py:528
  124.2 3.9 %collective-permute-done.44 = bf16[4,4224]{1,0:T(4,128)(2,1)S(1)} collective-permute-done((bf16[4,4224]{1,0:T(4,128)(2,1)S(1)}, bf16[4,4224]{1,0:T(4,128)(2,1)S(1)}, u32[]{:S(2)}, u32[]{:S(2)}) %collective-permute-start.44) | collective-permute-done | bytes 33824 | tf_op jit(solution)/shard_map/ppermute | solution.py:385
  130.1 2.0 collective-permute-done.45
  132.1 2.4 collective-permute-start.46
  136.9 2.1 collective-permute-start.31
  142.3 10.6 %all-gather.5.cloned.1.call-done = bf16[2,8192,128]{1,2,0:T(8,128)(2,1)} async-done(((bf16[2,1024,128]{1,2,0:T(8,128)(2,1)}), bf16[2,8192,128]{1,2,0:T(8,128)(2,1)}) %all-gather.5.cloned.1.call-update) | async-done | bytes 4194320 | tf_op jit(solution)/shard_map/all_gather | solution.py:505
  152.9 4.0 %fusion.52 = (bf16[1,8192,128]{1,2,0:T(8,128)(2,1)S(1)}, bf16[1,8192,128]{1,2,0:T(8,128)(2,1)}) fusion(bf16[2,8192,128]{1,2,0:T(8,128)(2,1)} %all-gather.5.cloned.1.call-done), kind=kLoop, calls=%fused_computation.161 | loop fusion | bytes 8388608 | tf_op jit(solution)/shard_map/slice | solution.py:591
  156.9 4.1 %copy.57 = bf16[1,8192,128]{2,1,0:T(8,128)(2,1)} copy(bf16[1,8192,128]{1,2,0:T(8,128)(2,1)} %get-tuple-element.96) | data formatting | bytes 4194304 | tf_op jit(solution)/shard_map/slice | solution.py:591
  164.6 3.9 %weight_terms.4 = (bf16[2,256,64]{2,1,0:T(8,128)(2,1)}, bf16[2,256,64]{2,1,0:T(8,128)(2,1)}) custom-call(s32[16]{0:T(128)} %concatenate.46.sc, bf16[8,1024,128]{2,1,0:T(8,128)(2,1)} %bitcast.182, bf16[128,64]{1,0:T(8,128)(2,1)} %bitcast.201, bf16[128,64]{1,0:T(8,128)(2,1)} %copy-done.30, bf16[128,64]{1,0:T(8,128)(2,1)} %copy-done.32, ...), custom_call_target="tpu_custom_call" | custom-call | tf_op jit(solution)/shard_map/weight_terms/pallas_call | solution.py:369
  170.1 3.9 %collective-permute-done.34 = bf16[2,256,64]{2,1,0:T(8,128)(2,1)S(1)} collective-permute-done((bf16[2,256,64]{2,1,0:T(8,128)(2,1)}, bf16[2,256,64]{2,1,0:T(8,128)(2,1)S(1)}, u32[]{:S(2)}, u32[]{:S(2)}) %collective-permute-start.34) | collective-permute-done | bytes 65568 | tf_op jit(solution)/shard_map/ppermute | solution.py:405
  175.0 2.5 collective-permute-start.35
  191.3 7.7 %collective-permute-done.48.refs_4_ = bf16[128,1280]{1,0:T(8,128)(2,1)S(1)} collective-permute-done((bf16[128,1280]{1,0:T(8,128)(2,1)}, bf16[128,1280]{1,0:T(8,128)(2,1)S(1)}, u32[]{:S(2)}, u32[]{:S(2)}) %collective-permute-start.48) | collective-permute-done | bytes 327712 | tf_op jit(solution)/shard_map/ppermute | solution.py:391
  200.9 11.7 %collective-permute-done.50.refs_6_ = bf16[128,1280]{1,0:T(8,128)(2,1)S(1)} collective-permute-done((bf16[128,1280]{1,0:T(8,128)(2,1)}, bf16[128,1280]{1,0:T(8,128)(2,1)S(1)}, u32[]{:S(2)}, u32[]{:S(2)}) %collective-permute-start.50) | collective-permute-done | bytes 327712 | tf_op jit(solution)/shard_map/ppermute | solution.py:391
  213.0 4.4 %fusion.51 = (bf16[1,8192,128]{2,1,0:T(8,128)(2,1)}, bf16[1,8192,128]{2,1,0:T(8,128)(2,1)}) fusion(bf16[2,8192,128]{2,1,0:T(8,128)(2,1)} %all-gather.7.cloned.1.call-done), kind=kLoop, calls=%fused_computation.160 | loop fusion | bytes 8388608 | tf_op jit(solution)/shard_map/slice | solution.py:592
  217.5 2.5 copy.74
  219.9 3.9 %weight_terms.3 = (bf16[2,256,128]{2,1,0:T(8,128)(2,1)}, bf16[2,256,128]{2,1,0:T(8,128)(2,1)}) custom-call(s32[16]{0:T(128)} %concatenate.46.sc, bf16[8,1024,128]{2,1,0:T(8,128)(2,1)} %bitcast.183, bf16[128,128]{1,0:T(8,128)(2,1)} %get-tuple-element.61.refs_1_, bf16[128,128]{1,0:T(8,128)(2,1)} %copy-done.27, bf16[128,128]{1,0:T(8,128)(2,1)} %copy-done.28, ...), custom_call_target="tpu_custom_call" | custom-call | tf_op jit(solution)/shard_map/weight_terms/pallas_call | solution.py:369
  225.7 9.3 %weight_terms.5 = (bf16[2,256,1280]{2,1,0:T(8,128)(2,1)}, bf16[2,256,1280]{2,1,0:T(8,128)(2,1)}) custom-call(s32[16]{0:T(128)} %concatenate.46.sc, bf16[8,1024,128]{2,1,0:T(8,128)(2,1)} %bitcast.187, bf16[8,1024,128]{2,1,0:T(8,128)(2,1)} %bitcast.185, bf16[8,1024,128]{2,1,0:T(8,128)(2,1)} %bitcast.186, bf16[128,1280]{1,0:T(8,128)(2,1)} %get-tuple-element.75.refs_3_, ...), custom_call_target="tpu_custom_call" | custom-call | tf_op jit(solution)/shard_map/weight_terms/pallas_call | solution.py:369
  246.6 19.0 %collective-permute-done.19 = bf16[1,256,128]{2,1,0:T(8,128)(2,1)S(1)} collective-permute-done((bf16[1,256,128]{2,1,0:T(8,128)(2,1)S(1)}, bf16[1,256,128]{2,1,0:T(8,128)(2,1)S(1)}, u32[]{:S(2)}, u32[]{:S(2)}) %collective-permute-start.19) | collective-permute-done | bytes 65568 | tf_op jit(solution)/shard_map/ppermute | solution.py:409
  274.2 3.4 %collective-permute-start.56 = (bf16[1,256,1280]{2,1,0:T(8,128)(2,1)S(1)}, bf16[1,256,1280]{2,1,0:T(8,128)(2,1)S(1)}, u32[]{:S(2)}, u32[]{:S(2)}) collective-permute-start(bf16[1,256,1280]{2,1,0:T(8,128)(2,1)S(1)} %dynamic-slice_convert_fusion), channel_id=1, source_target_pairs={{0,16},{8,24},{16,0},{24,8},{1,17},{9,25},{17,1},{25,9},{2,18},{10... | collective-permute-start | bytes 1966088 | tf_op jit(solution)/shard_map/ppermute | solution.py:409
  277.7 28.8 %collective-permute-done.56 = bf16[1,256,1280]{2,1,0:T(8,128)(2,1)S(1)} collective-permute-done((bf16[1,256,1280]{2,1,0:T(8,128)(2,1)S(1)}, bf16[1,256,1280]{2,1,0:T(8,128)(2,1)S(1)}, u32[]{:S(2)}, u32[]{:S(2)}) %collective-permute-start.56) | collective-permute-done | bytes 655392 | tf_op jit(solution)/shard_map/ppermute | solution.py:409
  313.6 2.1 collective-permute-start.63
  317.4 4.0 %collective-permute-done.61.refs_5_ = bf16[64,1280]{1,0:T(8,128)(2,1)S(1)} collective-permute-done((bf16[64,1280]{1,0:T(8,128)(2,1)S(1)}, bf16[64,1280]{1,0:T(8,128)(2,1)S(1)}, u32[]{:S(2)}, u32[]{:S(2)}) %collective-permute-start.61) | collective-permute-done | bytes 163872 | tf_op jit(solution)/shard_map/ppermute | solution.py:391
  323.0 3.6 %collective-permute-done.63.refs_7_ = bf16[64,1280]{1,0:T(8,128)(2,1)S(1)} collective-permute-done((bf16[64,1280]{1,0:T(8,128)(2,1)S(1)}, bf16[64,1280]{1,0:T(8,128)(2,1)S(1)}, u32[]{:S(2)}, u32[]{:S(2)}) %collective-permute-start.63) | collective-permute-done | bytes 163872 | tf_op jit(solution)/shard_map/ppermute | solution.py:391
  327.2 3.2 place_wide.1
  (328 shorter events, 105.9 us)
Async XLA Ops:
  7.2 145.7 %all-gather.5.cloned.1.call-start = ((), (), s32[]{:S(2)}) async-start(), calls=%async_computation | async-start | bytes 4718592 | tf_op jit(solution)/shard_map/all_gather | solution.py:505
  69.9 11.4 %collective-permute-start.7 = (bf16[4,128,256]{2,1,0:T(8,128)(2,1)}, bf16[4,128,256]{2,1,0:T(8,128)(2,1)}, u32[]{:S(2)}, u32[]{:S(2)}) collective-permute-start(bf16[4,128,256]{2,1,0:T(8,128)(2,1)} %fusion.12), channel_id=1, source_target_pairs={{0,4},{4,0},{1,5},{5,1},{2,6},{6,2},{3,7},{7,3},{8,12},{12,8},{9,1... | collective-permute-start | bytes 786440 | tf_op jit(solution)/shard_map/ppermute | solution.py:385
  84.0 21.6 %collective-permute-start.10 = (bf16[128,256]{1,0:T(8,128)(2,1)}, bf16[128,256]{1,0:T(8,128)(2,1)}, u32[]{:S(2)}, u32[]{:S(2)}) collective-permute-start(bf16[128,256]{1,0:T(8,128)(2,1)} %get-tuple-element.108), channel_id=1, source_target_pairs={{24,0},{25,1},{26,2},{27,3},{28,4},{29,5},{30,6},{31,7}} | collective-permute-start | bytes 196616 | tf_op jit(solution)/shard_map/ppermute | solution.py:528
  85.2 21.8 %collective-permute-start.9 = (bf16[128,256]{1,0:T(8,128)(2,1)}, bf16[128,256]{1,0:T(8,128)(2,1)}, u32[]{:S(2)}, u32[]{:S(2)}) collective-permute-start(bf16[128,256]{1,0:T(8,128)(2,1)} %get-tuple-element.109), channel_id=1, source_target_pairs={{16,0},{24,8},{17,1},{25,9},{18,2},{26,10},{19,3},{27,11},{20,4},{... | collective-permute-start | bytes 196616 | tf_op jit(solution)/shard_map/ppermute | solution.py:528
  86.5 20.5 %collective-permute-start.8 = (bf16[128,256]{1,0:T(8,128)(2,1)}, bf16[128,256]{1,0:T(8,128)(2,1)}, u32[]{:S(2)}, u32[]{:S(2)}) collective-permute-start(bf16[128,256]{1,0:T(8,128)(2,1)} %get-tuple-element.107), channel_id=1, source_target_pairs={{8,0},{16,8},{24,16},{9,1},{17,9},{25,17},{10,2},{18,10},{26,18},{... | collective-permute-start | bytes 196616 | tf_op jit(solution)/shard_map/ppermute | solution.py:528
  113.8 99.2 %all-gather.7.cloned.1.call-start = ((), (), s32[]{:S(2)}) async-start(), calls=%async_computation.1 | async-start | bytes 4718592 | tf_op jit(solution)/shard_map/all_gather | solution.py:510
  119.1 19.9 %collective-permute-start.27 = (bf16[128,64]{1,0:T(8,128)(2,1)S(1)}, bf16[128,64]{1,0:T(8,128)(2,1)S(1)}, u32[]{:S(2)}, u32[]{:S(2)}) collective-permute-start(bf16[128,64]{1,0:T(8,128)(2,1)S(1)} %bitcast.211), channel_id=1, source_target_pairs={{0,1},{1,0},{2,3},{3,2},{4,5},{5,4},{6,7},{7,6},{8,9},{9,8},{10,11... | collective-permute-start | bytes 49160 | tf_op jit(solution)/shard_map/ppermute | solution.py:391
  120.2 18.9 %collective-permute-start.28 = (bf16[128,64]{1,0:T(8,128)(2,1)S(1)}, bf16[128,64]{1,0:T(8,128)(2,1)S(1)}, u32[]{:S(2)}, u32[]{:S(2)}) collective-permute-start(bf16[128,64]{1,0:T(8,128)(2,1)S(1)} %bitcast.210), channel_id=1, source_target_pairs={{0,2},{1,3},{2,0},{3,1},{4,6},{5,7},{6,4},{7,5},{8,10},{9,11},{10,... | collective-permute-start | bytes 49160 | tf_op jit(solution)/shard_map/ppermute | solution.py:391
  120.6 20.2 %collective-permute-start.29 = (bf16[128,64]{1,0:T(8,128)(2,1)S(1)}, bf16[128,64]{1,0:T(8,128)(2,1)S(1)}, u32[]{:S(2)}, u32[]{:S(2)}) collective-permute-start(bf16[128,64]{1,0:T(8,128)(2,1)S(1)} %bitcast.209), channel_id=1, source_target_pairs={{0,3},{1,2},{2,1},{3,0},{4,7},{5,6},{6,5},{7,4},{8,11},{9,10},{10,... | collective-permute-start | bytes 49160 | tf_op jit(solution)/shard_map/ppermute | solution.py:391
  121.8 39.2 %collective-permute-start.30 = (bf16[128,64]{1,0:T(8,128)(2,1)S(1)}, bf16[128,64]{1,0:T(8,128)(2,1)S(1)}, u32[]{:S(2)}, u32[]{:S(2)}) collective-permute-start(bf16[128,64]{1,0:T(8,128)(2,1)S(1)} %bitcast.208), channel_id=1, source_target_pairs={{0,4},{1,5},{2,6},{3,7},{4,0},{5,1},{6,2},{7,3},{8,12},{9,13},{10,... | collective-permute-start | bytes 49160 | tf_op jit(solution)/shard_map/ppermute | solution.py:391
  136.9 25.7 %collective-permute-start.31 = (bf16[128,64]{1,0:T(8,128)(2,1)S(1)}, bf16[128,64]{1,0:T(8,128)(2,1)S(1)}, u32[]{:S(2)}, u32[]{:S(2)}) collective-permute-start(bf16[128,64]{1,0:T(8,128)(2,1)S(1)} %bitcast.214), channel_id=1, source_target_pairs={{0,5},{1,4},{2,7},{3,6},{4,1},{5,0},{6,3},{7,2},{8,13},{9,12},{10,... | collective-permute-start | bytes 49160 | tf_op jit(solution)/shard_map/ppermute | solution.py:391
  139.0 23.6 %collective-permute-start.32 = (bf16[128,64]{1,0:T(8,128)(2,1)S(1)}, bf16[128,64]{1,0:T(8,128)(2,1)S(1)}, u32[]{:S(2)}, u32[]{:S(2)}) collective-permute-start(bf16[128,64]{1,0:T(8,128)(2,1)S(1)} %bitcast.213), channel_id=1, source_target_pairs={{0,6},{1,7},{2,4},{3,5},{4,2},{5,3},{6,0},{7,1},{8,14},{9,15},{10,... | collective-permute-start | bytes 49160 | tf_op jit(solution)/shard_map/ppermute | solution.py:391
  139.1 24.3 %collective-permute-start.33 = (bf16[128,64]{1,0:T(8,128)(2,1)S(1)}, bf16[128,64]{1,0:T(8,128)(2,1)S(1)}, u32[]{:S(2)}, u32[]{:S(2)}) collective-permute-start(bf16[128,64]{1,0:T(8,128)(2,1)S(1)} %bitcast.212), channel_id=1, source_target_pairs={{0,7},{1,6},{2,5},{3,4},{4,3},{5,2},{6,1},{7,0},{8,15},{9,14},{10,... | collective-permute-start | bytes 49160 | tf_op jit(solution)/shard_map/ppermute | solution.py:391
  140.8 27.7 %collective-permute-start.47 = (bf16[4224]{0:T(1024)(128)(2,1)S(1)}, bf16[4224]{0:T(1024)(128)(2,1)S(1)}, u32[]{:S(2)}, u32[]{:S(2)}) collective-permute-start(bf16[4224]{0:T(1024)(128)(2,1)S(1)} %convert_reduce_fusion), channel_id=1, source_target_pairs={{0,1},{1,0},{2,3},{3,2},{4,5},{5,4},{6,7},{7,6},{8,9},{9,8},{10,11... | collective-permute-start | bytes 25352 | tf_op jit(solution)/shard_map/ppermute | solution.py:385
  161.0 17.6 %collective-permute-start.11 = (bf16[128,128]{1,0:T(8,128)(2,1)S(1)}, bf16[128,128]{1,0:T(8,128)(2,1)S(1)}, u32[]{:S(2)}, u32[]{:S(2)}) collective-permute-start(bf16[128,128]{1,0:T(8,128)(2,1)S(1)} %copy-done.56), channel_id=1, source_target_pairs={{0,1},{1,0},{2,3},{3,2},{4,5},{5,4},{6,7},{7,6},{8,9},{9,8},{10,11... | collective-permute-start | bytes 98312 | tf_op jit(solution)/shard_map/ppermute | solution.py:391
  162.6 17.9 %collective-permute-start.12 = (bf16[128,128]{1,0:T(8,128)(2,1)S(1)}, bf16[128,128]{1,0:T(8,128)(2,1)S(1)}, u32[]{:S(2)}, u32[]{:S(2)}) collective-permute-start(bf16[128,128]{1,0:T(8,128)(2,1)S(1)} %copy-done.55), channel_id=1, source_target_pairs={{0,2},{1,3},{2,0},{3,1},{4,6},{5,7},{6,4},{7,5},{8,10},{9,11},{10,... | collective-permute-start | bytes 98312 | tf_op jit(solution)/shard_map/ppermute | solution.py:391
  162.7 18.4 %collective-permute-start.13 = (bf16[128,128]{1,0:T(8,128)(2,1)S(1)}, bf16[128,128]{1,0:T(8,128)(2,1)S(1)}, u32[]{:S(2)}, u32[]{:S(2)}) collective-permute-start(bf16[128,128]{1,0:T(8,128)(2,1)S(1)} %copy-done.54), channel_id=1, source_target_pairs={{0,3},{1,2},{2,1},{3,0},{4,7},{5,6},{6,5},{7,4},{8,11},{9,10},{10,... | collective-permute-start | bytes 98312 | tf_op jit(solution)/shard_map/ppermute | solution.py:391
  163.4 19.4 %collective-permute-start.14 = (bf16[128,128]{1,0:T(8,128)(2,1)S(1)}, bf16[128,128]{1,0:T(8,128)(2,1)S(1)}, u32[]{:S(2)}, u32[]{:S(2)}) collective-permute-start(bf16[128,128]{1,0:T(8,128)(2,1)S(1)} %copy-done.53), channel_id=1, source_target_pairs={{0,4},{1,5},{2,6},{3,7},{4,0},{5,1},{6,2},{7,3},{8,12},{9,13},{10,... | collective-permute-start | bytes 98312 | tf_op jit(solution)/shard_map/ppermute | solution.py:391
  180.5 18.5 %collective-permute-start.48 = (bf16[128,1280]{1,0:T(8,128)(2,1)}, bf16[128,1280]{1,0:T(8,128)(2,1)S(1)}, u32[]{:S(2)}, u32[]{:S(2)}) collective-permute-start(bf16[128,1280]{1,0:T(8,128)(2,1)} %get-tuple-element.76), channel_id=1, source_target_pairs={{0,1},{1,0},{2,3},{3,2},{4,5},{5,4},{6,7},{7,6},{8,9},{9,8},{10,11... | collective-permute-start | bytes 983048 | tf_op jit(solution)/shard_map/ppermute | solution.py:391
  181.1 17.9 %collective-permute-start.49 = (bf16[128,1280]{1,0:T(8,128)(2,1)}, bf16[128,1280]{1,0:T(8,128)(2,1)S(1)}, u32[]{:S(2)}, u32[]{:S(2)}) collective-permute-start(bf16[128,1280]{1,0:T(8,128)(2,1)} %get-tuple-element.77), channel_id=1, source_target_pairs={{0,2},{1,3},{2,0},{3,1},{4,6},{5,7},{6,4},{7,5},{8,10},{9,11},{10,... | collective-permute-start | bytes 983048 | tf_op jit(solution)/shard_map/ppermute | solution.py:391
  181.7 30.9 %collective-permute-start.50 = (bf16[128,1280]{1,0:T(8,128)(2,1)}, bf16[128,1280]{1,0:T(8,128)(2,1)S(1)}, u32[]{:S(2)}, u32[]{:S(2)}) collective-permute-start(bf16[128,1280]{1,0:T(8,128)(2,1)} %get-tuple-element.78), channel_id=1, source_target_pairs={{0,3},{1,2},{2,1},{3,0},{4,7},{5,6},{6,5},{7,4},{8,11},{9,10},{10,... | collective-permute-start | bytes 983048 | tf_op jit(solution)/shard_map/ppermute | solution.py:391
  187.2 36.7 %collective-permute-start.51 = (bf16[128,1280]{1,0:T(8,128)(2,1)}, bf16[128,1280]{1,0:T(8,128)(2,1)}, u32[]{:S(2)}, u32[]{:S(2)}) collective-permute-start(bf16[128,1280]{1,0:T(8,128)(2,1)} %get-tuple-element.79), channel_id=1, source_target_pairs={{0,4},{1,5},{2,6},{3,7},{4,0},{5,1},{6,2},{7,3},{8,12},{9,13},{10,... | collective-permute-start | bytes 983048 | tf_op jit(solution)/shard_map/ppermute | solution.py:391
  189.6 36.0 %collective-permute-start.52 = (bf16[128,1280]{1,0:T(8,128)(2,1)}, bf16[128,1280]{1,0:T(8,128)(2,1)}, u32[]{:S(2)}, u32[]{:S(2)}) collective-permute-start(bf16[128,1280]{1,0:T(8,128)(2,1)} %get-tuple-element.80), channel_id=1, source_target_pairs={{0,5},{1,4},{2,7},{3,6},{4,1},{5,0},{6,3},{7,2},{8,13},{9,12},{10,... | collective-permute-start | bytes 983048 | tf_op jit(solution)/shard_map/ppermute | solution.py:391
  199.0 26.6 %collective-permute-start.53 = (bf16[128,1280]{1,0:T(8,128)(2,1)}, bf16[128,1280]{1,0:T(8,128)(2,1)}, u32[]{:S(2)}, u32[]{:S(2)}) collective-permute-start(bf16[128,1280]{1,0:T(8,128)(2,1)} %get-tuple-element.81), channel_id=1, source_target_pairs={{0,6},{1,7},{2,4},{3,5},{4,2},{5,3},{6,0},{7,1},{8,14},{9,15},{10,... | collective-permute-start | bytes 983048 | tf_op jit(solution)/shard_map/ppermute | solution.py:391
  199.0 26.6 %collective-permute-start.54 = (bf16[128,1280]{1,0:T(8,128)(2,1)}, bf16[128,1280]{1,0:T(8,128)(2,1)}, u32[]{:S(2)}, u32[]{:S(2)}) collective-permute-start(bf16[128,1280]{1,0:T(8,128)(2,1)} %get-tuple-element.82), channel_id=1, source_target_pairs={{0,7},{1,6},{2,5},{3,4},{4,3},{5,2},{6,1},{7,0},{8,15},{9,14},{10,... | collective-permute-start | bytes 983048 | tf_op jit(solution)/shard_map/ppermute | solution.py:391
  212.6 24.6 %collective-permute-start.36 = (bf16[64,64]{1,0:T(8,128)(2,1)}, bf16[64,64]{1,0:T(8,128)(2,1)}, u32[]{:S(2)}, u32[]{:S(2)}) collective-permute-start(bf16[64,64]{1,0:T(8,128)(2,1)} %get-tuple-element.124), channel_id=1, source_target_pairs={{0,1},{1,0},{2,3},{3,2},{4,5},{5,4},{6,7},{7,6},{8,9},{9,8},{10,11... | collective-permute-start | bytes 24584 | tf_op jit(solution)/shard_map/ppermute | solution.py:391
  223.9 20.5 %collective-permute-start.18 = (bf16[2,256,128]{2,1,0:T(8,128)(2,1)}, bf16[2,256,128]{2,1,0:T(8,128)(2,1)S(1)}, u32[]{:S(2)}, u32[]{:S(2)}) collective-permute-start(bf16[2,256,128]{2,1,0:T(8,128)(2,1)} %get-tuple-element.70), channel_id=1, source_target_pairs={{0,8},{8,0},{16,24},{24,16},{1,9},{9,1},{17,25},{25,17},{2,10},{10... | collective-permute-start | bytes 393224 | tf_op jit(solution)/shard_map/ppermute | solution.py:405
  235.0 38.8 %collective-permute-start.55 = (bf16[2,256,1280]{2,1,0:T(8,128)(2,1)}, bf16[2,256,1280]{2,1,0:T(8,128)(2,1)S(1)}, u32[]{:S(2)}, u32[]{:S(2)}) collective-permute-start(bf16[2,256,1280]{2,1,0:T(8,128)(2,1)} %get-tuple-element.84), channel_id=1, source_target_pairs={{0,8},{8,0},{16,24},{24,16},{1,9},{9,1},{17,25},{25,17},{2,10},{10... | collective-permute-start | bytes 3932168 | tf_op jit(solution)/shard_map/ppermute | solution.py:405
  244.4 21.3 %collective-permute-start.19 = (bf16[1,256,128]{2,1,0:T(8,128)(2,1)S(1)}, bf16[1,256,128]{2,1,0:T(8,128)(2,1)S(1)}, u32[]{:S(2)}, u32[]{:S(2)}) collective-permute-start(bf16[1,256,128]{2,1,0:T(8,128)(2,1)S(1)} %dynamic-slice_convert_fusion.3), channel_id=1, source_target_pairs={{0,16},{8,24},{16,0},{24,8},{1,17},{9,25},{17,1},{25,9},{2,18},{10... | collective-permute-start | bytes 196616 | tf_op jit(solution)/shard_map/ppermute | solution.py:409
  272.2 36.3 %collective-permute-start.26 = (bf16[64,128]{1,0:T(8,128)(2,1)S(1)}, bf16[64,128]{1,0:T(8,128)(2,1)S(1)}, u32[]{:S(2)}, u32[]{:S(2)}) collective-permute-start(bf16[64,128]{1,0:T(8,128)(2,1)S(1)} %get-tuple-element.126), channel_id=1, source_target_pairs={{0,7},{1,6},{2,5},{3,4},{4,3},{5,2},{6,1},{7,0},{8,15},{9,14},{10,... | collective-permute-start | bytes 49160 | tf_op jit(solution)/shard_map/ppermute | solution.py:391
  274.2 32.3 %collective-permute-start.56 = (bf16[1,256,1280]{2,1,0:T(8,128)(2,1)S(1)}, bf16[1,256,1280]{2,1,0:T(8,128)(2,1)S(1)}, u32[]{:S(2)}, u32[]{:S(2)}) collective-permute-start(bf16[1,256,1280]{2,1,0:T(8,128)(2,1)S(1)} %dynamic-slice_convert_fusion), channel_id=1, source_target_pairs={{0,16},{8,24},{16,0},{24,8},{1,17},{9,25},{17,1},{25,9},{2,18},{10... | collective-permute-start | bytes 1966088 | tf_op jit(solution)/shard_map/ppermute | solution.py:409
  313.6 12.9 %collective-permute-start.63 = (bf16[64,1280]{1,0:T(8,128)(2,1)S(1)}, bf16[64,1280]{1,0:T(8,128)(2,1)S(1)}, u32[]{:S(2)}, u32[]{:S(2)}) collective-permute-start(bf16[64,1280]{1,0:T(8,128)(2,1)S(1)} %get-tuple-element.97), channel_id=1, source_target_pairs={{0,7},{1,6},{2,5},{3,4},{4,3},{5,2},{6,1},{7,0},{8,15},{9,14},{10,... | collective-permute-start | bytes 491528 | tf_op jit(solution)/shard_map/ppermute | solution.py:391
  (91 other events, 852.9 us)
Sparse Core Ops, SparseCore 0:
  113.9 38.9 all-gather.4
  155.4 54.7 all-gather.6

commit v2 on v1

v2 whole, which is shorter than its diff:
```python
import functools

import jax
import jax.numpy as jnp
from jax import lax
from jax.experimental import pallas as pl
from jax.experimental.pallas import tpu as pltpu
from jax.sharding import Mesh
from jax.sharding import PartitionSpec as P

HEADS = 16
HD = 64
GROUPS = 2
PER = HEADS // GROUPS
LAT = 256
DOCS = 8
LANE = 128
CHUNK = 256

F32 = jnp.float32
BF16 = jnp.bfloat16
eps = 1e-05
scale = 0.125
masked = -1e30

SEQ = ("z", "x", "core")
PLANE = ("x", "batch")
FOUR = 4
TILES = 6
WIDE = TILES * LANE

VM = pl.BlockSpec(memory_space=pltpu.VMEM)
SM = pl.BlockSpec(memory_space=pltpu.SMEM)
ANY = pl.BlockSpec(memory_space=pl.ANY)
MIB = 1024 * 1024


def nn(left, right):
    return jnp.dot(left, right, preferred_element_type=F32)


def tn(left, right):
    return lax.dot_general(left, right, (((0,), (0,)), ((), ())), preferred_element_type=F32)


def nt(left, right):
    return lax.dot_general(left, right, (((1,), (1,)), ((), ())), preferred_element_type=F32)


def shape(dims, dtype):
    return jax.ShapeDtypeStruct(dims, dtype)


def cost(micros):
    return pl.CostEstimate(flops=0, bytes_accessed=int(micros * 3.6e6), transcendentals=0)


def call(kernel, name, ins, specs, outs, scratch=(), after=(), room=8, micros=0.01):
    count, extra = len(ins), len(after)

    def body(*refs):
        kernel(*refs[:count], *refs[count + extra :])

    return pl.pallas_call(
        body,
        out_shape=tuple(outs),
        in_specs=list(specs) + [ANY] * extra,
        out_specs=(VM,) * len(outs),
        scratch_shapes=list(scratch),
        compiler_params=pltpu.CompilerParams(vmem_limit_bytes=room * MIB),
        cost_estimate=cost(micros),
        name=name,
    )(*ins, *after)


def gain_row(gain):
    return gain[...].astype(F32)[None]


def norm_forward(hidden, gain):
    inverse = lax.rsqrt(jnp.mean(hidden * hidden, axis=-1, keepdims=True) + eps)
    return (hidden * inverse * gain, inverse)


def norm_backward(hidden, gain, inverse, grad):
    scaled = grad * gain
    gain_grad = jnp.sum(grad * hidden * inverse, axis=0, keepdims=True)
    cubed = inverse * inverse * inverse
    hidden_grad = inverse * scaled - hidden * cubed * jnp.mean(
        scaled * hidden, axis=-1, keepdims=True
    )
    return (hidden_grad, gain_grad)


def by_core(value, nz):
    size = value.shape[0] // (nz * 4)
    rows = [value[i * size : (i + 1) * size] for i in range(nz * 4)]
    return jnp.concatenate(rows[0::2] + rows[1::2], axis=0)


def doc_bounds(sc, tok):
    first = sc[0]
    query = first + lax.broadcasted_iota(jnp.int32, (1, tok), 1)
    begin = jnp.zeros((1, tok), jnp.int32)
    low = jnp.int32(0)
    end = jnp.int32(0)
    for d in range(DOCS):
        end = end + sc[8 + d]
        begin = jnp.where(query >= end, end, begin)
        low = jnp.where(first >= end, end, low)
    begin = jnp.where(query >= end, query, begin)
    low = jnp.where(first >= end, first, low)
    return query, begin, low // CHUNK, (first + tok - 1) // CHUNK + 1


def chunk_bias(chunk, query, begin):
    key = chunk * CHUNK + lax.broadcasted_iota(jnp.int32, (CHUNK, LANE), 0)
    bias = jnp.where((key >= begin) & (key <= query), 0.0, masked)
    return jnp.concatenate([bias] * PER, axis=1)


def attend_kernel(
    nz, relative, sc, k00, k01, k10, k11, qp, hidden, wo, gain,
    kvs, ot, logs, left_o, left_n, mid, normed, top, total, acc, mixed_all, wo_s, sem,
):
    load = pltpu.make_async_copy(wo, wo_s, sem)
    load.start()
    tok = hidden.shape[0]
    z, x, core = sc[1], sc[2], sc[3]
    for rc, rx, ref in ((0, 0, k00), (0, 1, k01), (1, 0, k10), (1, 1, k11)):
        for k in range(nz):
            where_z = z - k if relative else k
            slot = (where_z * 2 + (rx ^ x)) * 2 + (rc ^ core)

            @pl.when(where_z >= 0)
            def _():
                kvs[pl.ds(pl.multiple_of(slot * tok, tok), tok), :] = ref[k]

    query, begin, low, high = doc_bounds(sc, tok)
    top[...] = jnp.full(top.shape, masked, F32)
    total[...] = jnp.zeros(total.shape, F32)
    acc[...] = jnp.zeros(acc.shape, F32)

    @pl.loop(low, high)
    def _(chunk):
        kv = kvs[pl.ds(pl.multiple_of(chunk * CHUNK, CHUNK), CHUNK), :]
        bias = chunk_bias(chunk, query, begin)
        for g in range(GROUPS):
            part = kv[:, g * LANE : (g + 1) * LANE]
            raw = nn(part, qp[g]) + bias
            old = top[g]
            new = jnp.maximum(old, jnp.max(raw, axis=0, keepdims=True))
            prob = jnp.exp(raw - new)
            fade = jnp.exp(old - new)
            top[g] = new
            total[g] = total[g] * fade + jnp.sum(prob, axis=0, keepdims=True)
            acc[g] = acc[g] * fade + tn(part, prob.astype(BF16))

    for g in range(GROUPS):
        mixed = acc[g, HD : 2 * HD, :] * (1.0 / total[g])
        ot[g] = mixed
        logs[g] = top[g] + jnp.log(total[g])
        for h in range(PER):
            row = (g * PER + h) * HD
            mixed_all[row : row + HD, :] = mixed[:, h * LANE : (h + 1) * LANE]
    every = mixed_all[...]
    left_o[...] = by_core(every, nz).astype(BF16)
    load.wait()
    middle = hidden[...].astype(F32) + tn(every.astype(BF16), wo_s[...])
    mid[...] = middle
    value, unused = norm_forward(middle, gain_row(gain))
    normed[...] = value.astype(BF16)
    left_n[...] = by_core(value.T, nz).astype(BF16)


def attend(sc, kv_parts, qp, hidden, wo, gain, nz, relative, after=()):
    tok, width = hidden.shape
    left = shape((width, tok), BF16)
    return call(
        functools.partial(attend_kernel, nz, relative),
        "attend",
        (sc, *kv_parts, qp, hidden, wo, gain),
        [SM] + [VM] * 6 + [ANY, VM],
        (
            shape((nz * 4 * tok, 2 * LANE), BF16),
            shape((GROUPS, HD, PER * tok), F32),
            shape((GROUPS, 1, PER * tok), F32),
            left,
            left,
            shape((tok, width), F32),
            shape((tok, width), BF16),
        ),
        [
            pltpu.VMEM((GROUPS, 1, PER * tok), F32),
            pltpu.VMEM((GROUPS, 1, PER * tok), F32),
            pltpu.VMEM((GROUPS, 2 * HD, PER * tok), F32),
            pltpu.VMEM((HEADS * HD, tok), F32),
            pltpu.VMEM(wo.shape, BF16),
            pltpu.SemaphoreType.DMA,
        ],
        after,
        60,
    )


def start_tile(place):
    return (place * 11) // 2


def feed_kernel(tile, sc, normed, grad_out, mid, gain, wo, wg, wu, wd, *rest):
    sends = rest[:FOUR]
    output, dmid, dop, gain_grad = rest[FOUR : FOUR + 4]
    vg, vu, vd, vo, dgate_s, dup_s, act_s, sems = rest[FOUR + 4 :]
    steps = wd.shape[0] // tile
    copies = []
    for t in range(steps):
        span = pl.ds(t * tile, tile)
        copies.append(
            (
                pltpu.make_async_copy(wg.at[:, span], vg.at[:, span], sems.at[0, t]),
                pltpu.make_async_copy(wu.at[:, span], vu.at[:, span], sems.at[1, t]),
                pltpu.make_async_copy(wd.at[span, :], vd.at[span, :], sems.at[2, t]),
            )
        )
    copies.append((pltpu.make_async_copy(wo, vo, sems.at[3, 0]),))
    for group in copies:
        for copy in group:
            copy.start()
    n2 = normed[...]
    dy = grad_out[...]
    for t in range(steps):
        span = slice(t * tile, (t + 1) * tile)
        for copy in copies[t]:
            copy.wait()
        gate = nn(n2, vg[:, span])
        upper = nn(n2, vu[:, span])
        d_act = nt(dy, vd[span, :])
        sigma = jax.nn.sigmoid(gate)
        swish = gate * sigma
        act_s[:, span] = (swish * upper).astype(BF16)
        dgate_s[:, span] = (d_act * upper * sigma * (1.0 + gate * (1.0 - sigma))).astype(BF16)
        dup_s[:, span] = (d_act * swish).astype(BF16)
    copies[steps][0].wait()
    middle = mid[...]
    output[...] = (middle + nn(act_s[...], vd[...])).astype(BF16)
    back = nt(dgate_s[...], vg[...]) + nt(dup_s[...], vu[...])
    inverse = lax.rsqrt(jnp.mean(middle * middle, axis=-1, keepdims=True) + eps)
    grad, gains = norm_backward(middle, gain_row(gain), inverse, back)
    grad = grad + dy.astype(F32)
    dmid[...] = grad
    gain_grad[...] = gains
    for k in range(FOUR):
        cols = pl.ds(pl.multiple_of(start_tile(sc[4] ^ k) * LANE, LANE), WIDE)
        for i, ref in enumerate((dgate_s, dup_s, act_s)):
            sends[k][:, i * WIDE : (i + 1) * WIDE] = ref[:, cols]
    turned = nt(vo[...], grad.astype(BF16)).astype(BF16)
    dop[:, 0:HD, :] = jnp.zeros((GROUPS, HD, dop.shape[2]), BF16)
    for g in range(GROUPS):
        for h in range(PER):
            row = (g * PER + h) * HD
            dop[g, HD:, h * LANE : (h + 1) * LANE] = turned[row : row + HD, :]


def feed(sc, normed, grad_out, mid, gain, wo, wg, wu, wd, after=()):
    tok, width = normed.shape
    hidden = wg.shape[1]
    tile = 2 * LANE
    return call(
        functools.partial(feed_kernel, tile),
        "feed",
        (sc, normed, grad_out, mid, gain, wo, wg, wu, wd),
        [SM] + [VM] * 4 + [ANY] * 4,
        (shape((tok, 3 * WIDE), BF16),) * FOUR
        + (
            shape((tok, width), BF16),
            shape((tok, width), F32),
            shape((GROUPS, 2 * HD, PER * tok), BF16),
            shape((1, width), F32),
        ),
        [
            pltpu.VMEM((width, hidden), BF16),
            pltpu.VMEM((width, hidden), BF16),
            pltpu.VMEM((hidden, width), BF16),
            pltpu.VMEM((width, width), BF16),
            pltpu.VMEM((tok, hidden), BF16),
            pltpu.VMEM((tok, hidden), BF16),
            pltpu.VMEM((tok, hidden), BF16),
            pltpu.SemaphoreType.DMA((4, hidden // tile)),
        ],
        after,
        60,
    )


def back_kernel(
    nz, sc, kvs, qp, dop, ot, logs, dq, keep_own, keep_far, send_own, send_far, acc, rows, block
):
    tok = dq.shape[0]
    x, core = sc[2], sc[3]

    @pl.loop(0, nz)
    def _(i):
        for ref in (keep_own, keep_far, send_own, send_far):
            ref[i] = jnp.zeros(ref.shape[1:], BF16)

    query, begin, low, high = doc_bounds(sc, tok)
    acc[...] = jnp.zeros(acc.shape, F32)
    for g in range(GROUPS):
        rows[g] = jnp.sum(dop[g, HD:, :].astype(F32) * ot[g], axis=0, keepdims=True)

    @pl.loop(low, high)
    def _(chunk):
        kv = kvs[pl.ds(pl.multiple_of(chunk * CHUNK, CHUNK), CHUNK), :]
        bias = chunk_bias(chunk, query, begin)
        for g in range(GROUPS):
            part = kv[:, g * LANE : (g + 1) * LANE]
            prob = jnp.exp(nn(part, qp[g]) + bias - logs[g])
            slope = (prob * (nn(part, dop[g]) - rows[g])).astype(BF16)
            block[:, g * LANE : (g + 1) * LANE] = nt(slope, qp[g]) + nt(prob.astype(BF16), dop[g])
            acc[g] += tn(part, slope)
        where_z = chunk // 2
        near = (chunk % 2) == x
        mine = block[pl.ds(pl.multiple_of(core * tok, tok), tok), :].astype(BF16)
        other = block[pl.ds(pl.multiple_of((1 - core) * tok, tok), tok), :].astype(BF16)

        @pl.when(near)
        def _():
            keep_own[where_z] = mine
            send_own[where_z] = other

        @pl.when(jnp.logical_not(near))
        def _():
            keep_far[where_z] = mine
            send_far[where_z] = other

    for g in range(GROUPS):
        for h in range(0, PER, 2):
            pair = [acc[g, 0:HD, (h + i) * LANE : (h + i + 1) * LANE] for i in range(2)]
            col = (g * PER + h) * HD
            dq[:, col : col + LANE] = (jnp.concatenate(pair, axis=0).T * scale).astype(BF16)


def attend_back(sc, kvs, qp, dop, ot, logs, nz, tok, after=()):
    part = shape((nz, tok, 2 * LANE), BF16)
    return call(
        functools.partial(back_kernel, nz),
        "attend_back",
        (sc, kvs, qp, dop, ot, logs),
        [SM] + [VM] * 5,
        (shape((tok, HEADS * HD), BF16), part, part, part, part),
        [
            pltpu.VMEM((GROUPS, 2 * HD, PER * tok), F32),
            pltpu.VMEM((GROUPS, 1, PER * tok), F32),
            pltpu.VMEM((CHUNK, 2 * LANE), F32),
        ],
        after,
        60,
        9,
    )


def stack_kernel(*refs):
    for k, ref in enumerate(refs[:-1]):
        refs[-1][k] = ref[...]


def stack(arrays, after=()):
    dims = (len(arrays),) + arrays[0].shape
    return call(
        stack_kernel, "stack", arrays, [VM] * len(arrays), (shape(dims, BF16),), after=after
    )[0]


def kv_add_kernel(keep_own, keep_far, came_own, came_far, rest, side):
    rest[...] = keep_own[...].astype(F32) + came_own[...].astype(F32)
    side[...] = (keep_far[...].astype(F32) + came_far[...].astype(F32)).astype(BF16)


def kv_add(terms, after=()):
    dims = terms[0].shape
    return call(
        kv_add_kernel, "kv_add", terms, [VM] * 4, (shape(dims, F32), shape(dims, BF16)),
        after=after, room=60,
    )


def kv_split_kernel(sc, rest, came, own, *sends):
    z = sc[1]
    own[...] = rest[z] + came[z].astype(F32)
    for k, ref in enumerate(sends):
        at = jnp.maximum(z - k - 1, 0)
        ref[...] = (rest[at] + came[at].astype(F32)).astype(BF16)


def kv_split(sc, rest, came, after=()):
    nz, tok, width = rest.shape
    block = (tok, width)
    return call(
        kv_split_kernel,
        "kv_split",
        (sc, rest, came),
        [SM, VM, VM],
        (shape(block, F32),) + (shape(block, BF16),) * (nz - 1),
        after=after,
    )


def weight_kernel(counts, groups, extra, sc, *refs):
    lefts = []
    for count, unused in counts:
        lefts.append(refs[:count])
        refs = refs[count:]
    rights, refs = refs[:FOUR], refs[FOUR:]
    added, refs = refs[:extra], refs[extra:]
    outs, (wide, tall, sems) = refs[: 2 * len(groups)], refs[2 * len(groups) :]
    tok = rights[0].shape[0]
    copies = []
    for k in range(FOUR):
        span = pl.ds(k * tok, tok)
        copies.append(
            pltpu.make_async_copy(rights[k], tall.at[span, :], sems.at[len(counts), k])
        )
        for i, (count, kind) in enumerate(counts):
            if count == FOUR:
                source = lefts[i][k]
            elif kind is None:
                source = lefts[i][0].at[sc[4] ^ k]
            else:
                source = lefts[i][0].at[sc[4] ^ k, kind]
            copies.append(pltpu.make_async_copy(source, wide.at[i, :, span], sems.at[i, k]))
    for copy in copies:
        copy.start()
    for copy in copies:
        copy.wait()
    core = sc[3]
    half = wide.shape[1] // 2
    for i, group in enumerate(groups):
        first = group[0][1]
        for ref, where in ((outs[2 * i + 1], 1 - core), (outs[2 * i], core)):
            rows = pl.ds(pl.multiple_of(where * half, half), half)
            for index, begin, stop in group:
                for at in range(begin, stop, CHUNK):
                    upto = min(at + CHUNK, stop)
                    block = nn(wide[index, rows, :], tall[:, at:upto])
                    ref[:, at - first : upto - first] = block.astype(BF16)
            for other in added:
                ref[:, group[-1][2] - first :] = other[rows, :]


def weight_terms(sc, lefts, rights, groups, extra=(), after=()):
    tok, width = rights[0].shape
    rows = lefts[0][1][0].shape[-2]
    more = sum(array.shape[1] for array in extra)
    counts = tuple((len(arrays), kind) for kind, arrays in lefts)
    flat = [array for unused, arrays in lefts for array in arrays] + rights
    outs = ()
    for group in groups:
        outs += (shape((rows // 2, group[-1][2] - group[0][1] + more), BF16),) * 2
    return call(
        functools.partial(weight_kernel, counts, groups, len(extra)),
        "weight_terms",
        (sc, *flat, *extra),
        [SM] + [ANY] * len(flat) + [VM] * len(extra),
        outs,
        [
            pltpu.VMEM((len(lefts), rows, FOUR * tok), BF16),
            pltpu.VMEM((FOUR * tok, width), BF16),
            pltpu.SemaphoreType.DMA((len(lefts) + 1, FOUR)),
        ],
        after,
        16,
    )


def halve_kernel(step, sc, kept, came, keep, send):
    bit = (sc[1] >> step) & 1

    @pl.loop(0, keep.shape[0])
    def _(i):
        for ref, half in ((send, 1 - bit), (keep, bit)):
            total = kept[2 * i + half].astype(F32) + came[2 * i + half].astype(F32)
            ref[i] = total.astype(BF16)


def halve(sc, kept, came, step, after=()):
    half = shape((kept.shape[0] // 2,) + kept.shape[1:], BF16)
    return call(
        functools.partial(halve_kernel, step),
        "halve", (sc, kept, came), [SM, VM, VM], (half, half), after=after,
    )


def split_kernel(sc, *refs):
    ins, (mine, other, total) = refs[:-3], refs[-3:]
    rows = mine.shape[0]
    value = ins[0][...].astype(F32)
    for ref in ins[1:]:
        value = value + ref[...].astype(F32)
    total[...] = value
    x = sc[2]
    for ref, at in ((mine, x), (other, 1 - x)):
        ref[...] = total[pl.ds(pl.multiple_of(at * rows, rows), rows), :].astype(BF16)


def split_rows(sc, terms, after=()):
    rows, width = terms[0].shape
    mine, other = call(
        split_kernel, "split_rows", (sc, *terms), [SM] + [VM] * len(terms),
        (shape((rows // 2, width), BF16),) * 2,
        [pltpu.VMEM((rows, width), F32)], after=after,
    )
    return plane_swap([mine, mine, other, other])


def swap(value, axis):
    return lax.ppermute(value, axis, [(0, 1), (1, 0)])


def plane_swap(parts):
    moved = [parts[0]]
    for k in range(1, FOUR):
        moved.append(lax.ppermute(parts[k], PLANE, [(d, d ^ k) for d in range(FOUR)]))
    return moved


def put_tiles(place, part, ref):
    start = start_tile(place)
    twice = (place > 0) & (start < start_tile(place - 1) + TILES)
    for i in range(TILES):

        @pl.when(jnp.logical_not(twice) if i == 0 else start >= 0)
        def _():
            cols = pl.ds(pl.multiple_of((start + i) * LANE, LANE), LANE)
            ref[:, cols] = part[:, i * LANE : (i + 1) * LANE]


def place_kernel(plan, sc, *refs):
    parts = refs[:FOUR]
    outs = refs[FOUR:]
    for k in range(FOUR):
        place = sc[4] ^ k
        part = parts[k][...].astype(F32)
        for (begin, stop, tiled), ref in zip(plan, outs):
            size = stop - begin
            if tiled:
                put_tiles(place, part[:, begin:stop], ref)
            else:
                ref[:, pl.ds(pl.multiple_of(place * size, size), size)] = part[:, begin:stop]
    if len(outs) > len(plan):
        expand, gains = outs[len(plan) :]
        begin = plan[-1][1]
        total = [None] * FOUR
        for k in range(FOUR):
            total[k] = parts[k][:, begin:].astype(F32)
        even = [jnp.where(sc[4] % 2 == 0, total[i], total[i + 1]) for i in (0, 2)]
        odd = [jnp.where(sc[4] % 2 == 0, total[i + 1], total[i]) for i in (0, 2)]
        value = (even[0] + odd[0]) + (even[1] + odd[1])
        size = expand.shape[0]
        for j in range(FOUR):
            expand[:, j * HD : (j + 1) * HD] = value[j * size : (j + 1) * size, :HD]
        gains[...] = value.T[HD : HD + 8, :]


def put(sc, parts, plan, widths, small=0, after=()):
    rows = parts[0].shape[0]
    outs = tuple(shape((rows, width), F32) for width in widths)
    if small:
        outs += (shape((rows // FOUR, small), F32), shape((8, rows), F32))
    return call(
        functools.partial(place_kernel, plan), "put", (sc, *parts), [SM] + [VM] * FOUR,
        outs, after=after,
    )


def enter_kernel(hidden, gain, wl, we, normed, latent, kv):
    value, unused = norm_forward(hidden[...].astype(F32), gain_row(gain))
    low = value.astype(BF16)
    normed[...] = low
    rows = nn(low, wl[...]).astype(BF16)
    latent[...] = rows
    for g in range(GROUPS):
        span = slice(g * LANE, (g + 1) * LANE)
        kv[:, span] = nn(rows[:, g * LAT : (g + 1) * LAT], we[:, span]).astype(BF16)


def enter(hidden, gain, wl, we):
    tok, width = hidden.shape
    return call(
        enter_kernel,
        "enter",
        (hidden, gain, wl, we),
        [VM] * 4,
        (
            shape((tok, width), BF16),
            shape((tok, wl.shape[1]), BF16),
            shape((tok, we.shape[1]), BF16),
        ),
        room=60,
    )


def query_kernel(nz, normed, dy, wq, qp, left):
    low = normed[...]
    left[0] = by_core(dy[...].astype(F32).T, nz).astype(BF16)
    left[1] = by_core(low.astype(F32).T, nz).astype(BF16)
    turned = (nn(low, wq[...]).astype(BF16) * scale).T
    qp[:, HD:, :] = jnp.zeros((GROUPS, HD, qp.shape[2]), BF16)
    for g in range(GROUPS):
        for h in range(PER):
            row = (g * PER + h) * HD
            qp[g, 0:HD, h * LANE : (h + 1) * LANE] = turned[row : row + HD, :]


def query(normed, dy, wq, nz, after=()):
    tok, width = normed.shape
    return call(
        functools.partial(query_kernel, nz),
        "query",
        (normed, dy, wq),
        [VM] * 3,
        (
            shape((GROUPS, 2 * HD, PER * tok), BF16),
            shape((2, width, tok), BF16),
        ),
        after=after,
    )


def leave_kernel(nz, count, sc, hidden, dmid, gain, dq, base, latent, gain_two, we, wl, *refs):
    moved = refs[:count]
    input_grad, small = refs[count : count + 2]
    sends = refs[count + 2 : count + 2 + FOUR]
    lat, terms = refs[count + 2 + FOUR :]
    total = moved[0][...].astype(F32)
    for ref in moved[1:]:
        total = total + ref[...].astype(F32)
    kv_grad = total.astype(BF16)
    rows = latent[...]
    expand = []
    for g in range(GROUPS):
        span = slice(g * LANE, (g + 1) * LANE)
        wide = slice(g * LAT, (g + 1) * LAT)
        lat[:, wide] = nt(kv_grad[:, span], we[:, span])
        expand.append(tn(kv_grad[:, span], rows[:, wide]))
    expand = jnp.concatenate(expand, axis=0)
    grad = base[...] + nt(lat[...].astype(BF16), wl[...])
    value = hidden[...].astype(F32)
    inverse = lax.rsqrt(jnp.mean(value * value, axis=-1, keepdims=True) + eps)
    hidden_grad, gains = norm_backward(value, gain_row(gain), inverse, grad)
    input_grad[...] = (hidden_grad + dmid[...]).astype(BF16)
    width = gains.shape[1]
    blank = jnp.zeros((HD, width), F32)
    tail = jnp.zeros((LANE - HD - 2, width), F32)
    terms[...] = jnp.concatenate([blank, gains, gain_two[...], tail], axis=0).T
    count = nz * 4
    size, tall = width // count, expand.shape[0] // count
    for i in range(count):
        for j in range(FOUR):
            at = i * size + j * tall
            terms[at : at + tall, :HD] = expand[i * tall : (i + 1) * tall, j * HD : (j + 1) * HD]
    small[...] = by_core(terms[...], nz).astype(BF16)
    part, half = dq.shape[1] // FOUR, lat.shape[1] // FOUR
    for k in range(FOUR):
        place = sc[4] ^ k
        cols = pl.ds(pl.multiple_of(place * part, part), part)
        sends[k][:, :part] = dmid[:, cols].astype(BF16)
        sends[k][:, part : 2 * part] = dq[:, cols]
        cols = pl.ds(pl.multiple_of(place * half, half), half)
        sends[k][:, 2 * part :] = lat[:, cols].astype(BF16)


def leave(sc, hidden, dmid, gain, dq, base, latent, gain_two, we, wl, moved, nz, after=()):
    tok, width = hidden.shape
    lat = latent.shape[1]
    return call(
        functools.partial(leave_kernel, nz, len(moved)),
        "leave",
        (sc, hidden, dmid, gain, dq, base, latent, gain_two, we, wl, *moved),
        [SM] + [VM] * (9 + len(moved)),
        (shape((tok, width), BF16), shape((width, LANE), BF16))
        + (shape((tok, (2 * width + lat) // FOUR), BF16),) * FOUR,
        [pltpu.VMEM((tok, lat), F32), pltpu.VMEM((width, LANE), F32)],
        after,
        60,
    )


def shards(
    inputs, lengths, proj_query, proj_latent, proj_expand, proj_output,
    ffn_gate, ffn_up, ffn_down, norm_attn, norm_ffn, cotangent,
):
    tok, width = inputs.shape[1:]
    nz = lax.axis_size("z")
    z, x, core, batch = [lax.axis_index(a) for a in ("z", "x", "core", "batch")]
    place = x * 2 + batch
    hidden_size = ffn_gate.shape[1]
    first = ((z * 2 + x) * 2 + core) * tok
    sc = jnp.stack([first, z, x, core, place, place, place, place]).astype(jnp.int32)
    sc = jnp.concatenate([sc, lengths[0]])

    hidden = inputs[0]
    dy = cotangent[0]

    def across(value, step):
        return lax.ppermute(value, "z", [(i, i ^ (1 << step)) for i in range(nz)])

    normed, latent, kv = enter(hidden, norm_attn, proj_latent, proj_expand)
    relative = nz <= 4
    if relative:
        moved = [kv]
        for k in range(1, nz):
            moved.append(lax.ppermute(kv, "z", [(i, i + k) for i in range(nz - k)]))
        k00 = stack(moved, after=(sc,))
    else:
        k00 = lax.all_gather(kv, "z", axis=0)
    qp, left = query(normed, dy, proj_query, nz, after=(k00,))
    early = lax.all_gather(left, PLANE, axis=0)
    k01 = swap(k00, "x")
    k10 = swap(k00, "core")
    k11 = swap(k01, "core")

    kvs, ot, logs, left_o, left_n2, mid, normed_two = attend(
        sc, (k00, k01, k10, k11), qp, hidden, proj_output, norm_ffn, nz, relative
    )
    n2s = plane_swap([left_n2] * FOUR)
    os = lax.all_gather(left_o, PLANE, axis=0)
    fed = feed(sc, normed_two, dy, mid, norm_ffn, proj_output, ffn_gate, ffn_up, ffn_down)
    output, dmid, dop, gain_two = fed[FOUR:]
    parts_a = plane_swap(fed[:FOUR])

    def blocks(value):
        return value.reshape((nz, -1) + value.shape[1:])

    chunks = {}
    last = []

    def begin(name, keep, send):
        chunks[name] = (blocks(keep), blocks(swap(send, "core")), 0)

    def advance(name):
        keep, came, step = chunks[name]
        while True:
            keep, send = halve(sc, keep, came, step, after=last[-1:])
            last.append(keep)
            came = across(send, step)
            step += 1
            if step == 1 or (1 << step) >= nz:
                break
        chunks[name] = (keep, came, step)

    def finish(name):
        keep, came, unused = chunks[name]
        chunks[name] = split_rows(sc, (keep[0], came[0]), after=last[-1:])
        last.append(chunks[name][0])

    def place_out(name, plan, widths, small=0):
        outs = put(sc, chunks[name], plan, widths, small, after=last[-1:])
        last.append(outs[0])
        return outs

    dq, keep_own, keep_far, send_own, send_far = attend_back(
        sc, kvs, qp, dop, ot, logs, nz, tok, after=n2s[1:]
    )
    rest, side = kv_add(
        (keep_own, keep_far, swap(send_own, "core"), swap(send_far, "core")), after=(early,)
    )
    side = swap(side, "x")
    if relative:
        moved = list(kv_split(sc, rest, side, after=parts_a[1:]))
        last.append(moved[0])
        for k in range(1, nz):
            moved[k] = lax.ppermute(moved[k], "z", [(i, i - k) for i in range(k, nz)])
    else:
        term = rest + side.astype(F32)
        moved = [lax.psum_scatter(term, "z", scatter_dimension=0, tiled=False)]
    terms = weight_terms(
        sc,
        ((None, tuple(n2s)), (0, (early,))),
        parts_a,
        (((0, 0, WIDE),), ((0, WIDE, 2 * WIDE),), ((1, 2 * WIDE, 3 * WIDE),)),
        after=last[-1:],
    )
    last.append(terms[0])
    for i, name in enumerate(("gate", "up", "down")):
        begin(name, *terms[2 * i : 2 * i + 2])
    for name in ("gate", "up", "down"):
        advance(name)
    base = nt(dq, proj_query)
    left_out = leave(
        sc, hidden, dmid, norm_attn, dq, base, latent, gain_two, proj_expand, proj_latent,
        moved, nz, after=(last[-1], os),
    )
    input_grad, small = left_out[:2]
    last.append(input_grad)
    parts_c = plane_swap(left_out[2:])
    advance("gate")
    advance("up")
    finish("gate")
    part, lat_part = width // FOUR, latent.shape[1] // FOUR
    end = 2 * part + lat_part
    terms = weight_terms(
        sc,
        ((None, (os,)), (1, (early,))),
        parts_c,
        (((0, 0, part), (1, part, end)),),
        (small,),
        after=last[-1:],
    )
    last.append(terms[0])
    begin("rest", *terms)
    advance("down")
    advance("rest")
    finish("up")
    advance("rest")
    finish("down")
    (grad_gate,) = place_out("gate", ((0, WIDE, True),), (hidden_size,))
    (grad_up,) = place_out("up", ((0, WIDE, True),), (hidden_size,))
    finish("rest")
    (grad_down_t,) = place_out("down", ((0, WIDE, True),), (hidden_size,))
    grad_output, grad_query, grad_latent, expand_t, gains = place_out(
        "rest",
        ((0, part, False), (part, 2 * part, False), (2 * part, end, False)),
        (width, width, latent.shape[1]),
        LAT,
    )
    grad_expand = expand_t.T
    grad_norm_attn, grad_norm_ffn = gains[0], gains[1]
    return (
        output[None],
        input_grad[None],
        grad_query,
        grad_latent,
        grad_expand,
        grad_output,
        grad_gate,
        grad_up,
        grad_down_t.T,
        grad_norm_attn,
        grad_norm_ffn,
    )


def solution(mesh):
    seq, batch = mesh.shape["seq"], mesh.shape["batch"]
    fine = Mesh(mesh.devices.reshape(seq // 4, 2, 2, batch), SEQ + ("batch",))
    return jax.shard_map(
        shards,
        mesh=fine,
        in_specs=(P("batch", SEQ, None), P("batch", None))
        + (P(),) * 9
        + (P("batch", SEQ, None),),
        out_specs=(
            P("batch", SEQ, None),
            P("batch", SEQ, None),
            P(SEQ, None),
            P(SEQ, None),
            P(None, SEQ),
            P(SEQ, None),
            P(SEQ, None),
            P(SEQ, None),
            P(None, SEQ),
            P(SEQ),
            P(SEQ),
        ),
        check_vma=False,
    )
```

time: 339 us -> 224 us (0.66)
  waiting for transfers between devices: 141 us -> 80.8 us
  starting transfers between devices: 79.9 us -> 52.4 us
  local copies, waits for them, and re-layouts: 29.2 us -> 14.1 us
  other arithmetic: 14.1 us -> 0 us
  Pallas kernels: 49.5 us -> 60.2 us
  matrix products: 8.02 us -> 1.63 us
    ppermute x53 -> x32, waiting for transfers between devices: 111 us -> 60.2 us  [the longest x8 29.9 us: across(): return lax.ppermute(value, 'z', [(i, i ^ 1 << step) for i in range(nz)])]
    ppermute x53 -> x32, starting transfers between devices: 60.2 us -> 35.5 us  [the longest x21 25.5 us: plane_swap(): lax.ppermute(parts[k], PLANE, [(d, d ^ k) for d in range(FOUR)])]
    slice x6 -> x0, local copies, waits for them, and re-layouts: 15.6 us -> none  [the longest x3 10.6 us: shards(): dys, n1s = (early[0], early[1])]
    pallas_call x7 -> x27, Pallas kernels: 49.5 us -> 60.2 us  [call(): pl.pallas_call(body, out_shape=tuple(outs), in_specs=list(specs) + [ANY]...]
    all_gather x2, waiting for transfers between devices: 10.6 us -> 0.64 us  [the longest x1 0.64 us: shards(): early = lax.all_gather(left, PLANE, axis=0)]
    unnamed x128 -> x76, local copies, waits for them, and re-layouts: 3.26 us -> 12.8 us
    convert_element_type x10 -> x0, other arithmetic: 6.71 us -> none  [the longest x1 2 us: shards(): term_low = term.astype(BF16)]
    dot_general x6 -> x0, matrix products: 4.52 us -> none  [the longest x4 4.12 us: nn(): return jnp.dot(left, right, preferred_element_type=F32)]
  transfers between devices with their start and end apart: 66 -> 47, of which waited for: 25 -> 22; matrix products, arithmetic and copies ran while one was open for 9% -> 1% of each run, Pallas kernels for 5% -> 23%
where the time goes in v2:
time: 224 us
  waiting for transfers between devices  80.8 us (36%)
  Pallas kernels  60.2 us (27%)
  starting transfers between devices  52.4 us (23%)
  between operations  14.6 us (7%)
  local copies, waits for them, and re-layouts  14.1 us (6%)
    pallas_call x27, Pallas kernels, call(): pl.pallas_call(body, out_shape=tuple(outs), in_specs=list(specs) + [ANY]...  60.2 us
    ppermute x8, waiting for transfers between devices, across(): return lax.ppermute(value, 'z', [(i, i ^ 1 << step) for i in range(nz)])  29.9 us
    ppermute x21, starting transfers between devices, plane_swap(): lax.ppermute(parts[k], PLANE, [(d, d ^ k) for d in range(FOUR)])  25.5 us
    ppermute x21, waiting for transfers between devices, plane_swap(): lax.ppermute(parts[k], PLANE, [(d, d ^ k) for d in range(FOUR)])  19.7 us
    ppermute x10, waiting for transfers between devices, swap(): return lax.ppermute(value, axis, [(0, 1), (1, 0)])  18.5 us
    unnamed x76, local copies, waits for them, and re-layouts  12.8 us
    ppermute x3, starting transfers between devices, shards(): moved.append(lax.ppermute(kv, 'z', [(i, i + k) for i in range(nz - k)]))  10.7 us
    ppermute x3, waiting for transfers between devices, shards(): moved[k] = lax.ppermute(moved[k], 'z', [(i, i - k) for i in range(k, nz)])  10.6 us
  transfers between devices with their start and end apart: 47, of which 22 were waited for; matrix products, arithmetic and copies ran while one was open for 1% of the time, Pallas kernels for 23%

profile of v2, /device:TPU:0, one launch (start us, length us, event | category | flops | bytes accessed | tf_op | source)
XLA Modules:
  0.0 223.7 jit_solution(5665799895291102950)
XLA Ops:
  7.2 2.5 %enter.1 = (bf16[128,1024]{1,0:T(8,128)(2,1)}, bf16[128,512]{1,0:T(8,128)(2,1)}, bf16[128,256]{1,0:T(8,128)(2,1)}) custom-call(bf16[128,1024]{1,0:T(8,128)(2,1)} %bitcast.61, bf16[1024]{0:T(1024)(128)(2,1)} %refs_3_.3, bf16[1024,512]{1,0:T(8,128)(2,1)} %refs_9_.1, bf16[256,256]{1,0:T(8,128)(2,1)} %refs_8_.5), custom_call_target="tpu_custom_call" | custom-call | bytes 36000 | tf_op jit(solution)/shard_map/enter/pallas_call | solution.py:64
  9.7 4.9 %collective-permute-start = (bf16[128,256]{1,0:T(8,128)(2,1)}, bf16[128,256]{1,0:T(8,128)(2,1)S(1)}, u32[]{:S(2)}, u32[]{:S(2)}) collective-permute-start(bf16[128,256]{1,0:T(8,128)(2,1)} %get-tuple-element.85.refs_0_), channel_id=1, source_target_pairs={{0,8},{8,16},{16,24},{1,9},{9,17},{17,25},{2,10},{10,18},{18,26},{... | collective-permute-start | bytes 196616 | tf_op jit(solution)/shard_map/ppermute | solution.py:712
  14.7 4.5 %collective-permute-start.1 = (bf16[128,256]{1,0:T(8,128)(2,1)}, bf16[128,256]{1,0:T(8,128)(2,1)S(1)}, u32[]{:S(2)}, u32[]{:S(2)}) collective-permute-start(bf16[128,256]{1,0:T(8,128)(2,1)} %get-tuple-element.85.refs_0_), channel_id=1, source_target_pairs={{0,16},{8,24},{1,17},{9,25},{2,18},{10,26},{3,19},{11,27},{4,20},{... | collective-permute-start | bytes 196616 | tf_op jit(solution)/shard_map/ppermute | solution.py:712
  23.6 1.7 copy-done.1
  29.8 5.9 %collective-permute-done.3.refs_2_ = bf16[4,128,256]{2,1,0:T(8,128)(2,1)S(1)} collective-permute-done((bf16[4,128,256]{2,1,0:T(8,128)(2,1)S(1)}, bf16[4,128,256]{2,1,0:T(8,128)(2,1)S(1)}, u32[]{:S(2)}, u32[]{:S(2)}) %collective-permute-start.3) | collective-permute-done | bytes 262176 | tf_op jit(solution)/shard_map/ppermute | solution.py:516
  37.9 4.8 %attend.1 = (bf16[2048,256]{1,0:T(8,128)(2,1)}, f32[2,64,1024]{2,1,0:T(8,128)}, f32[2,1,1024]{2,1,0:T(1,128)}, bf16[1024,128]{1,0:T(8,128)(2,1)}, bf16[1024,128]...) custom-call(s32[16]{0:T(128)} %copy-done.21, bf16[4,128,256]{2,1,0:T(8,128)(2,1)} %copy-done.7, ...), custom_call_target="tpu_custom_call" | custom-call | bytes 36000 | tf_op jit(solution)/shard_map/attend/pallas_call | solution.py:64
  44.3 2.7 %collective-permute-start.7 = (bf16[1024,128]{1,0:T(8,128)(2,1)}, bf16[1024,128]{1,0:T(8,128)(2,1)S(1)}, u32[]{:S(2)}, u32[]{:S(2)}) collective-permute-start(bf16[1024,128]{1,0:T(8,128)(2,1)} %get-tuple-element.96.refs_1_), channel_id=1, source_target_pairs={{0,4},{1,5},{4,0},{5,1},{2,6},{3,7},{6,2},{7,3},{8,12},{9,13},{12,... | collective-permute-start | bytes 786440 | tf_op jit(solution)/shard_map/ppermute | solution.py:522
  47.0 15.9 %feed.1 = (bf16[128,2304]{1,0:T(8,128)(2,1)}, bf16[128,2304]{1,0:T(8,128)(2,1)}, bf16[128,2304]{1,0:T(8,128)(2,1)}, bf16[128,2304]{1,0:T(8,128)(2,1)}, bf16[128,...) custom-call(s32[16]{0:T(128)} %copy-done.21, ...), custom_call_target="tpu_custom_call" | custom-call | bytes 36000 | tf_op jit(solution)/shard_map/feed/pallas_call | solution.py:64
  64.4 2.0 collective-permute-start.13
  67.3 4.6 %attend_back.1 = (bf16[128,1024]{1,0:T(8,128)(2,1)}, bf16[4,128,256]{2,1,0:T(8,128)(2,1)}, bf16[4,128,256]{2,1,0:T(8,128)(2,1)}, bf16[4,128,256]{2,1,0:T(8,128)(2,1)}, bf16[4,128,256]{2,1,0:T(8,128)(2,1)}) custom-call(s32[16]{0:T(128)} %copy-done.21, bf16[2048,256]{1,0:T(8,128)(2,1)} %get-tuple-element.92.refs_1_, bf16[2,128,1024]{2,1,0:T(8,128)(2,1)} %copy-done.8, ...), custom_call_target="tpu_custom_call" | custom-call | bytes 32400000 | tf_op jit(solution)/shard_map/attend_back/pallas_call | solution.py:64
  74.8 2.3 %kv_add.1 = (f32[4,128,256]{2,1,0:T(8,128)}, bf16[4,128,256]{2,1,0:T(8,128)(2,1)}) custom-call(bf16[4,128,256]{2,1,0:T(8,128)(2,1)} %get-tuple-element.100.refs_0_, bf16[4,128,256]{2,1,0:T(8,128)(2,1)} %get-tuple-element.101.refs_1_, bf16[4,128,256]{2,1,0:T(8,128)(2,1)} %copy-done.34, bf16[4,128,256]{2,1,0:T(8,128)(2,1)} %copy-done.33, ...), custom_call_target="tpu_custom_call" | custom-call | bytes 36000 | tf_op jit(solution)/shard_map/kv_add/pallas_call | solution.py:64
  77.1 3.4 %collective-permute-start.11 = (bf16[4,128,256]{2,1,0:T(8,128)(2,1)}, bf16[4,128,256]{2,1,0:T(8,128)(2,1)S(1)}, u32[]{:S(2)}, u32[]{:S(2)}) collective-permute-start(bf16[4,128,256]{2,1,0:T(8,128)(2,1)} %get-tuple-element.106), channel_id=1, source_target_pairs={{0,4},{4,0},{1,5},{5,1},{2,6},{6,2},{3,7},{7,3},{8,12},{12,8},{9,1... | collective-permute-start | bytes 786440 | tf_op jit(solution)/shard_map/ppermute | solution.py:516
  80.5 2.6 %collective-permute-done.12.refs_3_.refs_7_ = bf16[128,2304]{1,0:T(8,128)(2,1)S(1)} collective-permute-done((bf16[128,2304]{1,0:T(8,128)(2,1)}, bf16[128,2304]{1,0:T(8,128)(2,1)S(1)}, u32[]{:S(2)}, u32[]{:S(2)}) %collective-permute-start.12) | collective-permute-done | bytes 589856 | tf_op jit(solution)/shard_map/ppermute | solution.py:522
  83.6 12.7 %collective-permute-done.14.refs_5_.refs_9_ = bf16[128,2304]{1,0:T(8,128)(2,1)} collective-permute-done((bf16[128,2304]{1,0:T(8,128)(2,1)}, bf16[128,2304]{1,0:T(8,128)(2,1)}, u32[]{:S(2)}, u32[]{:S(2)}) %collective-permute-start.14) | collective-permute-done | bytes 589856 | tf_op jit(solution)/shard_map/ppermute | solution.py:522
  96.3 7.8 %collective-permute-done.11.refs_2_ = bf16[4,128,256]{2,1,0:T(8,128)(2,1)S(1)} collective-permute-done((bf16[4,128,256]{2,1,0:T(8,128)(2,1)}, bf16[4,128,256]{2,1,0:T(8,128)(2,1)S(1)}, u32[]{:S(2)}, u32[]{:S(2)}) %collective-permute-start.11) | collective-permute-done | bytes 262176 | tf_op jit(solution)/shard_map/ppermute | solution.py:516
  106.5 5.0 %weight_terms.2 = (bf16[512,768]{1,0:T(8,128)(2,1)S(1)}, bf16[512,768]{1,0:T(8,128)(2,1)S(1)}, bf16[512,768]{1,0:T(8,128)(2,1)S(1)}, bf16[512,768]{1,0:T(8,128)(...) custom-call(s32[16]{0:T(128)S(1)} %copy-done.22, bf16[1024,128]{1,0:T(8,128)(2,1)S(1)} %copy-done.24, ...), custom_call_target="tpu_custom_call" | custom-call | bytes 36000 | tf_op jit(solution)/shard_map/weight_terms/pallas_call | solution.py:64
  112.1 1.7 collective-permute-done.20
  120.7 2.6 %collective-permute-start.26 = (bf16[2,128,768]{2,1,0:T(8,128)(2,1)}, bf16[2,128,768]{2,1,0:T(8,128)(2,1)S(1)}, u32[]{:S(2)}, u32[]{:S(2)}) collective-permute-start(bf16[2,128,768]{2,1,0:T(8,128)(2,1)} %get-tuple-element.134), channel_id=1, source_target_pairs={{0,8},{8,0},{16,24},{24,16},{1,9},{9,1},{17,25},{25,17},{2,10},{10... | collective-permute-start | bytes 1179656 | tf_op jit(solution)/shard_map/ppermute | solution.py:705
  127.2 3.2 %collective-permute-done.15.refs_11_ = bf16[128,256]{1,0:T(8,128)(2,1)} collective-permute-done((bf16[128,256]{1,0:T(8,128)(2,1)}, bf16[128,256]{1,0:T(8,128)(2,1)}, u32[]{:S(2)}, u32[]{:S(2)}) %collective-permute-start.15) | collective-permute-done | bytes 65568 | tf_op jit(solution)/shard_map/ppermute | solution.py:772
  130.4 7.4 %collective-permute-done.17.refs_13_ = bf16[128,256]{1,0:T(8,128)(2,1)} collective-permute-done((bf16[128,256]{1,0:T(8,128)(2,1)}, bf16[128,256]{1,0:T(8,128)(2,1)}, u32[]{:S(2)}, u32[]{:S(2)}) %collective-permute-start.17) | collective-permute-done | bytes 65568 | tf_op jit(solution)/shard_map/ppermute | solution.py:772
  137.8 3.8 %leave.1 = (bf16[128,1024]{1,0:T(8,128)(2,1)}, bf16[1024,128]{1,0:T(8,128)(2,1)}, bf16[128,640]{1,0:T(8,128)(2,1)}, bf16[128,640]{1,0:T(8,128)(2,1)}, bf16[128,6...) custom-call(s32[16]{0:T(128)} %copy-done.21, bf16[128,1024]{1,0:T(8,128)(2,1)} %bitcast.63, ...), custom_call_target="tpu_custom_call" | custom-call | bytes 36000 | tf_op jit(solution)/shard_map/leave/pallas_call | solution.py:64
  144.5 1.7 collective-permute-start.22
  148.1 5.4 %collective-permute-done.25 = bf16[1,128,768]{2,1,0:T(8,128)(2,1)S(1)} collective-permute-done((bf16[1,128,768]{2,1,0:T(8,128)(2,1)S(1)}, bf16[1,128,768]{2,1,0:T(8,128)(2,1)S(1)}, u32[]{:S(2)}, u32[]{:S(2)}) %collective-permute-start.25) | collective-permute-done | bytes 196640 | tf_op jit(solution)/shard_map/ppermute | solution.py:705
  154.2 2.9 %weight_terms.3 = (bf16[512,768]{1,0:T(8,128)(2,1)S(1)}, bf16[512,768]{1,0:T(8,128)(2,1)S(1)}) custom-call(s32[16]{0:T(128)S(1)} %copy-done.23, bf16[4,1024,128]{2,1,0:T(8,128)(2,1)S(1)} %bitcast.40, bf16[4,2,1024,128]{3,2,1,0:T(8,128)(2,1)S(1)} %bitcast.38, bf16[128,640]{1,0:T(8,128)(2,1)S(1)} %copy-done.28, ...), custom_call_target="tpu_custom_call" | custom-call | bytes 36000 | tf_op jit(solution)/shard_map/weight_terms/pallas_call | solution.py:64
  157.2 11.4 %collective-permute-done.28.refs_2_ = bf16[2,128,768]{2,1,0:T(8,128)(2,1)S(1)} collective-permute-done((bf16[2,128,768]{2,1,0:T(8,128)(2,1)S(1)}, bf16[2,128,768]{2,1,0:T(8,128)(2,1)S(1)}, u32[]{:S(2)}, u32[]{:S(2)}) %collective-permute-start.28) | collective-permute-done | bytes 393248 | tf_op jit(solution)/shard_map/ppermute | solution.py:705
  173.9 1.7 collective-permute-start.36
  175.6 8.6 %collective-permute-done.30 = bf16[1,128,768]{2,1,0:T(8,128)(2,1)S(1)} collective-permute-done((bf16[1,128,768]{2,1,0:T(8,128)(2,1)S(1)}, bf16[1,128,768]{2,1,0:T(8,128)(2,1)S(1)}, u32[]{:S(2)}, u32[]{:S(2)}) %collective-permute-start.30) | collective-permute-done | bytes 196640 | tf_op jit(solution)/shard_map/ppermute | solution.py:705
  184.8 4.4 %collective-permute-done.29.refs_2_ = bf16[2,128,768]{2,1,0:T(8,128)(2,1)S(1)} collective-permute-done((bf16[2,128,768]{2,1,0:T(8,128)(2,1)S(1)}, bf16[2,128,768]{2,1,0:T(8,128)(2,1)S(1)}, u32[]{:S(2)}, u32[]{:S(2)}) %collective-permute-start.29) | collective-permute-done | bytes 393248 | tf_op jit(solution)/shard_map/ppermute | solution.py:705
  190.0 1.7 collective-permute-start.37
  193.5 1.6 collective-permute-start.34
  200.3 1.7 collective-permute-start.44
  208.3 1.7 collective-permute-start.41
  (170 shorter events, 64.4 us)
Async XLA Ops:
  7.2 67.5 %all-gather.5.cloned.1.call-start = ((), (), s32[]{:S(2)}) async-start(), calls=%async_computation | async-start | bytes 2621440 | tf_op jit(solution)/shard_map/all_gather | solution.py:717
  9.7 11.5 %collective-permute-start = (bf16[128,256]{1,0:T(8,128)(2,1)}, bf16[128,256]{1,0:T(8,128)(2,1)S(1)}, u32[]{:S(2)}, u32[]{:S(2)}) collective-permute-start(bf16[128,256]{1,0:T(8,128)(2,1)} %get-tuple-element.85.refs_0_), channel_id=1, source_target_pairs={{0,8},{8,16},{16,24},{1,9},{9,17},{17,25},{2,10},{10,18},{18,26},{... | collective-permute-start | bytes 196616 | tf_op jit(solution)/shard_map/ppermute | solution.py:712
  28.2 99.0 %all-gather.7.cloned.1.call-start = ((), (), s32[]{:S(2)}) async-start(), calls=%async_computation.1 | async-start | bytes 1310720 | tf_op jit(solution)/shard_map/all_gather | solution.py:726
  42.7 23.8 %collective-permute-start.6 = (bf16[1024,128]{1,0:T(8,128)(2,1)}, bf16[1024,128]{1,0:T(8,128)(2,1)S(1)}, u32[]{:S(2)}, u32[]{:S(2)}) collective-permute-start(bf16[1024,128]{1,0:T(8,128)(2,1)} %get-tuple-element.96.refs_1_), channel_id=1, source_target_pairs={{0,1},{1,0},{4,5},{5,4},{2,3},{3,2},{6,7},{7,6},{8,9},{9,8},{12,13... | collective-permute-start | bytes 786440 | tf_op jit(solution)/shard_map/ppermute | solution.py:522
  44.3 22.2 %collective-permute-start.7 = (bf16[1024,128]{1,0:T(8,128)(2,1)}, bf16[1024,128]{1,0:T(8,128)(2,1)S(1)}, u32[]{:S(2)}, u32[]{:S(2)}) collective-permute-start(bf16[1024,128]{1,0:T(8,128)(2,1)} %get-tuple-element.96.refs_1_), channel_id=1, source_target_pairs={{0,4},{1,5},{4,0},{5,1},{2,6},{3,7},{6,2},{7,3},{8,12},{9,13},{12,... | collective-permute-start | bytes 786440 | tf_op jit(solution)/shard_map/ppermute | solution.py:522
  47.0 19.5 %collective-permute-start.8 = (bf16[1024,128]{1,0:T(8,128)(2,1)}, bf16[1024,128]{1,0:T(8,128)(2,1)S(1)}, u32[]{:S(2)}, u32[]{:S(2)}) collective-permute-start(bf16[1024,128]{1,0:T(8,128)(2,1)} %get-tuple-element.96.refs_1_), channel_id=1, source_target_pairs={{0,5},{1,4},{4,1},{5,0},{2,7},{3,6},{6,3},{7,2},{8,13},{9,12},{12,... | collective-permute-start | bytes 786440 | tf_op jit(solution)/shard_map/ppermute | solution.py:522
  62.9 20.1 %collective-permute-start.12 = (bf16[128,2304]{1,0:T(8,128)(2,1)}, bf16[128,2304]{1,0:T(8,128)(2,1)S(1)}, u32[]{:S(2)}, u32[]{:S(2)}) collective-permute-start(bf16[128,2304]{1,0:T(8,128)(2,1)} %get-tuple-element.107), channel_id=1, source_target_pairs={{0,1},{1,0},{4,5},{5,4},{2,3},{3,2},{6,7},{7,6},{8,9},{9,8},{12,13... | collective-permute-start | bytes 1769480 | tf_op jit(solution)/shard_map/ppermute | solution.py:522
  64.4 19.2 %collective-permute-start.13 = (bf16[128,2304]{1,0:T(8,128)(2,1)}, bf16[128,2304]{1,0:T(8,128)(2,1)S(1)}, u32[]{:S(2)}, u32[]{:S(2)}) collective-permute-start(bf16[128,2304]{1,0:T(8,128)(2,1)} %get-tuple-element.108), channel_id=1, source_target_pairs={{0,4},{1,5},{4,0},{5,1},{2,6},{3,7},{6,2},{7,3},{8,12},{9,13},{12,... | collective-permute-start | bytes 1769480 | tf_op jit(solution)/shard_map/ppermute | solution.py:522
  66.5 29.8 %collective-permute-start.14 = (bf16[128,2304]{1,0:T(8,128)(2,1)}, bf16[128,2304]{1,0:T(8,128)(2,1)}, u32[]{:S(2)}, u32[]{:S(2)}) collective-permute-start(bf16[128,2304]{1,0:T(8,128)(2,1)} %get-tuple-element.109), channel_id=1, source_target_pairs={{0,5},{1,4},{4,1},{5,0},{2,7},{3,6},{6,3},{7,2},{8,13},{9,12},{12,... | collective-permute-start | bytes 1769480 | tf_op jit(solution)/shard_map/ppermute | solution.py:522
  77.1 27.0 %collective-permute-start.11 = (bf16[4,128,256]{2,1,0:T(8,128)(2,1)}, bf16[4,128,256]{2,1,0:T(8,128)(2,1)S(1)}, u32[]{:S(2)}, u32[]{:S(2)}) collective-permute-start(bf16[4,128,256]{2,1,0:T(8,128)(2,1)} %get-tuple-element.106), channel_id=1, source_target_pairs={{0,4},{4,0},{1,5},{5,1},{2,6},{6,2},{3,7},{7,3},{8,12},{12,8},{9,1... | collective-permute-start | bytes 786440 | tf_op jit(solution)/shard_map/ppermute | solution.py:516
  112.0 8.7 %collective-permute-start.18 = (bf16[512,768]{1,0:T(8,128)(2,1)S(1)}, bf16[512,768]{1,0:T(8,128)(2,1)S(1)}, u32[]{:S(2)}, u32[]{:S(2)}) collective-permute-start(bf16[512,768]{1,0:T(8,128)(2,1)S(1)} %get-tuple-element.116), channel_id=1, source_target_pairs={{0,2},{2,0},{1,3},{3,1},{4,6},{6,4},{5,7},{7,5},{8,10},{10,8},{9,1... | collective-permute-start | bytes 2359304 | tf_op jit(solution)/shard_map/ppermute | solution.py:516
  115.3 26.3 %collective-permute-start.24 = (bf16[2,128,768]{2,1,0:T(8,128)(2,1)}, bf16[2,128,768]{2,1,0:T(8,128)(2,1)}, u32[]{:S(2)}, u32[]{:S(2)}) collective-permute-start(bf16[2,128,768]{2,1,0:T(8,128)(2,1)} %get-tuple-element.131), channel_id=1, source_target_pairs={{0,8},{8,0},{16,24},{24,16},{1,9},{9,1},{17,25},{25,17},{2,10},{10... | collective-permute-start | bytes 1179656 | tf_op jit(solution)/shard_map/ppermute | solution.py:705
  115.3 15.1 %collective-permute-start.15 = (bf16[128,256]{1,0:T(8,128)(2,1)}, bf16[128,256]{1,0:T(8,128)(2,1)}, u32[]{:S(2)}, u32[]{:S(2)}) collective-permute-start(bf16[128,256]{1,0:T(8,128)(2,1)} %get-tuple-element.111), channel_id=1, source_target_pairs={{8,0},{16,8},{24,16},{9,1},{17,9},{25,17},{10,2},{18,10},{26,18},{... | collective-permute-start | bytes 196616 | tf_op jit(solution)/shard_map/ppermute | solution.py:772
  116.6 13.8 %collective-permute-start.16 = (bf16[128,256]{1,0:T(8,128)(2,1)}, bf16[128,256]{1,0:T(8,128)(2,1)}, u32[]{:S(2)}, u32[]{:S(2)}) collective-permute-start(bf16[128,256]{1,0:T(8,128)(2,1)} %get-tuple-element.112), channel_id=1, source_target_pairs={{16,0},{24,8},{17,1},{25,9},{18,2},{26,10},{19,3},{27,11},{20,4},{... | collective-permute-start | bytes 196616 | tf_op jit(solution)/shard_map/ppermute | solution.py:772
  117.9 19.9 %collective-permute-start.17 = (bf16[128,256]{1,0:T(8,128)(2,1)}, bf16[128,256]{1,0:T(8,128)(2,1)}, u32[]{:S(2)}, u32[]{:S(2)}) collective-permute-start(bf16[128,256]{1,0:T(8,128)(2,1)} %get-tuple-element.113), channel_id=1, source_target_pairs={{24,0},{25,1},{26,2},{27,3},{28,4},{29,5},{30,6},{31,7}} | collective-permute-start | bytes 196616 | tf_op jit(solution)/shard_map/ppermute | solution.py:772
  120.7 26.7 %collective-permute-start.26 = (bf16[2,128,768]{2,1,0:T(8,128)(2,1)}, bf16[2,128,768]{2,1,0:T(8,128)(2,1)S(1)}, u32[]{:S(2)}, u32[]{:S(2)}) collective-permute-start(bf16[2,128,768]{2,1,0:T(8,128)(2,1)} %get-tuple-element.134), channel_id=1, source_target_pairs={{0,8},{8,0},{16,24},{24,16},{1,9},{9,1},{17,25},{25,17},{2,10},{10... | collective-permute-start | bytes 1179656 | tf_op jit(solution)/shard_map/ppermute | solution.py:705
  143.8 9.7 %collective-permute-start.25 = (bf16[1,128,768]{2,1,0:T(8,128)(2,1)S(1)}, bf16[1,128,768]{2,1,0:T(8,128)(2,1)S(1)}, u32[]{:S(2)}, u32[]{:S(2)}) collective-permute-start(bf16[1,128,768]{2,1,0:T(8,128)(2,1)S(1)} %get-tuple-element.133), channel_id=1, source_target_pairs={{0,16},{8,24},{16,0},{24,8},{1,17},{9,25},{17,1},{25,9},{2,18},{10... | collective-permute-start | bytes 589832 | tf_op jit(solution)/shard_map/ppermute | solution.py:705
  143.9 10.2 %collective-permute-start.21 = (bf16[128,640]{1,0:T(8,128)(2,1)}, bf16[128,640]{1,0:T(8,128)(2,1)S(1)}, u32[]{:S(2)}, u32[]{:S(2)}) collective-permute-start(bf16[128,640]{1,0:T(8,128)(2,1)} %get-tuple-element.127), channel_id=1, source_target_pairs={{0,1},{1,0},{4,5},{5,4},{2,3},{3,2},{6,7},{7,6},{8,9},{9,8},{12,13... | collective-permute-start | bytes 491528 | tf_op jit(solution)/shard_map/ppermute | solution.py:522
  144.5 9.7 %collective-permute-start.22 = (bf16[128,640]{1,0:T(8,128)(2,1)}, bf16[128,640]{1,0:T(8,128)(2,1)S(1)}, u32[]{:S(2)}, u32[]{:S(2)}) collective-permute-start(bf16[128,640]{1,0:T(8,128)(2,1)} %get-tuple-element.128), channel_id=1, source_target_pairs={{0,4},{1,5},{4,0},{5,1},{2,6},{3,7},{6,2},{7,3},{8,12},{9,13},{12,... | collective-permute-start | bytes 491528 | tf_op jit(solution)/shard_map/ppermute | solution.py:522
  157.1 12.3 %collective-permute-start.27 = (bf16[512,768]{1,0:T(8,128)(2,1)S(1)}, bf16[512,768]{1,0:T(8,128)(2,1)S(1)}, u32[]{:S(2)}, u32[]{:S(2)}) collective-permute-start(bf16[512,768]{1,0:T(8,128)(2,1)S(1)} %get-tuple-element.138), channel_id=1, source_target_pairs={{0,2},{2,0},{1,3},{3,1},{4,6},{6,4},{5,7},{7,5},{8,10},{10,8},{9,1... | collective-permute-start | bytes 2359304 | tf_op jit(solution)/shard_map/ppermute | solution.py:516
  157.1 11.5 %collective-permute-start.28 = (bf16[2,128,768]{2,1,0:T(8,128)(2,1)S(1)}, bf16[2,128,768]{2,1,0:T(8,128)(2,1)S(1)}, u32[]{:S(2)}, u32[]{:S(2)}) collective-permute-start(bf16[2,128,768]{2,1,0:T(8,128)(2,1)S(1)} %copy-done.31), channel_id=1, source_target_pairs={{0,8},{8,0},{16,24},{24,16},{1,9},{9,1},{17,25},{25,17},{2,10},{10... | collective-permute-start | bytes 1179656 | tf_op jit(solution)/shard_map/ppermute | solution.py:705
  170.1 19.1 %collective-permute-start.29 = (bf16[2,128,768]{2,1,0:T(8,128)(2,1)S(1)}, bf16[2,128,768]{2,1,0:T(8,128)(2,1)S(1)}, u32[]{:S(2)}, u32[]{:S(2)}) collective-permute-start(bf16[2,128,768]{2,1,0:T(8,128)(2,1)S(1)} %get-tuple-element.142), channel_id=1, source_target_pairs={{0,8},{8,0},{16,24},{24,16},{1,9},{9,1},{17,25},{25,17},{2,10},{10... | collective-permute-start | bytes 1179656 | tf_op jit(solution)/shard_map/ppermute | solution.py:705
  170.4 13.8 %collective-permute-start.30 = (bf16[1,128,768]{2,1,0:T(8,128)(2,1)S(1)}, bf16[1,128,768]{2,1,0:T(8,128)(2,1)S(1)}, u32[]{:S(2)}, u32[]{:S(2)}) collective-permute-start(bf16[1,128,768]{2,1,0:T(8,128)(2,1)S(1)} %get-tuple-element.143), channel_id=1, source_target_pairs={{0,16},{8,24},{16,0},{24,8},{1,17},{9,25},{17,1},{25,9},{2,18},{10... | collective-permute-start | bytes 589832 | tf_op jit(solution)/shard_map/ppermute | solution.py:705
  172.0 21.5 %collective-permute-start.38 = (bf16[1,128,768]{2,1,0:T(8,128)(2,1)S(1)}, bf16[1,128,768]{2,1,0:T(8,128)(2,1)S(1)}, u32[]{:S(2)}, u32[]{:S(2)}) collective-permute-start(bf16[1,128,768]{2,1,0:T(8,128)(2,1)S(1)} %get-tuple-element.149), channel_id=1, source_target_pairs={{0,16},{8,24},{16,0},{24,8},{1,17},{9,25},{17,1},{25,9},{2,18},{10... | collective-permute-start | bytes 589832 | tf_op jit(solution)/shard_map/ppermute | solution.py:705
  173.3 18.3 %collective-permute-start.35 = (bf16[64,768]{1,0:T(8,128)(2,1)S(1)}, bf16[64,768]{1,0:T(8,128)(2,1)S(1)}, u32[]{:S(2)}, u32[]{:S(2)}) collective-permute-start(bf16[64,768]{1,0:T(8,128)(2,1)S(1)} %get-tuple-element.136.refs_8_.refs_1_), channel_id=1, source_target_pairs={{0,1},{1,0},{4,5},{5,4},{2,3},{3,2},{6,7},{7,6},{8,9},{9,8},{12,13... | collective-permute-start | bytes 294920 | tf_op jit(solution)/shard_map/ppermute | solution.py:522
  173.9 19.3 %collective-permute-start.36 = (bf16[64,768]{1,0:T(8,128)(2,1)S(1)}, bf16[64,768]{1,0:T(8,128)(2,1)S(1)}, u32[]{:S(2)}, u32[]{:S(2)}) collective-permute-start(bf16[64,768]{1,0:T(8,128)(2,1)S(1)} %get-tuple-element.148), channel_id=1, source_target_pairs={{0,4},{1,5},{4,0},{5,1},{2,6},{3,7},{6,2},{7,3},{8,12},{9,13},{12,... | collective-permute-start | bytes 294920 | tf_op jit(solution)/shard_map/ppermute | solution.py:522
  189.9 14.8 %collective-permute-start.31 = (bf16[1,128,768]{2,1,0:T(8,128)(2,1)S(1)}, bf16[1,128,768]{2,1,0:T(8,128)(2,1)S(1)}, u32[]{:S(2)}, u32[]{:S(2)}) collective-permute-start(bf16[1,128,768]{2,1,0:T(8,128)(2,1)S(1)} %get-tuple-element.146), channel_id=1, source_target_pairs={{0,16},{8,24},{16,0},{24,8},{1,17},{9,25},{17,1},{25,9},{2,18},{10... | collective-permute-start | bytes 589832 | tf_op jit(solution)/shard_map/ppermute | solution.py:705
  191.7 8.1 %collective-permute-start.32 = (bf16[64,768]{1,0:T(8,128)(2,1)S(1)}, bf16[64,768]{1,0:T(8,128)(2,1)S(1)}, u32[]{:S(2)}, u32[]{:S(2)}) collective-permute-start(bf16[64,768]{1,0:T(8,128)(2,1)S(1)} %get-tuple-element.144.refs_3_.refs_1_), channel_id=1, source_target_pairs={{0,1},{1,0},{4,5},{5,4},{2,3},{3,2},{6,7},{7,6},{8,9},{9,8},{12,13... | collective-permute-start | bytes 294920 | tf_op jit(solution)/shard_map/ppermute | solution.py:522
  193.5 8.5 %collective-permute-start.34 = (bf16[64,768]{1,0:T(8,128)(2,1)S(1)}, bf16[64,768]{1,0:T(8,128)(2,1)S(1)}, u32[]{:S(2)}, u32[]{:S(2)}) collective-permute-start(bf16[64,768]{1,0:T(8,128)(2,1)S(1)} %get-tuple-element.147), channel_id=1, source_target_pairs={{0,5},{1,4},{4,1},{5,0},{2,7},{3,6},{6,3},{7,2},{8,13},{9,12},{12,... | collective-permute-start | bytes 294920 | tf_op jit(solution)/shard_map/ppermute | solution.py:522
  196.6 11.7 %collective-permute-start.42 = (bf16[64,768]{1,0:T(8,128)(2,1)S(1)}, bf16[64,768]{1,0:T(8,128)(2,1)S(1)}, u32[]{:S(2)}, u32[]{:S(2)}) collective-permute-start(bf16[64,768]{1,0:T(8,128)(2,1)S(1)} %get-tuple-element.150.refs_5_.refs_1_), channel_id=1, source_target_pairs={{0,1},{1,0},{4,5},{5,4},{2,3},{3,2},{6,7},{7,6},{8,9},{9,8},{12,13... | collective-permute-start | bytes 294920 | tf_op jit(solution)/shard_map/ppermute | solution.py:522
  199.8 10.2 %collective-permute-start.43 = (bf16[64,768]{1,0:T(8,128)(2,1)S(1)}, bf16[64,768]{1,0:T(8,128)(2,1)S(1)}, u32[]{:S(2)}, u32[]{:S(2)}) collective-permute-start(bf16[64,768]{1,0:T(8,128)(2,1)S(1)} %get-tuple-element.153), channel_id=1, source_target_pairs={{0,4},{1,5},{4,0},{5,1},{2,6},{3,7},{6,2},{7,3},{8,12},{9,13},{12,... | collective-permute-start | bytes 294920 | tf_op jit(solution)/shard_map/ppermute | solution.py:522
  200.3 9.6 %collective-permute-start.44 = (bf16[64,768]{1,0:T(8,128)(2,1)S(1)}, bf16[64,768]{1,0:T(8,128)(2,1)S(1)}, u32[]{:S(2)}, u32[]{:S(2)}) collective-permute-start(bf16[64,768]{1,0:T(8,128)(2,1)S(1)} %get-tuple-element.153), channel_id=1, source_target_pairs={{0,5},{1,4},{4,1},{5,0},{2,7},{3,6},{6,3},{7,2},{8,13},{9,12},{12,... | collective-permute-start | bytes 294920 | tf_op jit(solution)/shard_map/ppermute | solution.py:522
  (53 other events, 411.5 us)
Sparse Core Ops, SparseCore 0:
  28.3 46.3 all-gather.4
  76.6 41.3 all-gather.6

commit v3 on v2

--- a/solution.py
+++ b/solution.py
@@ -32,6 +32,7 @@
 VM = pl.BlockSpec(memory_space=pltpu.VMEM)
 SM = pl.BlockSpec(memory_space=pltpu.SMEM)
 ANY = pl.BlockSpec(memory_space=pl.ANY)
+HB = pl.BlockSpec(memory_space=pltpu.HBM)
 MIB = 1024 * 1024
 
 
@@ -95,7 +96,8 @@
 def by_core(value, nz):
     size = value.shape[0] // (nz * 4)
     rows = [value[i * size : (i + 1) * size] for i in range(nz * 4)]
-    return jnp.concatenate(rows[0::2] + rows[1::2], axis=0)
+    order = [i + j for i in range(0, nz * 4, 4) for j in (0, 2, 1, 3)]
+    return jnp.concatenate([rows[i] for i in order], axis=0)
 
 
 def doc_bounds(sc, tok):
@@ -154,10 +156,10 @@
             fade = jnp.exp(old - new)
             top[g] = new
             total[g] = total[g] * fade + jnp.sum(prob, axis=0, keepdims=True)
-            acc[g] = acc[g] * fade + tn(part, prob.astype(BF16))
+            acc[g] = acc[g] * fade + tn(part[:, HD:], prob.astype(BF16))
 
     for g in range(GROUPS):
-        mixed = acc[g, HD : 2 * HD, :] * (1.0 / total[g])
+        mixed = acc[g] * (1.0 / total[g])
         ot[g] = mixed
         logs[g] = top[g] + jnp.log(total[g])
         for h in range(PER):
@@ -193,7 +195,7 @@
         [
             pltpu.VMEM((GROUPS, 1, PER * tok), F32),
             pltpu.VMEM((GROUPS, 1, PER * tok), F32),
-            pltpu.VMEM((GROUPS, 2 * HD, PER * tok), F32),
+            pltpu.VMEM((GROUPS, HD, PER * tok), F32),
             pltpu.VMEM((HEADS * HD, tok), F32),
             pltpu.VMEM(wo.shape, BF16),
             pltpu.SemaphoreType.DMA,
@@ -371,93 +373,120 @@
     )[0]
 
 
-def kv_add_kernel(keep_own, keep_far, came_own, came_far, rest, side):
-    rest[...] = keep_own[...].astype(F32) + came_own[...].astype(F32)
-    side[...] = (keep_far[...].astype(F32) + came_far[...].astype(F32)).astype(BF16)
-
-
-def kv_add(terms, after=()):
-    dims = terms[0].shape
-    return call(
-        kv_add_kernel, "kv_add", terms, [VM] * 4, (shape(dims, F32), shape(dims, BF16)),
-        after=after, room=60,
-    )
-
-
-def kv_split_kernel(sc, rest, came, own, *sends):
+def kv_cut_kernel(sc, *refs):
+    given, rest = refs[:4], refs[4:]
+    own, sends, held, sems = rest[0], rest[1:-2], rest[-2], rest[-1]
+    copies = [pltpu.make_async_copy(given[i], held.at[i], sems.at[i]) for i in range(4)]
+    for copy in copies:
+        copy.start()
+    for copy in copies:
+        copy.wait()
     z = sc[1]
-    own[...] = rest[z] + came[z].astype(F32)
-    for k, ref in enumerate(sends):
-        at = jnp.maximum(z - k - 1, 0)
-        ref[...] = (rest[at] + came[at].astype(F32)).astype(BF16)
-
-
-def kv_split(sc, rest, came, after=()):
-    nz, tok, width = rest.shape
-    block = (tok, width)
-    return call(
-        kv_split_kernel,
-        "kv_split",
-        (sc, rest, came),
-        [SM, VM, VM],
-        (shape(block, F32),) + (shape(block, BF16),) * (nz - 1),
+    for i in range(2):
+        own[i] = held[i, z].astype(F32) + held[i + 2, z].astype(F32)
+        for k, ref in enumerate(sends):
+            at = jnp.maximum(z - k - 1, 0)
+            ref[i] = (held[i, at].astype(F32) + held[i + 2, at].astype(F32)).astype(BF16)
+
+
+def kv_cut(sc, terms, count, after=()):
+    dims = (2,) + terms[0].shape[1:]
+    return call(
+        kv_cut_kernel, "kv_cut", (sc, *terms), [SM] + [HB] * 4,
+        (shape(dims, F32),) + (shape(dims, BF16),) * count,
+        [pltpu.VMEM((4,) + terms[0].shape, BF16), pltpu.SemaphoreType.DMA((4,))],
+        after=after, room=12,
+    )
+
+
+def base_kernel(dq, wq, base):
+    base[...] = nt(dq[...], wq[...])
+
+
+def base_terms(dq, wq, after=()):
+    return call(
+        base_kernel, "base", (dq, wq), [VM] * 2, (shape((dq.shape[0], wq.shape[0]), F32),),
+        after=after, room=12,
+    )[0]
+
+
+def kv_sum_kernel(*refs):
+    moved, (rest, side) = refs[:-2], refs[-2:]
+    total = moved[0][...].astype(F32)
+    for ref in moved[1:]:
+        total = total + ref[...].astype(F32)
+    rest[...] = total[0]
+    side[...] = total[1].astype(BF16)
+
+
+def kv_sum(moved, after=()):
+    dims = moved[0].shape[1:]
+    return call(
+        kv_sum_kernel, "kv_sum", moved, [VM] * len(moved), (shape(dims, F32), shape(dims, BF16)),
         after=after,
     )
 
 
-def weight_kernel(counts, groups, extra, sc, *refs):
+def weight_kernel(counts, plan, extra, split, sc, *refs):
     lefts = []
-    for count, unused in counts:
+    for count in counts:
         lefts.append(refs[:count])
         refs = refs[count:]
     rights, refs = refs[:FOUR], refs[FOUR:]
     added, refs = refs[:extra], refs[extra:]
-    outs, (wide, tall, sems) = refs[: 2 * len(groups)], refs[2 * len(groups) :]
-    tok = rights[0].shape[0]
+    outs, (wide, tall, made, sems) = refs[:-4], refs[-4:]
+    tok = rights[0].shape[-2]
     copies = []
     for k in range(FOUR):
         span = pl.ds(k * tok, tok)
-        copies.append(
-            pltpu.make_async_copy(rights[k], tall.at[span, :], sems.at[len(counts), k])
-        )
-        for i, (count, kind) in enumerate(counts):
-            if count == FOUR:
-                source = lefts[i][k]
-            elif kind is None:
-                source = lefts[i][0].at[sc[4] ^ k]
-            else:
-                source = lefts[i][0].at[sc[4] ^ k, kind]
+        count = tall.shape[1]
+        pairs = [(rights[k].at[:, 0:count], tall.at[span, :])]
+        for at in range(count, rights[k].shape[1], LANE):
+            which, row = divmod(at - count, wide.shape[1])
+            pairs.append((rights[k].at[:, at : at + LANE], wide.at[which, row : row + LANE, span]))
+        for t, (source, target) in enumerate(pairs):
+            copies.append(pltpu.make_async_copy(source, target, sems.at[len(counts) + t, k]))
+        for i, count in enumerate(counts):
+            if count == 0:
+                continue
+            source = lefts[i][0].at[sc[4] ^ k]
             copies.append(pltpu.make_async_copy(source, wide.at[i, :, span], sems.at[i, k]))
     for copy in copies:
         copy.start()
     for copy in copies:
         copy.wait()
-    core = sc[3]
-    half = wide.shape[1] // 2
-    for i, group in enumerate(groups):
-        first = group[0][1]
-        for ref, where in ((outs[2 * i + 1], 1 - core), (outs[2 * i], core)):
-            rows = pl.ds(pl.multiple_of(where * half, half), half)
-            for index, begin, stop in group:
-                for at in range(begin, stop, CHUNK):
-                    upto = min(at + CHUNK, stop)
-                    block = nn(wide[index, rows, :], tall[:, at:upto])
-                    ref[:, at - first : upto - first] = block.astype(BF16)
-            for other in added:
-                ref[:, group[-1][2] - first :] = other[rows, :]
-
-
-def weight_terms(sc, lefts, rights, groups, extra=(), after=()):
-    tok, width = rights[0].shape
-    rows = lefts[0][1][0].shape[-2]
-    more = sum(array.shape[1] for array in extra)
-    counts = tuple((len(arrays), kind) for kind, arrays in lefts)
+    ref = outs[0] if not split else made
+    for index, begin, stop in plan:
+        for at in range(begin, stop, CHUNK):
+            cols = slice(at, min(at + CHUNK, stop))
+            ref[:, cols] = nn(wide[index], tall[:, cols]).astype(BF16)
+    for other in added:
+        ref[:, plan[-1][2] :] = other[...]
+    if split:
+        keep, send = outs
+        nz, size, unused = keep.shape
+
+        @pl.loop(0, nz)
+        def _(i):
+            for out, where in ((send, 1 - sc[3]), (keep, sc[3])):
+                rows = pl.ds(pl.multiple_of((2 * i + where) * size, size), size)
+                out[i] = made[rows, :]
+
+
+def weight_terms(sc, lefts, rights, plan, extra=(), nz=None, after=()):
+    tok = rights[0].shape[-2]
+    width = plan[-1][2]
+    rows = lefts[0][0]
+    moves = 1 + (rights[0].shape[1] - width) // LANE
+    wide = width + sum(array.shape[1] for array in extra)
+    counts = tuple(len(arrays) for unused, arrays in lefts)
     flat = [array for unused, arrays in lefts for array in arrays] + rights
-    outs = ()
-    for group in groups:
-        outs += (shape((rows // 2, group[-1][2] - group[0][1] + more), BF16),) * 2
-    return call(
-        functools.partial(weight_kernel, counts, groups, len(extra)),
+    if nz:
+        outs = (shape((nz, rows // (2 * nz), wide), BF16),) * 2
+    else:
+        outs = (shape((rows, wide), BF16),)
+    return call(
+        functools.partial(weight_kernel, counts, plan, len(extra), bool(nz)),
         "weight_terms",
         (sc, *flat, *extra),
         [SM] + [ANY] * len(flat) + [VM] * len(extra),
@@ -465,10 +494,11 @@
         [
             pltpu.VMEM((len(lefts), rows, FOUR * tok), BF16),
             pltpu.VMEM((FOUR * tok, width), BF16),
-            pltpu.SemaphoreType.DMA((len(lefts) + 1, FOUR)),
+            pltpu.VMEM((rows, wide) if nz else (16, LANE), BF16),
+            pltpu.SemaphoreType.DMA((len(lefts) + moves, FOUR)),
         ],
         after,
-        16,
+        20,
     )
 
 
@@ -493,7 +523,7 @@
 def split_kernel(sc, *refs):
     ins, (mine, other, total) = refs[:-3], refs[-3:]
     rows = mine.shape[0]
-    value = ins[0][...].astype(F32)
+    value = (ins[0][sc[1]] if len(ins[0].shape) == 3 else ins[0][...]).astype(F32)
     for ref in ins[1:]:
         value = value + ref[...].astype(F32)
     total[...] = value
@@ -503,11 +533,11 @@
 
 
 def split_rows(sc, terms, after=()):
-    rows, width = terms[0].shape
+    rows, width = terms[0].shape[-2:]
     mine, other = call(
         split_kernel, "split_rows", (sc, *terms), [SM] + [VM] * len(terms),
         (shape((rows // 2, width), BF16),) * 2,
-        [pltpu.VMEM((rows, width), F32)], after=after,
+        [pltpu.VMEM((rows, width), F32)], after=after, room=16,
     )
     return plane_swap([mine, mine, other, other])
 
@@ -523,35 +553,31 @@
     return moved
 
 
-def put_tiles(place, part, ref):
-    start = start_tile(place)
-    twice = (place > 0) & (start < start_tile(place - 1) + TILES)
-    for i in range(TILES):
-
-        @pl.when(jnp.logical_not(twice) if i == 0 else start >= 0)
-        def _():
-            cols = pl.ds(pl.multiple_of((start + i) * LANE, LANE), LANE)
-            ref[:, cols] = part[:, i * LANE : (i + 1) * LANE]
-
-
-def place_kernel(plan, sc, *refs):
-    parts = refs[:FOUR]
-    outs = refs[FOUR:]
+def place_kernel(plan, count, sc, *refs):
+    results = refs[count : count + max(entry[3] for entry in plan) + 1]
+    small = refs[count + len(results) :]
     for k in range(FOUR):
         place = sc[4] ^ k
-        part = parts[k][...].astype(F32)
-        for (begin, stop, tiled), ref in zip(plan, outs):
+        start = start_tile(place)
+        twice = (place > 0) & (start < start_tile(place - 1) + TILES)
+        for chunk, begin, stop, to, first in plan:
+            part = refs[chunk * FOUR + k][:, begin:stop].astype(F32)
             size = stop - begin
-            if tiled:
-                put_tiles(place, part[:, begin:stop], ref)
-            else:
-                ref[:, pl.ds(pl.multiple_of(place * size, size), size)] = part[:, begin:stop]
-    if len(outs) > len(plan):
-        expand, gains = outs[len(plan) :]
-        begin = plan[-1][1]
-        total = [None] * FOUR
-        for k in range(FOUR):
-            total[k] = parts[k][:, begin:].astype(F32)
+            if first is None:
+                cols = pl.ds(pl.multiple_of(place * size, size), size)
+                results[to][:, cols] = part
+                continue
+            for i in range(size // LANE):
+
+                @pl.when(jnp.logical_not(twice) if first + i == 0 else start >= 0)
+                def _():
+                    cols = pl.ds(pl.multiple_of((start + first + i) * LANE, LANE), LANE)
+                    results[to][:, cols] = part[:, i * LANE : (i + 1) * LANE]
+
+    if small:
+        expand, gains = small
+        begin = plan[-1][2]
+        total = [refs[k][:, begin:].astype(F32) for k in range(FOUR)]
         even = [jnp.where(sc[4] % 2 == 0, total[i], total[i + 1]) for i in (0, 2)]
         odd = [jnp.where(sc[4] % 2 == 0, total[i + 1], total[i]) for i in (0, 2)]
         value = (even[0] + odd[0]) + (even[1] + odd[1])
@@ -567,66 +593,55 @@
     if small:
         outs += (shape((rows // FOUR, small), F32), shape((8, rows), F32))
     return call(
-        functools.partial(place_kernel, plan), "put", (sc, *parts), [SM] + [VM] * FOUR,
-        outs, after=after,
-    )
-
-
-def enter_kernel(hidden, gain, wl, we, normed, latent, kv):
+        functools.partial(place_kernel, plan, len(parts)), "put", (sc, *parts),
+        [SM] + [VM] * len(parts), outs, after=after,
+    )
+
+
+def enter_kernel(nz, hidden, gain, wl, we, dy, wq, latent, kv, left_dy, left_one, qp, wq_s, sem):
+    load = pltpu.make_async_copy(wq, wq_s, sem)
+    load.start()
     value, unused = norm_forward(hidden[...].astype(F32), gain_row(gain))
     low = value.astype(BF16)
-    normed[...] = low
     rows = nn(low, wl[...]).astype(BF16)
     latent[...] = rows
     for g in range(GROUPS):
         span = slice(g * LANE, (g + 1) * LANE)
         kv[:, span] = nn(rows[:, g * LAT : (g + 1) * LAT], we[:, span]).astype(BF16)
-
-
-def enter(hidden, gain, wl, we):
-    tok, width = hidden.shape
-    return call(
-        enter_kernel,
-        "enter",
-        (hidden, gain, wl, we),
-        [VM] * 4,
-        (
-            shape((tok, width), BF16),
-            shape((tok, wl.shape[1]), BF16),
-            shape((tok, we.shape[1]), BF16),
-        ),
-        room=60,
-    )
-
-
-def query_kernel(nz, normed, dy, wq, qp, left):
-    low = normed[...]
-    left[0] = by_core(dy[...].astype(F32).T, nz).astype(BF16)
-    left[1] = by_core(low.astype(F32).T, nz).astype(BF16)
-    turned = (nn(low, wq[...]).astype(BF16) * scale).T
+    left_dy[...] = by_core(dy[...].astype(F32).T, nz).astype(BF16)
+    left_one[...] = by_core(value.T, nz).astype(BF16)
+    load.wait()
+    turned = (nn(low, wq_s[...]).astype(BF16) * scale).T
     qp[:, HD:, :] = jnp.zeros((GROUPS, HD, qp.shape[2]), BF16)
     for g in range(GROUPS):
         for h in range(PER):
-            row = (g * PER + h) * HD
-            qp[g, 0:HD, h * LANE : (h + 1) * LANE] = turned[row : row + HD, :]
-
-
-def query(normed, dy, wq, nz, after=()):
-    tok, width = normed.shape
-    return call(
-        functools.partial(query_kernel, nz),
-        "query",
-        (normed, dy, wq),
-        [VM] * 3,
+            at = (g * PER + h) * HD
+            qp[g, 0:HD, h * LANE : (h + 1) * LANE] = turned[at : at + HD, :]
+
+
+def enter(hidden, gain, wl, we, dy, wq, nz):
+    tok, width = hidden.shape
+    left = shape((width, tok), BF16)
+    return call(
+        functools.partial(enter_kernel, nz),
+        "enter",
+        (hidden, gain, wl, we, dy, wq),
+        [VM] * 5 + [HB],
         (
+            shape((tok, wl.shape[1]), BF16),
+            shape((tok, we.shape[1]), BF16),
+            left,
+            left,
             shape((GROUPS, 2 * HD, PER * tok), BF16),
-            shape((2, width, tok), BF16),
         ),
-        after=after,
-    )
-
-
-def leave_kernel(nz, count, sc, hidden, dmid, gain, dq, base, latent, gain_two, we, wl, *refs):
+        [pltpu.VMEM(wq.shape, BF16), pltpu.SemaphoreType.DMA],
+        room=60,
+    )
+
+
+def leave_kernel(
+    nz, count, sc, hidden, dmid, gain, dq, base, latent, gain_two, we, wl, left_o, left_one, *refs
+):
     moved = refs[:count]
     input_grad, small = refs[count : count + 2]
     sends = refs[count + 2 : count + 2 + FOUR]
@@ -666,19 +681,24 @@
         sends[k][:, :part] = dmid[:, cols].astype(BF16)
         sends[k][:, part : 2 * part] = dq[:, cols]
         cols = pl.ds(pl.multiple_of(place * half, half), half)
-        sends[k][:, 2 * part :] = lat[:, cols].astype(BF16)
-
-
-def leave(sc, hidden, dmid, gain, dq, base, latent, gain_two, we, wl, moved, nz, after=()):
+        end = 2 * part + half
+        sends[k][:, 2 * part : end] = lat[:, cols].astype(BF16)
+        for left in (left_o, left_one):
+            for at in range(0, left.shape[0], LANE):
+                sends[k][:, end : end + LANE] = left[at : at + LANE, :]
+                end += LANE
+
+
+def leave(sc, hidden, dmid, gain, dq, base, latent, gain_two, we, wl, lefts, moved, nz, after=()):
     tok, width = hidden.shape
     lat = latent.shape[1]
     return call(
         functools.partial(leave_kernel, nz, len(moved)),
         "leave",
-        (sc, hidden, dmid, gain, dq, base, latent, gain_two, we, wl, *moved),
-        [SM] + [VM] * (9 + len(moved)),
+        (sc, hidden, dmid, gain, dq, base, latent, gain_two, we, wl, *lefts, *moved),
+        [SM] + [VM] * (11 + len(moved)),
         (shape((tok, width), BF16), shape((width, LANE), BF16))
-        + (shape((tok, (2 * width + lat) // FOUR), BF16),) * FOUR,
+        + (shape((tok, (2 * width + lat) // FOUR + 2 * width), BF16),) * FOUR,
         [pltpu.VMEM((tok, lat), F32), pltpu.VMEM((width, LANE), F32)],
         after,
         60,
@@ -701,11 +721,11 @@
     hidden = inputs[0]
     dy = cotangent[0]
 
-    def across(value, step):
-        return lax.ppermute(value, "z", [(i, i ^ (1 << step)) for i in range(nz)])
-
-    normed, latent, kv = enter(hidden, norm_attn, proj_latent, proj_expand)
-    relative = nz <= 4
+    latent, kv, left_dy, left_one, qp = enter(
+        hidden, norm_attn, proj_latent, proj_expand, dy, proj_query, nz
+    )
+    dys = lax.all_gather(left_dy, PLANE, axis=0)
+    relative = nz == 4
     if relative:
         moved = [kv]
         for k in range(1, nz):
@@ -713,8 +733,6 @@
         k00 = stack(moved, after=(sc,))
     else:
         k00 = lax.all_gather(kv, "z", axis=0)
-    qp, left = query(normed, dy, proj_query, nz, after=(k00,))
-    early = lax.all_gather(left, PLANE, axis=0)
     k01 = swap(k00, "x")
     k10 = swap(k00, "core")
     k11 = swap(k01, "core")
@@ -722,106 +740,87 @@
     kvs, ot, logs, left_o, left_n2, mid, normed_two = attend(
         sc, (k00, k01, k10, k11), qp, hidden, proj_output, norm_ffn, nz, relative
     )
-    n2s = plane_swap([left_n2] * FOUR)
-    os = lax.all_gather(left_o, PLANE, axis=0)
-    fed = feed(sc, normed_two, dy, mid, norm_ffn, proj_output, ffn_gate, ffn_up, ffn_down)
+    n2s = lax.all_gather(left_n2, PLANE, axis=0)
+    fed = feed(
+        sc, normed_two, dy, mid, norm_ffn, proj_output, ffn_gate, ffn_up, ffn_down,
+        after=(dys,),
+    )
     output, dmid, dop, gain_two = fed[FOUR:]
     parts_a = plane_swap(fed[:FOUR])
 
-    def blocks(value):
-        return value.reshape((nz, -1) + value.shape[1:])
-
-    chunks = {}
     last = []
 
-    def begin(name, keep, send):
-        chunks[name] = (blocks(keep), blocks(swap(send, "core")), 0)
-
-    def advance(name):
-        keep, came, step = chunks[name]
-        while True:
-            keep, send = halve(sc, keep, came, step, after=last[-1:])
-            last.append(keep)
-            came = across(send, step)
-            step += 1
-            if step == 1 or (1 << step) >= nz:
-                break
-        chunks[name] = (keep, came, step)
-
-    def finish(name):
-        keep, came, unused = chunks[name]
-        chunks[name] = split_rows(sc, (keep[0], came[0]), after=last[-1:])
-        last.append(chunks[name][0])
-
-    def place_out(name, plan, widths, small=0):
-        outs = put(sc, chunks[name], plan, widths, small, after=last[-1:])
-        last.append(outs[0])
-        return outs
-
     dq, keep_own, keep_far, send_own, send_far = attend_back(
-        sc, kvs, qp, dop, ot, logs, nz, tok, after=n2s[1:]
-    )
-    rest, side = kv_add(
-        (keep_own, keep_far, swap(send_own, "core"), swap(send_far, "core")), after=(early,)
-    )
-    side = swap(side, "x")
+        sc, kvs, qp, dop, ot, logs, nz, tok
+    )
+    pieces = (keep_own, keep_far, swap(send_own, "core"), swap(send_far, "core"))
     if relative:
-        moved = list(kv_split(sc, rest, side, after=parts_a[1:]))
-        last.append(moved[0])
+        moved = list(kv_cut(sc, pieces, nz - 1, after=(n2s, *parts_a[1:3])))
         for k in range(1, nz):
             moved[k] = lax.ppermute(moved[k], "z", [(i, i - k) for i in range(k, nz)])
+        last.append(moved[0])
     else:
-        term = rest + side.astype(F32)
-        moved = [lax.psum_scatter(term, "z", scatter_dimension=0, tiled=False)]
-    terms = weight_terms(
+        both = [pieces[i].astype(F32) + pieces[i + 2].astype(F32) for i in range(2)]
+        both = jnp.stack(both, axis=1)
+        moved = [lax.psum_scatter(both, "z", scatter_dimension=0, tiled=False)]
+    base = base_terms(dq, proj_query, after=last[-1:])
+    rest, side = kv_sum(moved, after=(base,))
+    last.append(rest)
+    moved = [rest, swap(side, "x")]
+    (main,) = weight_terms(
         sc,
-        ((None, tuple(n2s)), (0, (early,))),
+        ((width, (n2s,)), (width, (dys,))),
         parts_a,
-        (((0, 0, WIDE),), ((0, WIDE, 2 * WIDE),), ((1, 2 * WIDE, 3 * WIDE),)),
+        ((0, 0, 2 * WIDE), (1, 2 * WIDE, 3 * WIDE)),
         after=last[-1:],
     )
-    last.append(terms[0])
-    for i, name in enumerate(("gate", "up", "down")):
-        begin(name, *terms[2 * i : 2 * i + 2])
-    for name in ("gate", "up", "down"):
-        advance(name)
-    base = nt(dq, proj_query)
+    last.append(main)
+    main = lax.psum_scatter(main, ("z", "core"), scatter_dimension=0, tiled=True)
     left_out = leave(
         sc, hidden, dmid, norm_attn, dq, base, latent, gain_two, proj_expand, proj_latent,
-        moved, nz, after=(last[-1], os),
+        (left_o, left_one), moved, nz, after=last[-1:],
     )
     input_grad, small = left_out[:2]
     last.append(input_grad)
     parts_c = plane_swap(left_out[2:])
-    advance("gate")
-    advance("up")
-    finish("gate")
     part, lat_part = width // FOUR, latent.shape[1] // FOUR
     end = 2 * part + lat_part
-    terms = weight_terms(
+    keep, send = weight_terms(
         sc,
-        ((None, (os,)), (1, (early,))),
+        ((width, ()), (width, ())),
         parts_c,
-        (((0, 0, part), (1, part, end)),),
+        ((0, 0, part), (1, part, end)),
         (small,),
+        nz,
         after=last[-1:],
     )
-    last.append(terms[0])
-    begin("rest", *terms)
-    advance("down")
-    advance("rest")
-    finish("up")
-    advance("rest")
-    finish("down")
-    (grad_gate,) = place_out("gate", ((0, WIDE, True),), (hidden_size,))
-    (grad_up,) = place_out("up", ((0, WIDE, True),), (hidden_size,))
-    finish("rest")
-    (grad_down_t,) = place_out("down", ((0, WIDE, True),), (hidden_size,))
-    grad_output, grad_query, grad_latent, expand_t, gains = place_out(
-        "rest",
-        ((0, part, False), (part, 2 * part, False), (2 * part, end, False)),
+    last.append(keep)
+    came = swap(send, "core")
+    step = 0
+    while (1 << step) < nz:
+        keep, send = halve(sc, keep, came, step, after=last[-1:])
+        last.append(keep)
+        came = lax.ppermute(send, "z", [(i, i ^ (1 << step)) for i in range(nz)])
+        step += 1
+        if step == 1:
+            main = split_rows(sc, (main,), after=last[-1:])
+            last.append(main[0])
+    rest = split_rows(sc, (keep[0], came[0]), after=last[-1:])
+    last.append(rest[0])
+    grad_gate, grad_up, grad_down_t = put(
+        sc,
+        main,
+        tuple((0, i * WIDE, (i + 1) * WIDE, i, 0) for i in range(3)),
+        (hidden_size,) * 3,
+        after=last[-1:],
+    )
+    grad_output, grad_query, grad_latent, expand_t, gains = put(
+        sc,
+        rest,
+        ((0, 0, part, 0, None), (0, part, 2 * part, 1, None), (0, 2 * part, end, 2, None)),
         (width, width, latent.shape[1]),
         LAT,
+        after=(grad_gate,),
     )
     grad_expand = expand_t.T
     grad_norm_attn, grad_norm_ffn = gains[0], gains[1]

time: 224 us -> 203 us (0.906)
  starting transfers between devices: 52.4 us -> 35.2 us
  Pallas kernels: 60.2 us -> 49.6 us
  waiting for transfers between devices: 80.8 us -> 87.4 us
    ppermute x8 -> x2, waiting for transfers between devices: 29.9 us -> 6.26 us  [shards(): came = lax.ppermute(send, 'z', [(i, i ^ 1 << step) for i in range(nz)])]
    all_gather x2, waiting for transfers between devices: 0.64 us -> 14.9 us  [the longest x1 13.7 us: shards(): n2s = lax.all_gather(left_n2, PLANE, axis=0)]
    pallas_call x27 -> x17, Pallas kernels: 60.2 us -> 49.6 us  [call(): pl.pallas_call(body, out_shape=tuple(outs), in_specs=list(specs) + [ANY]...]
    ppermute x21 -> x12, starting transfers between devices: 25.5 us -> 15.5 us  [plane_swap(): lax.ppermute(parts[k], PLANE, [(d, d ^ k) for d in range(FOUR)])]
    reduce_scatter x0 -> x1, waiting for transfers between devices: none -> 9.26 us  [shards(): lax.psum_scatter(main, ('z', 'core'), scatter_dimension=0, tiled=True)]
    ppermute x21 -> x12, waiting for transfers between devices: 19.7 us -> 27 us  [plane_swap(): lax.ppermute(parts[k], PLANE, [(d, d ^ k) for d in range(FOUR)])]
    ppermute x8 -> x2, starting transfers between devices: 6.11 us -> 1.05 us  [shards(): came = lax.ppermute(send, 'z', [(i, i ^ 1 << step) for i in range(nz)])]
    ppermute x10 -> x7, waiting for transfers between devices: 18.5 us -> 13.8 us  [swap(): return lax.ppermute(value, axis, [(0, 1), (1, 0)])]
  transfers between devices with their start and end apart: 47 -> 30, of which waited for: 22 -> 18; matrix products, arithmetic and copies ran while one was open for 1% -> 0% of each run, Pallas kernels for 23% -> 19%
where the time goes in v3:
time: 203 us; the launch traced here: 202 us
  waiting for transfers between devices  87.4 us (43%)
  Pallas kernels  49.6 us (24%)
  starting transfers between devices  35.2 us (17%)
  local copies, waits for them, and re-layouts  16.1 us (8%)
  between operations  14.1 us (7%)
    pallas_call x17, Pallas kernels, call(): pl.pallas_call(body, out_shape=tuple(outs), in_specs=list(specs) + [ANY]...  49.6 us
    ppermute x12, waiting for transfers between devices, plane_swap(): lax.ppermute(parts[k], PLANE, [(d, d ^ k) for d in range(FOUR)])  27 us
    ppermute x12, starting transfers between devices, plane_swap(): lax.ppermute(parts[k], PLANE, [(d, d ^ k) for d in range(FOUR)])  15.5 us
    unnamed x50, local copies, waits for them, and re-layouts  14.8 us
    ppermute x3, waiting for transfers between devices, shards(): moved[k] = lax.ppermute(moved[k], 'z', [(i, i - k) for i in range(k, nz)])  14.7 us
    ppermute x7, waiting for transfers between devices, swap(): return lax.ppermute(value, axis, [(0, 1), (1, 0)])  13.8 us
    all_gather x1, waiting for transfers between devices, shards(): n2s = lax.all_gather(left_n2, PLANE, axis=0)  13.7 us
    ppermute x3, starting transfers between devices, shards(): moved.append(lax.ppermute(kv, 'z', [(i, i + k) for i in range(nz - k)]))  10.7 us
  transfers between devices with their start and end apart: 30, of which 18 were waited for; matrix products, arithmetic and copies ran while one was open for 0% of the time, Pallas kernels for 19%

profile of v3, /device:TPU:0, one launch (start us, length us, event | category | flops | bytes accessed | tf_op | source)
XLA Modules:
  0.0 202.4 jit_solution(13633674416349836229)
XLA Ops:
  7.2 4.4 %enter.1 = (bf16[128,512]{1,0:T(8,128)(2,1)}, bf16[128,256]{1,0:T(8,128)(2,1)}, bf16[1024,128]{1,0:T(8,128)(2,1)}, bf16[1024,128]{1,0:T(8,128)(2,1)}, bf16[2,128,1024]{2,1,0:T(8,128)(2,1)}) custom-call(bf16[128,1024]{1,0:T(8,128)(2,1)} %bitcast.27, bf16[1024]{0:T(1024)(128)(2,1)} %refs_3_.3, bf16[1024,512]{1,0:T(8,128)(2,1)} %refs_9_.1, ...), custom_call_target="tpu_custom_call" | custom-call | bytes 36000 | tf_op jit(solution)/shard_map/enter/pallas_call | solution.py:65
  11.7 7.0 %collective-permute-start.2 = (bf16[128,256]{1,0:T(8,128)(2,1)}, bf16[128,256]{1,0:T(8,128)(2,1)S(1)}, u32[]{:S(2)}, u32[]{:S(2)}) collective-permute-start(bf16[128,256]{1,0:T(8,128)(2,1)} %get-tuple-element.66.refs_0_), channel_id=1, source_target_pairs={{0,24},{1,25},{2,26},{3,27},{4,28},{5,29},{6,30},{7,31}} | collective-permute-start | bytes 196616 | tf_op jit(solution)/shard_map/ppermute | solution.py:732
  19.9 2.5 %collective-permute-start = (bf16[128,256]{1,0:T(8,128)(2,1)}, bf16[128,256]{1,0:T(8,128)(2,1)S(1)}, u32[]{:S(2)}, u32[]{:S(2)}) collective-permute-start(bf16[128,256]{1,0:T(8,128)(2,1)} %get-tuple-element.66.refs_0_), channel_id=1, source_target_pairs={{0,8},{8,16},{16,24},{1,9},{9,17},{17,25},{2,10},{10,18},{18,26},{... | collective-permute-start | bytes 196616 | tf_op jit(solution)/shard_map/ppermute | solution.py:732
  23.2 1.4 collective-permute-done.refs_1_
  25.5 1.6 collective-permute-start.3
  27.1 5.9 %collective-permute-done.3.refs_2_ = bf16[4,128,256]{2,1,0:T(8,128)(2,1)S(1)} collective-permute-done((bf16[4,128,256]{2,1,0:T(8,128)(2,1)S(1)}, bf16[4,128,256]{2,1,0:T(8,128)(2,1)S(1)}, u32[]{:S(2)}, u32[]{:S(2)}) %collective-permute-start.3) | collective-permute-done | bytes 262176 | tf_op jit(solution)/shard_map/ppermute | solution.py:546
  33.0 1.5 collective-permute-done.5.refs_4_
  35.2 4.6 %attend.1 = (bf16[2048,256]{1,0:T(8,128)(2,1)}, f32[2,64,1024]{2,1,0:T(8,128)}, f32[2,1,1024]{2,1,0:T(1,128)}, bf16[1024,128]{1,0:T(8,128)(2,1)}, bf16[1024,128]...) custom-call(s32[16]{0:T(128)} %copy-done.17, bf16[4,128,256]{2,1,0:T(8,128)(2,1)} %copy-done.7, ...), custom_call_target="tpu_custom_call" | custom-call | bytes 36000 | tf_op jit(solution)/shard_map/attend/pallas_call | solution.py:65
  41.2 15.5 %feed.1 = (bf16[128,2304]{1,0:T(8,128)(2,1)}, bf16[128,2304]{1,0:T(8,128)(2,1)}, bf16[128,2304]{1,0:T(8,128)(2,1)}, bf16[128,2304]{1,0:T(8,128)(2,1)}, bf16[128,...) custom-call(s32[16]{0:T(128)} %copy-done.17, ...), custom_call_target="tpu_custom_call" | custom-call | bytes 36000 | tf_op jit(solution)/shard_map/feed/pallas_call | solution.py:65
  56.7 1.5 collective-permute-start.8
  60.3 4.6 %attend_back.1 = (bf16[128,1024]{1,0:T(8,128)(2,1)}, bf16[4,128,256]{2,1,0:T(8,128)(2,1)}, bf16[4,128,256]{2,1,0:T(8,128)(2,1)}, bf16[4,128,256]{2,1,0:T(8,128)(2,1)}, bf16[4,128,256]{2,1,0:T(8,128)(2,1)}) custom-call(s32[16]{0:T(128)} %copy-done.17, bf16[2048,256]{1,0:T(8,128)(2,1)} %get-tuple-element.73.refs_1_, ...), custom_call_target="tpu_custom_call" | custom-call | bytes 32400000 | tf_op jit(solution)/shard_map/attend_back/pallas_call | solution.py:65
  67.0 13.7 %all-gather.7.cloned.1.call-done = bf16[4096,128]{1,0:T(8,128)(2,1)} async-done(((bf16[1024,128]{1,0:T(8,128)(2,1)}), bf16[4096,128]{1,0:T(8,128)(2,1)}) %all-gather.7.cloned.1.call-update) | async-done | bytes 1048592 | tf_op jit(solution)/shard_map/all_gather | solution.py:743
  90.3 2.5 %collective-permute-done.10.refs_1_ = bf16[2,128,256]{2,1,0:T(8,128)(2,1)S(1)} collective-permute-done((bf16[2,128,256]{2,1,0:T(8,128)(2,1)S(1)}, bf16[2,128,256]{2,1,0:T(8,128)(2,1)S(1)}, u32[]{:S(2)}, u32[]{:S(2)}) %collective-permute-start.10) | collective-permute-done | bytes 131104 | tf_op jit(solution)/shard_map/ppermute | solution.py:760
  92.8 12.2 %collective-permute-done.11.refs_2_ = bf16[2,128,256]{2,1,0:T(8,128)(2,1)S(1)} collective-permute-done((bf16[2,128,256]{2,1,0:T(8,128)(2,1)S(1)}, bf16[2,128,256]{2,1,0:T(8,128)(2,1)S(1)}, u32[]{:S(2)}, u32[]{:S(2)}) %collective-permute-start.11) | collective-permute-done | bytes 131104 | tf_op jit(solution)/shard_map/ppermute | solution.py:760
  106.4 5.0 %weight_terms.2.refs_14_ = bf16[1024,2304]{1,0:T(8,128)(2,1)S(1)} custom-call(s32[16]{0:T(128)S(1)} %copy-done.18, bf16[4,1024,128]{2,1,0:T(8,128)(2,1)S(1)} %bitcast.23, bf16[4,1024,128]{2,1,0:T(8,128)(2,1)S(1)} %bitcast.21, bf16[128,2304]{1,0:T(8,128)(2,1)S(1)} %copy-done.10, bf16[128,2304]{1,0:T(8,128)(2,1)S(1)} %collective-permute-done.8.refs_6_.refs_4_, ...), custom_call_target="tpu_custom_call" | custom-call | bytes 36000 | tf_op jit(solution)/shard_map/weight_terms/pallas_call | solution.py:65
  111.3 2.1 %copy-done = bf16[1024,2304]{1,0:T(8,128)(2,1)} copy-done((bf16[1024,2304]{1,0:T(8,128)(2,1)}, bf16[1024,2304]{1,0:T(8,128)(2,1)S(1)}, u32[]{:S(2)}) %copy-start) | copy-done | bytes 4718616
  113.5 1.8 collective-permute-start.13
  115.3 2.5 %collective-permute-done.13.refs_13_ = bf16[128,256]{1,0:T(8,128)(2,1)S(1)} collective-permute-done((bf16[128,256]{1,0:T(8,128)(2,1)S(1)}, bf16[128,256]{1,0:T(8,128)(2,1)S(1)}, u32[]{:S(2)}, u32[]{:S(2)}) %collective-permute-start.13) | collective-permute-done | bytes 65568 | tf_op jit(solution)/shard_map/ppermute | solution.py:546
  118.5 4.5 %leave.1 = (bf16[128,1024]{1,0:T(8,128)(2,1)}, bf16[1024,128]{1,0:T(8,128)(2,1)}, bf16[128,2688]{1,0:T(8,128)(2,1)}, bf16[128,2688]{1,0:T(8,128)(2,1)}, bf16[128...) custom-call(s32[16]{0:T(128)} %copy-done.17, bf16[128,1024]{1,0:T(8,128)(2,1)} %bitcast.29, ...), custom_call_target="tpu_custom_call" | custom-call | bytes 36000 | tf_op jit(solution)/shard_map/leave/pallas_call | solution.py:65
  123.5 1.6 collective-permute-start.16
  126.5 14.2 %collective-permute-done.15.refs_2_ = bf16[128,2688]{1,0:T(8,128)(2,1)S(1)} collective-permute-done((bf16[128,2688]{1,0:T(8,128)(2,1)}, bf16[128,2688]{1,0:T(8,128)(2,1)S(1)}, u32[]{:S(2)}, u32[]{:S(2)}) %collective-permute-start.15) | collective-permute-done | bytes 688160 | tf_op jit(solution)/shard_map/ppermute | solution.py:552
  142.1 9.0 %collective-permute-done.17.refs_4_ = bf16[128,2688]{1,0:T(8,128)(2,1)S(1)} collective-permute-done((bf16[128,2688]{1,0:T(8,128)(2,1)}, bf16[128,2688]{1,0:T(8,128)(2,1)S(1)}, u32[]{:S(2)}, u32[]{:S(2)}) %collective-permute-start.17) | collective-permute-done | bytes 688160 | tf_op jit(solution)/shard_map/ppermute | solution.py:552
  154.2 2.9 %weight_terms.3 = (bf16[4,128,768]{2,1,0:T(8,128)(2,1)S(1)}, bf16[4,128,768]{2,1,0:T(8,128)(2,1)S(1)}) custom-call(s32[16]{0:T(128)S(1)} %copy-done.19, bf16[128,2688]{1,0:T(8,128)(2,1)S(1)} %copy-done.9, bf16[128,2688]{1,0:T(8,128)(2,1)S(1)} %collective-permute-done.15.refs_2_, bf16[128,2688]{1,0:T(8,128)(2,1)S(1)} %collective-permute-done.16.refs_3_, ...), custom_call_target="tpu_custom_call" | custom-call | bytes 36000 | tf_op jit(solution)/shard_map/weight_terms/pallas_call | solution.py:65
  157.2 2.3 %collective-permute-done.18.refs_2_ = bf16[4,128,768]{2,1,0:T(8,128)(2,1)S(1)} collective-permute-done((bf16[4,128,768]{2,1,0:T(8,128)(2,1)S(1)}, bf16[4,128,768]{2,1,0:T(8,128)(2,1)S(1)}, u32[]{:S(2)}, u32[]{:S(2)}) %collective-permute-start.18) | collective-permute-done | bytes 786464 | tf_op jit(solution)/shard_map/ppermute | solution.py:546
  160.3 9.3 %reduce-scatter.2.cloned.1.call-done.refs_1_ = bf16[128,2304]{1,0:T(8,128)(2,1)} async-done(((bf16[1024,2304]{1,0:T(8,128)(2,1)}), bf16[128,2304]{1,0:T(8,128)(2,1)}) %reduce-scatter.2.cloned.1.call-update) | async-done | bytes 589840 | tf_op jit(solution)/shard_map/reduce_scatter | solution.py:778
  171.3 2.0 collective-permute-start.26
  174.9 1.5 collective-permute-start.25
  176.4 1.5 collective-permute-start.24
  177.9 6.3 %collective-permute-done.20 = bf16[1,128,768]{2,1,0:T(8,128)(2,1)S(1)} collective-permute-done((bf16[1,128,768]{2,1,0:T(8,128)(2,1)S(1)}, bf16[1,128,768]{2,1,0:T(8,128)(2,1)S(1)}, u32[]{:S(2)}, u32[]{:S(2)}) %collective-permute-start.20) | collective-permute-done | bytes 196640 | tf_op jit(solution)/shard_map/ppermute | solution.py:803
  184.8 2.7 %collective-permute-start.23 = (bf16[64,768]{1,0:T(8,128)(2,1)S(1)}, bf16[64,768]{1,0:T(8,128)(2,1)S(1)}, u32[]{:S(2)}, u32[]{:S(2)}) collective-permute-start(bf16[64,768]{1,0:T(8,128)(2,1)S(1)} %get-tuple-element.111), channel_id=1, source_target_pairs={{0,5},{1,4},{4,1},{5,0},{2,7},{3,6},{6,3},{7,2},{8,13},{9,12},{12,... | collective-permute-start | bytes 294920 | tf_op jit(solution)/shard_map/ppermute | solution.py:552
  188.3 2.2 %put.2 = (f32[64,2816]{1,0:T(8,128)}, f32[64,2816]{1,0:T(8,128)}, f32[64,2816]{1,0:T(8,128)}) custom-call(s32[16]{0:T(128)S(1)} %copy-done.19, bf16[64,2304]{1,0:T(8,128)(2,1)S(1)} %get-tuple-element.107.refs_3_.refs_1_, bf16[64,2304]{1,0:T(8,128)(2,1)S(1)} %collective-permute-done.24.refs_2_, bf16[64,2304]{1,0:T(8,128)(2,1)S(1)} %collective-permute-done.25.refs_3_, ...), custom_call_target="tpu_custom_call" | custom-call | bytes 36000 | tf_op jit(solution)/shard_map/put/pallas_call | solution.py:65
  191.2 1.6 collective-permute-done.22.refs_3_
  (100 shorter events, 36.5 us)
Async XLA Ops:
  7.2 34.0 %all-gather.5.cloned.1.call-start = ((), (), s32[]{:S(2)}) async-start(), calls=%async_computation.2 | async-start | bytes 1310720 | tf_op jit(solution)/shard_map/all_gather | solution.py:727
  11.6 69.1 %all-gather.7.cloned.1.call-start = ((), (), s32[]{:S(2)}) async-start(), calls=%async_computation.3 | async-start | bytes 1310720 | tf_op jit(solution)/shard_map/all_gather | solution.py:743
  11.7 11.5 %collective-permute-start.2 = (bf16[128,256]{1,0:T(8,128)(2,1)}, bf16[128,256]{1,0:T(8,128)(2,1)S(1)}, u32[]{:S(2)}, u32[]{:S(2)}) collective-permute-start(bf16[128,256]{1,0:T(8,128)(2,1)} %get-tuple-element.66.refs_0_), channel_id=1, source_target_pairs={{0,24},{1,25},{2,26},{3,27},{4,28},{5,29},{6,30},{7,31}} | collective-permute-start | bytes 196616 | tf_op jit(solution)/shard_map/ppermute | solution.py:732
  18.6 4.5 %collective-permute-start.1 = (bf16[128,256]{1,0:T(8,128)(2,1)}, bf16[128,256]{1,0:T(8,128)(2,1)S(1)}, u32[]{:S(2)}, u32[]{:S(2)}) collective-permute-start(bf16[128,256]{1,0:T(8,128)(2,1)} %get-tuple-element.66.refs_0_), channel_id=1, source_target_pairs={{0,16},{8,24},{1,17},{9,25},{2,18},{10,26},{3,19},{11,27},{4,20},{... | collective-permute-start | bytes 196616 | tf_op jit(solution)/shard_map/ppermute | solution.py:732
  19.9 4.7 %collective-permute-start = (bf16[128,256]{1,0:T(8,128)(2,1)}, bf16[128,256]{1,0:T(8,128)(2,1)S(1)}, u32[]{:S(2)}, u32[]{:S(2)}) collective-permute-start(bf16[128,256]{1,0:T(8,128)(2,1)} %get-tuple-element.66.refs_0_), channel_id=1, source_target_pairs={{0,8},{8,16},{16,24},{1,9},{9,17},{17,25},{2,10},{10,18},{18,26},{... | collective-permute-start | bytes 196616 | tf_op jit(solution)/shard_map/ppermute | solution.py:732
  25.5 7.5 %collective-permute-start.3 = (bf16[4,128,256]{2,1,0:T(8,128)(2,1)S(1)}, bf16[4,128,256]{2,1,0:T(8,128)(2,1)S(1)}, u32[]{:S(2)}, u32[]{:S(2)}) collective-permute-start(bf16[4,128,256]{2,1,0:T(8,128)(2,1)S(1)} %stack.24.refs_1_), channel_id=1, source_target_pairs={{0,4},{4,0},{1,5},{5,1},{2,6},{6,2},{3,7},{7,3},{8,12},{12,8},{9,1... | collective-permute-start | bytes 786440 | tf_op jit(solution)/shard_map/ppermute | solution.py:546
  27.1 5.9 %collective-permute-start.4 = (bf16[4,128,256]{2,1,0:T(8,128)(2,1)S(1)}, bf16[4,128,256]{2,1,0:T(8,128)(2,1)S(1)}, u32[]{:S(2)}, u32[]{:S(2)}) collective-permute-start(bf16[4,128,256]{2,1,0:T(8,128)(2,1)S(1)} %stack.24.refs_1_), channel_id=1, source_target_pairs={{0,2},{2,0},{1,3},{3,1},{4,6},{6,4},{5,7},{7,5},{8,10},{10,8},{9,1... | collective-permute-start | bytes 786440 | tf_op jit(solution)/shard_map/ppermute | solution.py:546
  33.0 1.5 collective-permute-start.5
  39.9 129.7 %reduce-scatter.2.cloned.1.call-start = ((), (), s32[]{:S(2)}) async-start(), calls=%async_computation.1 | async-start | bytes 5308416 | tf_op jit(solution)/shard_map/reduce_scatter | solution.py:778
  41.2 39.5 %copy-start.18 = (s32[16]{0:T(128)S(1)}, s32[16]{0:T(128)}, u32[]{:S(2)}) copy-start(s32[16]{0:T(128)} %copy-done.17) | copy-start | bytes 196
  56.7 24.0 %collective-permute-start.8 = (bf16[128,2304]{1,0:T(8,128)(2,1)}, bf16[128,2304]{1,0:T(8,128)(2,1)S(1)}, u32[]{:S(2)}, u32[]{:S(2)}) collective-permute-start(bf16[128,2304]{1,0:T(8,128)(2,1)} %get-tuple-element.83), channel_id=1, source_target_pairs={{0,1},{1,0},{4,5},{5,4},{2,3},{3,2},{6,7},{7,6},{8,9},{9,8},{12,13... | collective-permute-start | bytes 1769480 | tf_op jit(solution)/shard_map/ppermute | solution.py:552
  58.3 22.5 %collective-permute-start.9 = (bf16[128,2304]{1,0:T(8,128)(2,1)}, bf16[128,2304]{1,0:T(8,128)(2,1)}, u32[]{:S(2)}, u32[]{:S(2)}) collective-permute-start(bf16[128,2304]{1,0:T(8,128)(2,1)} %get-tuple-element.84), channel_id=1, source_target_pairs={{0,4},{1,5},{4,0},{5,1},{2,6},{3,7},{6,2},{7,3},{8,12},{9,13},{12,... | collective-permute-start | bytes 1769480 | tf_op jit(solution)/shard_map/ppermute | solution.py:552
  59.2 45.9 %collective-permute-start.14 = (bf16[128,2304]{1,0:T(8,128)(2,1)}, bf16[128,2304]{1,0:T(8,128)(2,1)}, u32[]{:S(2)}, u32[]{:S(2)}) collective-permute-start(bf16[128,2304]{1,0:T(8,128)(2,1)} %get-tuple-element.96), channel_id=1, source_target_pairs={{0,5},{1,4},{4,1},{5,0},{2,7},{3,6},{6,3},{7,2},{8,13},{9,12},{12,... | collective-permute-start | bytes 1769480 | tf_op jit(solution)/shard_map/ppermute | solution.py:552
  64.9 1.7 collective-permute-start.6
  64.9 2.1 %collective-permute-start.7 = (bf16[4,128,256]{2,1,0:T(8,128)(2,1)}, bf16[4,128,256]{2,1,0:T(8,128)(2,1)S(1)}, u32[]{:S(2)}, u32[]{:S(2)}) collective-permute-start(bf16[4,128,256]{2,1,0:T(8,128)(2,1)} %get-tuple-element.81), channel_id=1, source_target_pairs={{0,2},{2,0},{1,3},{3,1},{4,6},{6,4},{5,7},{7,5},{8,10},{10,8},{9,1... | collective-permute-start | bytes 786440 | tf_op jit(solution)/shard_map/ppermute | solution.py:546
  84.6 8.2 %collective-permute-start.10 = (bf16[2,128,256]{2,1,0:T(8,128)(2,1)S(1)}, bf16[2,128,256]{2,1,0:T(8,128)(2,1)S(1)}, u32[]{:S(2)}, u32[]{:S(2)}) collective-permute-start(bf16[2,128,256]{2,1,0:T(8,128)(2,1)S(1)} %get-tuple-element.90), channel_id=1, source_target_pairs={{8,0},{16,8},{24,16},{9,1},{17,9},{25,17},{10,2},{18,10},{26,18},{... | collective-permute-start | bytes 393224 | tf_op jit(solution)/shard_map/ppermute | solution.py:760
  85.9 19.1 %collective-permute-start.11 = (bf16[2,128,256]{2,1,0:T(8,128)(2,1)S(1)}, bf16[2,128,256]{2,1,0:T(8,128)(2,1)S(1)}, u32[]{:S(2)}, u32[]{:S(2)}) collective-permute-start(bf16[2,128,256]{2,1,0:T(8,128)(2,1)S(1)} %get-tuple-element.91), channel_id=1, source_target_pairs={{16,0},{24,8},{17,1},{25,9},{18,2},{26,10},{19,3},{27,11},{20,4},{... | collective-permute-start | bytes 393224 | tf_op jit(solution)/shard_map/ppermute | solution.py:760
  87.2 17.8 %collective-permute-start.12 = (bf16[2,128,256]{2,1,0:T(8,128)(2,1)S(1)}, bf16[2,128,256]{2,1,0:T(8,128)(2,1)S(1)}, u32[]{:S(2)}, u32[]{:S(2)}) collective-permute-start(bf16[2,128,256]{2,1,0:T(8,128)(2,1)S(1)} %get-tuple-element.92), channel_id=1, source_target_pairs={{24,0},{25,1},{26,2},{27,3},{28,4},{29,5},{30,6},{31,7}} | collective-permute-start | bytes 393224 | tf_op jit(solution)/shard_map/ppermute | solution.py:760
  113.5 37.7 %copy-start.19 = (s32[16]{0:T(128)S(1)}, s32[16]{0:T(128)}, u32[]{:S(2)}) copy-start(s32[16]{0:T(128)} %copy-done.17) | copy-start | bytes 196
  113.5 4.3 %collective-permute-start.13 = (bf16[128,256]{1,0:T(8,128)(2,1)S(1)}, bf16[128,256]{1,0:T(8,128)(2,1)S(1)}, u32[]{:S(2)}, u32[]{:S(2)}) collective-permute-start(bf16[128,256]{1,0:T(8,128)(2,1)S(1)} %get-tuple-element.94), channel_id=1, source_target_pairs={{0,4},{4,0},{1,5},{5,1},{2,6},{6,2},{3,7},{7,3},{8,12},{12,8},{9,1... | collective-permute-start | bytes 196616 | tf_op jit(solution)/shard_map/ppermute | solution.py:546
  123.0 17.7 %collective-permute-start.15 = (bf16[128,2688]{1,0:T(8,128)(2,1)}, bf16[128,2688]{1,0:T(8,128)(2,1)S(1)}, u32[]{:S(2)}, u32[]{:S(2)}) collective-permute-start(bf16[128,2688]{1,0:T(8,128)(2,1)} %get-tuple-element.99), channel_id=1, source_target_pairs={{0,1},{1,0},{4,5},{5,4},{2,3},{3,2},{6,7},{7,6},{8,9},{9,8},{12,13... | collective-permute-start | bytes 2064392 | tf_op jit(solution)/shard_map/ppermute | solution.py:552
  123.5 18.6 %collective-permute-start.16 = (bf16[128,2688]{1,0:T(8,128)(2,1)}, bf16[128,2688]{1,0:T(8,128)(2,1)S(1)}, u32[]{:S(2)}, u32[]{:S(2)}) collective-permute-start(bf16[128,2688]{1,0:T(8,128)(2,1)} %get-tuple-element.100), channel_id=1, source_target_pairs={{0,4},{1,5},{4,0},{5,1},{2,6},{3,7},{6,2},{7,3},{8,12},{9,13},{12,... | collective-permute-start | bytes 2064392 | tf_op jit(solution)/shard_map/ppermute | solution.py:552
  125.1 26.1 %collective-permute-start.17 = (bf16[128,2688]{1,0:T(8,128)(2,1)}, bf16[128,2688]{1,0:T(8,128)(2,1)S(1)}, u32[]{:S(2)}, u32[]{:S(2)}) collective-permute-start(bf16[128,2688]{1,0:T(8,128)(2,1)} %get-tuple-element.101), channel_id=1, source_target_pairs={{0,5},{1,4},{4,1},{5,0},{2,7},{3,6},{6,3},{7,2},{8,13},{9,12},{12,... | collective-permute-start | bytes 2064392 | tf_op jit(solution)/shard_map/ppermute | solution.py:552
  157.2 2.4 %collective-permute-start.18 = (bf16[4,128,768]{2,1,0:T(8,128)(2,1)S(1)}, bf16[4,128,768]{2,1,0:T(8,128)(2,1)S(1)}, u32[]{:S(2)}, u32[]{:S(2)}) collective-permute-start(bf16[4,128,768]{2,1,0:T(8,128)(2,1)S(1)} %get-tuple-element.104), channel_id=1, source_target_pairs={{0,2},{2,0},{1,3},{3,1},{4,6},{6,4},{5,7},{7,5},{8,10},{10,8},{9,1... | collective-permute-start | bytes 2359304 | tf_op jit(solution)/shard_map/ppermute | solution.py:546
  160.2 13.1 %collective-permute-start.19 = (bf16[2,128,768]{2,1,0:T(8,128)(2,1)S(1)}, bf16[2,128,768]{2,1,0:T(8,128)(2,1)S(1)}, u32[]{:S(2)}, u32[]{:S(2)}) collective-permute-start(bf16[2,128,768]{2,1,0:T(8,128)(2,1)S(1)} %get-tuple-element.106), channel_id=1, source_target_pairs={{0,8},{8,0},{16,24},{24,16},{1,9},{9,1},{17,25},{25,17},{2,10},{10... | collective-permute-start | bytes 1179656 | tf_op jit(solution)/shard_map/ppermute | solution.py:803
  171.3 16.7 %collective-permute-start.26 = (bf16[64,2304]{1,0:T(8,128)(2,1)S(1)}, bf16[64,2304]{1,0:T(8,128)(2,1)S(1)}, u32[]{:S(2)}, u32[]{:S(2)}) collective-permute-start(bf16[64,2304]{1,0:T(8,128)(2,1)S(1)} %get-tuple-element.112), channel_id=1, source_target_pairs={{0,5},{1,4},{4,1},{5,0},{2,7},{3,6},{6,3},{7,2},{8,13},{9,12},{12,... | collective-permute-start | bytes 884744 | tf_op jit(solution)/shard_map/ppermute | solution.py:552
  174.0 10.2 %collective-permute-start.20 = (bf16[1,128,768]{2,1,0:T(8,128)(2,1)S(1)}, bf16[1,128,768]{2,1,0:T(8,128)(2,1)S(1)}, u32[]{:S(2)}, u32[]{:S(2)}) collective-permute-start(bf16[1,128,768]{2,1,0:T(8,128)(2,1)S(1)} %get-tuple-element.109), channel_id=1, source_target_pairs={{0,16},{8,24},{16,0},{24,8},{1,17},{9,25},{17,1},{25,9},{2,18},{10... | collective-permute-start | bytes 589832 | tf_op jit(solution)/shard_map/ppermute | solution.py:803
  174.9 13.4 %collective-permute-start.25 = (bf16[64,2304]{1,0:T(8,128)(2,1)S(1)}, bf16[64,2304]{1,0:T(8,128)(2,1)S(1)}, u32[]{:S(2)}, u32[]{:S(2)}) collective-permute-start(bf16[64,2304]{1,0:T(8,128)(2,1)S(1)} %get-tuple-element.112), channel_id=1, source_target_pairs={{0,4},{1,5},{4,0},{5,1},{2,6},{3,7},{6,2},{7,3},{8,12},{9,13},{12,... | collective-permute-start | bytes 884744 | tf_op jit(solution)/shard_map/ppermute | solution.py:552
  176.4 11.9 %collective-permute-start.24 = (bf16[64,2304]{1,0:T(8,128)(2,1)S(1)}, bf16[64,2304]{1,0:T(8,128)(2,1)S(1)}, u32[]{:S(2)}, u32[]{:S(2)}) collective-permute-start(bf16[64,2304]{1,0:T(8,128)(2,1)S(1)} %get-tuple-element.107.refs_3_.refs_1_), channel_id=1, source_target_pairs={{0,1},{1,0},{4,5},{5,4},{2,3},{3,2},{6,7},{7,6},{8,9},{9,8},{12,13... | collective-permute-start | bytes 884744 | tf_op jit(solution)/shard_map/ppermute | solution.py:552
  184.8 6.4 %collective-permute-start.23 = (bf16[64,768]{1,0:T(8,128)(2,1)S(1)}, bf16[64,768]{1,0:T(8,128)(2,1)S(1)}, u32[]{:S(2)}, u32[]{:S(2)}) collective-permute-start(bf16[64,768]{1,0:T(8,128)(2,1)S(1)} %get-tuple-element.111), channel_id=1, source_target_pairs={{0,5},{1,4},{4,1},{5,0},{2,7},{3,6},{6,3},{7,2},{8,13},{9,12},{12,... | collective-permute-start | bytes 294920 | tf_op jit(solution)/shard_map/ppermute | solution.py:552
  187.5 5.4 %collective-permute-start.22 = (bf16[64,768]{1,0:T(8,128)(2,1)S(1)}, bf16[64,768]{1,0:T(8,128)(2,1)S(1)}, u32[]{:S(2)}, u32[]{:S(2)}) collective-permute-start(bf16[64,768]{1,0:T(8,128)(2,1)S(1)} %get-tuple-element.111), channel_id=1, source_target_pairs={{0,4},{1,5},{4,0},{5,1},{2,6},{3,7},{6,2},{7,3},{8,12},{9,13},{12,... | collective-permute-start | bytes 294920 | tf_op jit(solution)/shard_map/ppermute | solution.py:552
  188.0 4.8 %collective-permute-start.21 = (bf16[64,768]{1,0:T(8,128)(2,1)S(1)}, bf16[64,768]{1,0:T(8,128)(2,1)S(1)}, u32[]{:S(2)}, u32[]{:S(2)}) collective-permute-start(bf16[64,768]{1,0:T(8,128)(2,1)S(1)} %get-tuple-element.110.refs_5_.refs_1_), channel_id=1, source_target_pairs={{0,1},{1,0},{4,5},{5,4},{2,3},{3,2},{6,7},{7,6},{8,9},{9,8},{12,13... | collective-permute-start | bytes 294920 | tf_op jit(solution)/shard_map/ppermute | solution.py:552
  (23 other events, 144.2 us)
Sparse Core Ops, SparseCore 0:
  11.7 29.3 all-gather.4
  43.0 37.6 all-gather.6
  113.6 55.9 reduce-scatter.1

commit v4 on v3

--- a/solution.py
+++ b/solution.py
@@ -26,8 +26,6 @@
 SEQ = ("z", "x", "core")
 PLANE = ("x", "batch")
 FOUR = 4
-TILES = 6
-WIDE = TILES * LANE
 
 VM = pl.BlockSpec(memory_space=pltpu.VMEM)
 SM = pl.BlockSpec(memory_space=pltpu.SMEM)
@@ -56,11 +54,19 @@
     return pl.CostEstimate(flops=0, bytes_accessed=int(micros * 3.6e6), transcendentals=0)
 
 
-def call(kernel, name, ins, specs, outs, scratch=(), after=(), room=8, micros=0.01):
+def call(kernel, name, ins, specs, outs, scratch=(), after=(), room=8, micros=0.01, token=False):
     count, extra = len(ins), len(after)
 
+    if token:
+        outs = (*outs, shape((8, LANE), F32))
+
     def body(*refs):
-        kernel(*refs[:count], *refs[count + extra :])
+        refs = refs[:count] + refs[count + extra :]
+        if token:
+            at = count + len(outs) - 1
+            refs[at][...] = jnp.zeros((8, LANE), F32)
+            refs = refs[:at] + refs[at + 1 :]
+        kernel(*refs)
 
     return pl.pallas_call(
         body,
@@ -205,8 +211,8 @@
     )
 
 
-def start_tile(place):
-    return (place * 11) // 2
+def packed(hidden):
+    return -(-(3 * hidden // FOUR) // LANE) * LANE
 
 
 def feed_kernel(tile, sc, normed, grad_out, mid, gain, wo, wg, wu, wd, *rest):
@@ -251,10 +257,16 @@
     grad = grad + dy.astype(F32)
     dmid[...] = grad
     gain_grad[...] = gains
+    part = wg.shape[1] // FOUR
     for k in range(FOUR):
-        cols = pl.ds(pl.multiple_of(start_tile(sc[4] ^ k) * LANE, LANE), WIDE)
-        for i, ref in enumerate((dgate_s, dup_s, act_s)):
-            sends[k][:, i * WIDE : (i + 1) * WIDE] = ref[:, cols]
+        place = sc[4] ^ k
+        cols = pl.ds(pl.multiple_of((place // 2) * 2 * part, LANE), 2 * part)
+        pieces = []
+        for ref in (dgate_s, dup_s, act_s):
+            both = ref[:, cols].astype(F32)
+            pieces.append(jnp.where(place % 2 == 0, both[:, :part], both[:, part:]))
+        pieces.append(jnp.zeros((both.shape[0], sends[k].shape[1] - 3 * part), F32))
+        sends[k][...] = jnp.concatenate(pieces, axis=1).astype(BF16)
     turned = nt(vo[...], grad.astype(BF16)).astype(BF16)
     dop[:, 0:HD, :] = jnp.zeros((GROUPS, HD, dop.shape[2]), BF16)
     for g in range(GROUPS):
@@ -267,12 +279,13 @@
     tok, width = normed.shape
     hidden = wg.shape[1]
     tile = 2 * LANE
+    wide = packed(hidden)
     return call(
         functools.partial(feed_kernel, tile),
         "feed",
         (sc, normed, grad_out, mid, gain, wo, wg, wu, wd),
         [SM] + [VM] * 4 + [ANY] * 4,
-        (shape((tok, 3 * WIDE), BF16),) * FOUR
+        (shape((tok, wide), BF16),) * FOUR
         + (
             shape((tok, width), BF16),
             shape((tok, width), F32),
@@ -395,7 +408,7 @@
         kv_cut_kernel, "kv_cut", (sc, *terms), [SM] + [HB] * 4,
         (shape(dims, F32),) + (shape(dims, BF16),) * count,
         [pltpu.VMEM((4,) + terms[0].shape, BF16), pltpu.SemaphoreType.DMA((4,))],
-        after=after, room=12,
+        after=after, room=6,
     )
 
 
@@ -406,7 +419,7 @@
 def base_terms(dq, wq, after=()):
     return call(
         base_kernel, "base", (dq, wq), [VM] * 2, (shape((dq.shape[0], wq.shape[0]), F32),),
-        after=after, room=12,
+        after=after, room=6,
     )[0]
 
 
@@ -429,7 +442,7 @@
 
 def weight_kernel(counts, plan, extra, split, sc, *refs):
     lefts = []
-    for count in counts:
+    for count, unused in counts:
         lefts.append(refs[:count])
         refs = refs[count:]
     rights, refs = refs[:FOUR], refs[FOUR:]
@@ -446,10 +459,12 @@
             pairs.append((rights[k].at[:, at : at + LANE], wide.at[which, row : row + LANE, span]))
         for t, (source, target) in enumerate(pairs):
             copies.append(pltpu.make_async_copy(source, target, sems.at[len(counts) + t, k]))
-        for i, count in enumerate(counts):
+        for i, (count, kind) in enumerate(counts):
             if count == 0:
                 continue
             source = lefts[i][0].at[sc[4] ^ k]
+            if kind is not None:
+                source = lefts[i][0].at[sc[4] ^ k, kind]
             copies.append(pltpu.make_async_copy(source, wide.at[i, :, span], sems.at[i, k]))
     for copy in copies:
         copy.start()
@@ -479,8 +494,8 @@
     rows = lefts[0][0]
     moves = 1 + (rights[0].shape[1] - width) // LANE
     wide = width + sum(array.shape[1] for array in extra)
-    counts = tuple(len(arrays) for unused, arrays in lefts)
-    flat = [array for unused, arrays in lefts for array in arrays] + rights
+    counts = tuple((len(arrays), kind) for unused, arrays, kind in lefts)
+    flat = [array for unused, arrays, kind in lefts for array in arrays] + rights
     if nz:
         outs = (shape((nz, rows // (2 * nz), wide), BF16),) * 2
     else:
@@ -498,7 +513,7 @@
             pltpu.SemaphoreType.DMA((len(lefts) + moves, FOUR)),
         ],
         after,
-        20,
+        14,
     )
 
 
@@ -554,29 +569,21 @@
 
 
 def place_kernel(plan, count, sc, *refs):
-    results = refs[count : count + max(entry[3] for entry in plan) + 1]
-    small = refs[count + len(results) :]
-    for k in range(FOUR):
+    results = refs[count : count + len(plan)]
+    small = refs[count + len(plan) :]
+    for k in range(0, FOUR, 2):
         place = sc[4] ^ k
-        start = start_tile(place)
-        twice = (place > 0) & (start < start_tile(place - 1) + TILES)
-        for chunk, begin, stop, to, first in plan:
-            part = refs[chunk * FOUR + k][:, begin:stop].astype(F32)
+        even = place % 2 == 0
+        for (begin, stop), result in zip(plan, results):
             size = stop - begin
-            if first is None:
-                cols = pl.ds(pl.multiple_of(place * size, size), size)
-                results[to][:, cols] = part
-                continue
-            for i in range(size // LANE):
-
-                @pl.when(jnp.logical_not(twice) if first + i == 0 else start >= 0)
-                def _():
-                    cols = pl.ds(pl.multiple_of((start + first + i) * LANE, LANE), LANE)
-                    results[to][:, cols] = part[:, i * LANE : (i + 1) * LANE]
-
+            near = refs[k][:, begin:stop].astype(F32)
+            next_one = refs[k + 1][:, begin:stop].astype(F32)
+            pair = [jnp.where(even, near, next_one), jnp.where(even, next_one, near)]
+            cols = pl.ds(pl.multiple_of((place // 2) * 2 * size, LANE), 2 * size)
+            result[:, cols] = jnp.concatenate(pair, axis=1)
     if small:
         expand, gains = small
-        begin = plan[-1][2]
+        begin = plan[-1][1]
         total = [refs[k][:, begin:].astype(F32) for k in range(FOUR)]
         even = [jnp.where(sc[4] % 2 == 0, total[i], total[i + 1]) for i in (0, 2)]
         odd = [jnp.where(sc[4] % 2 == 0, total[i + 1], total[i]) for i in (0, 2)]
@@ -587,18 +594,18 @@
         gains[...] = value.T[HD : HD + 8, :]
 
 
-def put(sc, parts, plan, widths, small=0, after=()):
+def put(sc, parts, plan, widths, small=0, after=(), token=False):
     rows = parts[0].shape[0]
     outs = tuple(shape((rows, width), F32) for width in widths)
     if small:
         outs += (shape((rows // FOUR, small), F32), shape((8, rows), F32))
     return call(
         functools.partial(place_kernel, plan, len(parts)), "put", (sc, *parts),
-        [SM] + [VM] * len(parts), outs, after=after,
-    )
-
-
-def enter_kernel(nz, hidden, gain, wl, we, dy, wq, latent, kv, left_dy, left_one, qp, wq_s, sem):
+        [SM] + [VM] * len(parts), outs, after=after, token=token,
+    )
+
+
+def enter_kernel(nz, hidden, gain, wl, we, dy, wq, latent, kv, left, qp, wq_s, sem):
     load = pltpu.make_async_copy(wq, wq_s, sem)
     load.start()
     value, unused = norm_forward(hidden[...].astype(F32), gain_row(gain))
@@ -608,8 +615,8 @@
     for g in range(GROUPS):
         span = slice(g * LANE, (g + 1) * LANE)
         kv[:, span] = nn(rows[:, g * LAT : (g + 1) * LAT], we[:, span]).astype(BF16)
-    left_dy[...] = by_core(dy[...].astype(F32).T, nz).astype(BF16)
-    left_one[...] = by_core(value.T, nz).astype(BF16)
+    left[0] = by_core(dy[...].astype(F32).T, nz).astype(BF16)
+    left[1] = by_core(value.T, nz).astype(BF16)
     load.wait()
     turned = (nn(low, wq_s[...]).astype(BF16) * scale).T
     qp[:, HD:, :] = jnp.zeros((GROUPS, HD, qp.shape[2]), BF16)
@@ -621,7 +628,6 @@
 
 def enter(hidden, gain, wl, we, dy, wq, nz):
     tok, width = hidden.shape
-    left = shape((width, tok), BF16)
     return call(
         functools.partial(enter_kernel, nz),
         "enter",
@@ -630,8 +636,7 @@
         (
             shape((tok, wl.shape[1]), BF16),
             shape((tok, we.shape[1]), BF16),
-            left,
-            left,
+            shape((2, width, tok), BF16),
             shape((GROUPS, 2 * HD, PER * tok), BF16),
         ),
         [pltpu.VMEM(wq.shape, BF16), pltpu.SemaphoreType.DMA],
@@ -640,7 +645,7 @@
 
 
 def leave_kernel(
-    nz, count, sc, hidden, dmid, gain, dq, base, latent, gain_two, we, wl, left_o, left_one, *refs
+    nz, count, sc, hidden, dmid, gain, dq, base, latent, gain_two, we, wl, left, *refs
 ):
     moved = refs[:count]
     input_grad, small = refs[count : count + 2]
@@ -683,22 +688,20 @@
         cols = pl.ds(pl.multiple_of(place * half, half), half)
         end = 2 * part + half
         sends[k][:, 2 * part : end] = lat[:, cols].astype(BF16)
-        for left in (left_o, left_one):
-            for at in range(0, left.shape[0], LANE):
-                sends[k][:, end : end + LANE] = left[at : at + LANE, :]
-                end += LANE
-
-
-def leave(sc, hidden, dmid, gain, dq, base, latent, gain_two, we, wl, lefts, moved, nz, after=()):
+        for at in range(0, left.shape[0], LANE):
+            sends[k][:, end + at : end + at + LANE] = left[at : at + LANE, :]
+
+
+def leave(sc, hidden, dmid, gain, dq, base, latent, gain_two, we, wl, left, moved, nz, after=()):
     tok, width = hidden.shape
     lat = latent.shape[1]
     return call(
         functools.partial(leave_kernel, nz, len(moved)),
         "leave",
-        (sc, hidden, dmid, gain, dq, base, latent, gain_two, we, wl, *lefts, *moved),
-        [SM] + [VM] * (11 + len(moved)),
+        (sc, hidden, dmid, gain, dq, base, latent, gain_two, we, wl, left, *moved),
+        [SM] + [VM] * (10 + len(moved)),
         (shape((tok, width), BF16), shape((width, LANE), BF16))
-        + (shape((tok, (2 * width + lat) // FOUR + 2 * width), BF16),) * FOUR,
+        + (shape((tok, (2 * width + lat) // FOUR + width), BF16),) * FOUR,
         [pltpu.VMEM((tok, lat), F32), pltpu.VMEM((width, LANE), F32)],
         after,
         60,
@@ -721,10 +724,10 @@
     hidden = inputs[0]
     dy = cotangent[0]
 
-    latent, kv, left_dy, left_one, qp = enter(
+    latent, kv, left, qp = enter(
         hidden, norm_attn, proj_latent, proj_expand, dy, proj_query, nz
     )
-    dys = lax.all_gather(left_dy, PLANE, axis=0)
+    early = lax.all_gather(left, PLANE, axis=0)
     relative = nz == 4
     if relative:
         moved = [kv]
@@ -743,19 +746,19 @@
     n2s = lax.all_gather(left_n2, PLANE, axis=0)
     fed = feed(
         sc, normed_two, dy, mid, norm_ffn, proj_output, ffn_gate, ffn_up, ffn_down,
-        after=(dys,),
     )
     output, dmid, dop, gain_two = fed[FOUR:]
     parts_a = plane_swap(fed[:FOUR])
 
+    quarter = hidden_size // FOUR
     last = []
 
     dq, keep_own, keep_far, send_own, send_far = attend_back(
-        sc, kvs, qp, dop, ot, logs, nz, tok
+        sc, kvs, qp, dop, ot, logs, nz, tok, after=(early,)
     )
     pieces = (keep_own, keep_far, swap(send_own, "core"), swap(send_far, "core"))
     if relative:
-        moved = list(kv_cut(sc, pieces, nz - 1, after=(n2s, *parts_a[1:3])))
+        moved = list(kv_cut(sc, pieces, nz - 1, after=parts_a[1:3]))
         for k in range(1, nz):
             moved[k] = lax.ppermute(moved[k], "z", [(i, i - k) for i in range(k, nz)])
         last.append(moved[0])
@@ -769,16 +772,16 @@
     moved = [rest, swap(side, "x")]
     (main,) = weight_terms(
         sc,
-        ((width, (n2s,)), (width, (dys,))),
+        ((width, (n2s,), None), (width, (early,), 0)),
         parts_a,
-        ((0, 0, 2 * WIDE), (1, 2 * WIDE, 3 * WIDE)),
+        ((0, 0, 2 * quarter), (1, 2 * quarter, packed(hidden_size))),
         after=last[-1:],
     )
     last.append(main)
     main = lax.psum_scatter(main, ("z", "core"), scatter_dimension=0, tiled=True)
     left_out = leave(
         sc, hidden, dmid, norm_attn, dq, base, latent, gain_two, proj_expand, proj_latent,
-        (left_o, left_one), moved, nz, after=last[-1:],
+        left_o, moved, nz, after=last[-1:],
     )
     input_grad, small = left_out[:2]
     last.append(input_grad)
@@ -787,12 +790,11 @@
     end = 2 * part + lat_part
     keep, send = weight_terms(
         sc,
-        ((width, ()), (width, ())),
+        ((width, (), None), (width, (early,), 1)),
         parts_c,
         ((0, 0, part), (1, part, end)),
         (small,),
         nz,
-        after=last[-1:],
     )
     last.append(keep)
     came = swap(send, "core")
@@ -802,25 +804,25 @@
         last.append(keep)
         came = lax.ppermute(send, "z", [(i, i ^ (1 << step)) for i in range(nz)])
         step += 1
-        if step == 1:
-            main = split_rows(sc, (main,), after=last[-1:])
-            last.append(main[0])
+    main = split_rows(sc, (main,), after=last[-1:])
+    last.append(main[0])
     rest = split_rows(sc, (keep[0], came[0]), after=last[-1:])
     last.append(rest[0])
-    grad_gate, grad_up, grad_down_t = put(
+    grad_gate, grad_up, grad_down_t, token = put(
         sc,
         main,
-        tuple((0, i * WIDE, (i + 1) * WIDE, i, 0) for i in range(3)),
+        tuple((i * quarter, (i + 1) * quarter) for i in range(3)),
         (hidden_size,) * 3,
         after=last[-1:],
+        token=True,
     )
     grad_output, grad_query, grad_latent, expand_t, gains = put(
         sc,
         rest,
-        ((0, 0, part, 0, None), (0, part, 2 * part, 1, None), (0, 2 * part, end, 2, None)),
+        ((0, part), (part, 2 * part), (2 * part, end)),
         (width, width, latent.shape[1]),
         LAT,
-        after=(grad_gate,),
+        after=(token,),
     )
     grad_expand = expand_t.T
     grad_norm_attn, grad_norm_ffn = gains[0], gains[1]

time: 203 us -> 201 us (level)
  starting transfers between devices: 35.2 us -> 31.2 us
  waiting for transfers between devices: 87.4 us -> 90.9 us
    ppermute x2, waiting for transfers between devices: 6.26 us -> 28.1 us  [shards(): came = lax.ppermute(send, 'z', [(i, i ^ 1 << step) for i in range(nz)])]
    all_gather x1, waiting for transfers between devices: 13.7 us -> 0.02 us  [shards(): n2s = lax.all_gather(left_n2, PLANE, axis=0)]
    reduce_scatter x1, waiting for transfers between devices: 9.26 us -> 2.86 us  [shards(): lax.psum_scatter(main, ('z', 'core'), scatter_dimension=0, tiled=True)]
    ppermute x7, waiting for transfers between devices: 13.8 us -> 16.9 us  [swap(): return lax.ppermute(value, axis, [(0, 1), (1, 0)])]
    ppermute x3, waiting for transfers between devices: 14.7 us -> 12.2 us  [shards(): moved[k] = lax.ppermute(moved[k], 'z', [(i, i - k) for i in range(k, nz)])]
    ppermute x12, waiting for transfers between devices: 27 us -> 29.3 us  [plane_swap(): lax.ppermute(parts[k], PLANE, [(d, d ^ k) for d in range(FOUR)])]
    unnamed x50 -> x44, local copies, waits for them, and re-layouts: 14.8 us -> 14 us
  transfers between devices with their start and end apart: 30 -> 30, of which waited for: 18 -> 19; matrix products, arithmetic and copies ran while one was open for 0% -> 0% of each run, Pallas kernels for 19% -> 19%
where the time goes in v4:
time: 201 us
  waiting for transfers between devices  90.9 us (45%)
  Pallas kernels  49.2 us (24%)
  starting transfers between devices  31.2 us (16%)
  local copies, waits for them, and re-layouts  15.3 us (8%)
  between operations  14.1 us (7%)
    pallas_call x17, Pallas kernels, call(): pl.pallas_call(body, out_shape=tuple(outs), in_specs=list(specs) + [ANY]...  49.2 us
    ppermute x12, waiting for transfers between devices, plane_swap(): lax.ppermute(parts[k], PLANE, [(d, d ^ k) for d in range(FOUR)])  29.3 us
    ppermute x2, waiting for transfers between devices, shards(): came = lax.ppermute(send, 'z', [(i, i ^ 1 << step) for i in range(nz)])  28.1 us
    ppermute x7, waiting for transfers between devices, swap(): return lax.ppermute(value, axis, [(0, 1), (1, 0)])  16.9 us
    ppermute x12, starting transfers between devices, plane_swap(): lax.ppermute(parts[k], PLANE, [(d, d ^ k) for d in range(FOUR)])  14.1 us
    unnamed x44, local copies, waits for them, and re-layouts  14 us
    ppermute x3, waiting for transfers between devices, shards(): moved[k] = lax.ppermute(moved[k], 'z', [(i, i - k) for i in range(k, nz)])  12.2 us
    ppermute x3, starting transfers between devices, shards(): moved.append(lax.ppermute(kv, 'z', [(i, i + k) for i in range(nz - k)]))  10.7 us
  transfers between devices with their start and end apart: 30, of which 19 were waited for; matrix products, arithmetic and copies ran while one was open for 0% of the time, Pallas kernels for 19%

profile of v4, /device:TPU:0, one launch (start us, length us, event | category | flops | bytes accessed | tf_op | source)
XLA Modules:
  0.0 200.7 jit_solution(10708346583565182320)
XLA Ops:
  7.2 4.4 %enter.1 = (bf16[128,512]{1,0:T(8,128)(2,1)}, bf16[128,256]{1,0:T(8,128)(2,1)}, bf16[2,1024,128]{2,1,0:T(8,128)(2,1)}, bf16[2,128,1024]{2,1,0:T(8,128)(2,1)}) custom-call(bf16[128,1024]{1,0:T(8,128)(2,1)} %bitcast.26, bf16[1024]{0:T(1024)(128)(2,1)} %refs_3_.3, bf16[1024,512]{1,0:T(8,128)(2,1)} %refs_9_.1, bf16[256,256]{1,0:T(8,128)(2,1)} %refs_8_.5, ...), custom_call_target="tpu_custom_call" | custom-call | bytes 36000 | tf_op jit(solution)/shard_map/enter/pallas_call | solution.py:71
  11.7 7.0 %collective-permute-start.2 = (bf16[128,256]{1,0:T(8,128)(2,1)}, bf16[128,256]{1,0:T(8,128)(2,1)S(1)}, u32[]{:S(2)}, u32[]{:S(2)}) collective-permute-start(bf16[128,256]{1,0:T(8,128)(2,1)} %get-tuple-element.66.refs_0_), channel_id=1, source_target_pairs={{0,24},{1,25},{2,26},{3,27},{4,28},{5,29},{6,30},{7,31}} | collective-permute-start | bytes 196616 | tf_op jit(solution)/shard_map/ppermute | solution.py:735
  19.9 2.5 %collective-permute-start = (bf16[128,256]{1,0:T(8,128)(2,1)}, bf16[128,256]{1,0:T(8,128)(2,1)S(1)}, u32[]{:S(2)}, u32[]{:S(2)}) collective-permute-start(bf16[128,256]{1,0:T(8,128)(2,1)} %get-tuple-element.66.refs_0_), channel_id=1, source_target_pairs={{0,8},{8,16},{16,24},{1,9},{9,17},{17,25},{2,10},{10,18},{18,26},{... | collective-permute-start | bytes 196616 | tf_op jit(solution)/shard_map/ppermute | solution.py:735
  23.2 1.4 collective-permute-done.refs_1_
  25.5 1.6 collective-permute-start.3
  27.0 8.9 %collective-permute-done.3.refs_2_ = bf16[4,128,256]{2,1,0:T(8,128)(2,1)S(1)} collective-permute-done((bf16[4,128,256]{2,1,0:T(8,128)(2,1)S(1)}, bf16[4,128,256]{2,1,0:T(8,128)(2,1)S(1)}, u32[]{:S(2)}, u32[]{:S(2)}) %collective-permute-start.3) | collective-permute-done | bytes 262176 | tf_op jit(solution)/shard_map/ppermute | solution.py:561
  35.9 1.5 collective-permute-done.5.refs_4_
  38.1 4.9 %attend.1 = (bf16[2048,256]{1,0:T(8,128)(2,1)}, f32[2,64,1024]{2,1,0:T(8,128)}, f32[2,1,1024]{2,1,0:T(1,128)}, bf16[1024,128]{1,0:T(8,128)(2,1)}, bf16[1024,128]...) custom-call(s32[16]{0:T(128)} %copy-done.14, bf16[4,128,256]{2,1,0:T(8,128)(2,1)} %copy-done.6, ...), custom_call_target="tpu_custom_call" | custom-call | bytes 36000 | tf_op jit(solution)/shard_map/attend/pallas_call | solution.py:71
  43.1 15.7 %feed.1 = (bf16[128,2176]{1,0:T(8,128)(2,1)}, bf16[128,2176]{1,0:T(8,128)(2,1)}, bf16[128,2176]{1,0:T(8,128)(2,1)}, bf16[128,2176]{1,0:T(8,128)(2,1)}, bf16[128,...) custom-call(s32[16]{0:T(128)} %copy-done.14, ...), custom_call_target="tpu_custom_call" | custom-call | bytes 36000 | tf_op jit(solution)/shard_map/feed/pallas_call | solution.py:71
  58.8 1.7 collective-permute-start.8
  62.4 4.8 %attend_back.1 = (bf16[128,1024]{1,0:T(8,128)(2,1)}, bf16[4,128,256]{2,1,0:T(8,128)(2,1)}, bf16[4,128,256]{2,1,0:T(8,128)(2,1)}, bf16[4,128,256]{2,1,0:T(8,128)(2,1)}, bf16[4,128,256]{2,1,0:T(8,128)(2,1)}) custom-call(s32[16]{0:T(128)} %copy-done.14, bf16[2048,256]{1,0:T(8,128)(2,1)} %get-tuple-element.72.refs_1_, ...), custom_call_target="tpu_custom_call" | custom-call | bytes 32400000 | tf_op jit(solution)/shard_map/attend_back/pallas_call | solution.py:71
  67.7 9.0 %collective-permute-done.8.refs_5_.refs_4_ = bf16[128,2176]{1,0:T(8,128)(2,1)S(1)} collective-permute-done((bf16[128,2176]{1,0:T(8,128)(2,1)}, bf16[128,2176]{1,0:T(8,128)(2,1)S(1)}, u32[]{:S(2)}, u32[]{:S(2)}) %collective-permute-start.8) | collective-permute-done | bytes 557088 | tf_op jit(solution)/shard_map/ppermute | solution.py:567
  76.7 3.5 %collective-permute-done.9.refs_6_.refs_5_ = bf16[128,2176]{1,0:T(8,128)(2,1)} collective-permute-done((bf16[128,2176]{1,0:T(8,128)(2,1)}, bf16[128,2176]{1,0:T(8,128)(2,1)}, u32[]{:S(2)}, u32[]{:S(2)}) %collective-permute-start.9) | collective-permute-done | bytes 557088 | tf_op jit(solution)/shard_map/ppermute | solution.py:567
  86.8 1.6 copy-done.2
  91.5 6.9 %collective-permute-done.11.refs_2_ = bf16[2,128,256]{2,1,0:T(8,128)(2,1)S(1)} collective-permute-done((bf16[2,128,256]{2,1,0:T(8,128)(2,1)S(1)}, bf16[2,128,256]{2,1,0:T(8,128)(2,1)S(1)}, u32[]{:S(2)}, u32[]{:S(2)}) %collective-permute-start.11) | collective-permute-done | bytes 131104 | tf_op jit(solution)/shard_map/ppermute | solution.py:763
  98.4 3.9 %collective-permute-done.12.refs_3_ = bf16[2,128,256]{2,1,0:T(8,128)(2,1)S(1)} collective-permute-done((bf16[2,128,256]{2,1,0:T(8,128)(2,1)S(1)}, bf16[2,128,256]{2,1,0:T(8,128)(2,1)S(1)}, u32[]{:S(2)}, u32[]{:S(2)}) %collective-permute-start.12) | collective-permute-done | bytes 131104 | tf_op jit(solution)/shard_map/ppermute | solution.py:763
  104.8 4.9 %weight_terms.2.refs_13_ = bf16[1024,2176]{1,0:T(8,128)(2,1)S(1)} custom-call(s32[16]{0:T(128)S(1)} %copy-done.15, bf16[4,1024,128]{2,1,0:T(8,128)(2,1)S(1)} %bitcast.23, bf16[4,2,1024,128]{3,2,1,0:T(8,128)(2,1)S(1)} %bitcast.21, bf16[128,2176]{1,0:T(8,128)(2,1)S(1)} %copy-done.7, bf16[128,2176]{1,0:T(8,128)(2,1)S(1)} %collective-permute-done.8.refs_5_.refs_4_, ...), custom_call_target="tpu_custom_call" | custom-call | bytes 36000 | tf_op jit(solution)/shard_map/weight_terms/pallas_call | solution.py:71
  109.6 2.1 %copy-done = bf16[1024,2176]{1,0:T(8,128)(2,1)} copy-done((bf16[1024,2176]{1,0:T(8,128)(2,1)}, bf16[1024,2176]{1,0:T(8,128)(2,1)S(1)}, u32[]{:S(2)}) %copy-start) | copy-done | bytes 4456472
  111.8 4.3 %collective-permute-done.13.refs_12_ = bf16[128,256]{1,0:T(8,128)(2,1)S(1)} collective-permute-done((bf16[128,256]{1,0:T(8,128)(2,1)S(1)}, bf16[128,256]{1,0:T(8,128)(2,1)S(1)}, u32[]{:S(2)}, u32[]{:S(2)}) %collective-permute-start.13) | collective-permute-done | bytes 65568 | tf_op jit(solution)/shard_map/ppermute | solution.py:561
  116.7 4.1 %leave.1 = (bf16[128,1024]{1,0:T(8,128)(2,1)}, bf16[1024,128]{1,0:T(8,128)(2,1)}, bf16[128,1664]{1,0:T(8,128)(2,1)}, bf16[128,1664]{1,0:T(8,128)(2,1)}, bf16[128...) custom-call(s32[16]{0:T(128)} %copy-done.14, bf16[128,1024]{1,0:T(8,128)(2,1)} %bitcast.28, ...), custom_call_target="tpu_custom_call" | custom-call | bytes 36000 | tf_op jit(solution)/shard_map/leave/pallas_call | solution.py:71
  122.4 1.9 collective-permute-start.17
  124.3 9.4 %collective-permute-done.15.refs_3_ = bf16[128,1664]{1,0:T(8,128)(2,1)S(1)} collective-permute-done((bf16[128,1664]{1,0:T(8,128)(2,1)}, bf16[128,1664]{1,0:T(8,128)(2,1)S(1)}, u32[]{:S(2)}, u32[]{:S(2)}) %collective-permute-start.15) | collective-permute-done | bytes 426016 | tf_op jit(solution)/shard_map/ppermute | solution.py:567
  134.7 4.4 %collective-permute-done.17.refs_5_ = bf16[128,1664]{1,0:T(8,128)(2,1)S(1)} collective-permute-done((bf16[128,1664]{1,0:T(8,128)(2,1)}, bf16[128,1664]{1,0:T(8,128)(2,1)S(1)}, u32[]{:S(2)}, u32[]{:S(2)}) %collective-permute-start.17) | collective-permute-done | bytes 426016 | tf_op jit(solution)/shard_map/ppermute | solution.py:567
  141.0 2.6 %weight_terms.3 = (bf16[4,128,768]{2,1,0:T(8,128)(2,1)S(1)}, bf16[4,128,768]{2,1,0:T(8,128)(2,1)S(1)}) custom-call(s32[16]{0:T(128)S(1)} %copy-done.16, bf16[4,2,1024,128]{3,2,1,0:T(8,128)(2,1)S(1)} %bitcast.22, bf16[128,1664]{1,0:T(8,128)(2,1)S(1)} %copy-done.10, bf16[128,1664]{1,0:T(8,128)(2,1)S(1)} %collective-permute-done.15.refs_3_, ...), custom_call_target="tpu_custom_call" | custom-call | bytes 36000 | tf_op jit(solution)/shard_map/weight_terms/pallas_call | solution.py:71
  143.7 2.3 %collective-permute-done.18.refs_2_ = bf16[4,128,768]{2,1,0:T(8,128)(2,1)S(1)} collective-permute-done((bf16[4,128,768]{2,1,0:T(8,128)(2,1)S(1)}, bf16[4,128,768]{2,1,0:T(8,128)(2,1)S(1)}, u32[]{:S(2)}, u32[]{:S(2)}) %collective-permute-start.18) | collective-permute-done | bytes 786464 | tf_op jit(solution)/shard_map/ppermute | solution.py:561
  146.8 19.7 %collective-permute-done.19.refs_2_ = bf16[2,128,768]{2,1,0:T(8,128)(2,1)S(1)} collective-permute-done((bf16[2,128,768]{2,1,0:T(8,128)(2,1)S(1)}, bf16[2,128,768]{2,1,0:T(8,128)(2,1)S(1)}, u32[]{:S(2)}, u32[]{:S(2)}) %collective-permute-start.19) | collective-permute-done | bytes 393248 | tf_op jit(solution)/shard_map/ppermute | solution.py:805
  167.1 2.9 %reduce-scatter.2.cloned.1.call-done.refs_1_ = bf16[128,2176]{1,0:T(8,128)(2,1)} async-done(((bf16[1024,2176]{1,0:T(8,128)(2,1)}), bf16[128,2176]{1,0:T(8,128)(2,1)}) %reduce-scatter.2.cloned.1.call-update) | async-done | bytes 557072 | tf_op jit(solution)/shard_map/reduce_scatter | solution.py:781
  171.7 2.5 %collective-permute-start.26 = (bf16[64,2176]{1,0:T(8,128)(2,1)S(1)}, bf16[64,2176]{1,0:T(8,128)(2,1)S(1)}, u32[]{:S(2)}, u32[]{:S(2)}) collective-permute-start(bf16[64,2176]{1,0:T(8,128)(2,1)S(1)} %get-tuple-element.111), channel_id=1, source_target_pairs={{0,5},{1,4},{4,1},{5,0},{2,7},{3,6},{6,3},{7,2},{8,13},{9,12},{12,... | collective-permute-start | bytes 835592 | tf_op jit(solution)/shard_map/ppermute | solution.py:567
  175.3 8.5 %collective-permute-done.20 = bf16[1,128,768]{2,1,0:T(8,128)(2,1)S(1)} collective-permute-done((bf16[1,128,768]{2,1,0:T(8,128)(2,1)S(1)}, bf16[1,128,768]{2,1,0:T(8,128)(2,1)S(1)}, u32[]{:S(2)}, u32[]{:S(2)}) %collective-permute-start.20) | collective-permute-done | bytes 196640 | tf_op jit(solution)/shard_map/ppermute | solution.py:805
  184.8 1.6 collective-permute-start.22
  186.5 1.5 collective-permute-start.21
  188.0 2.1 %put.2 = (f32[64,2816]{1,0:T(8,128)}, f32[64,2816]{1,0:T(8,128)}, f32[64,2816]{1,0:T(8,128)}, f32[8,128]{1,0:T(8,128)S(1)}) custom-call(s32[16]{0:T(128)S(1)} %copy-done.16, bf16[64,2176]{1,0:T(8,128)(2,1)S(1)} %get-tuple-element.108.refs_3_.refs_1_, bf16[64,2176]{1,0:T(8,128)(2,1)S(1)} %collective-permute-done.24.refs_2_, ...), custom_call_target="tpu_custom_call" | custom-call | bytes 36000 | tf_op jit(solution)/shard_map/put/pallas_call | solution.py:71
  (94 shorter events, 32.8 us)
Async XLA Ops:
  7.2 55.2 %all-gather.5.cloned.1.call-start = ((), (), s32[]{:S(2)}) async-start(), calls=%async_computation.2 | async-start | bytes 2621440 | tf_op jit(solution)/shard_map/all_gather | solution.py:730
  11.6 90.8 %all-gather.7.cloned.1.call-start = ((), (), s32[]{:S(2)}) async-start(), calls=%async_computation.3 | async-start | bytes 1310720 | tf_op jit(solution)/shard_map/all_gather | solution.py:746
  11.7 11.5 %collective-permute-start.2 = (bf16[128,256]{1,0:T(8,128)(2,1)}, bf16[128,256]{1,0:T(8,128)(2,1)S(1)}, u32[]{:S(2)}, u32[]{:S(2)}) collective-permute-start(bf16[128,256]{1,0:T(8,128)(2,1)} %get-tuple-element.66.refs_0_), channel_id=1, source_target_pairs={{0,24},{1,25},{2,26},{3,27},{4,28},{5,29},{6,30},{7,31}} | collective-permute-start | bytes 196616 | tf_op jit(solution)/shard_map/ppermute | solution.py:735
  18.6 4.5 %collective-permute-start.1 = (bf16[128,256]{1,0:T(8,128)(2,1)}, bf16[128,256]{1,0:T(8,128)(2,1)S(1)}, u32[]{:S(2)}, u32[]{:S(2)}) collective-permute-start(bf16[128,256]{1,0:T(8,128)(2,1)} %get-tuple-element.66.refs_0_), channel_id=1, source_target_pairs={{0,16},{8,24},{1,17},{9,25},{2,18},{10,26},{3,19},{11,27},{4,20},{... | collective-permute-start | bytes 196616 | tf_op jit(solution)/shard_map/ppermute | solution.py:735
  19.9 4.7 %collective-permute-start = (bf16[128,256]{1,0:T(8,128)(2,1)}, bf16[128,256]{1,0:T(8,128)(2,1)S(1)}, u32[]{:S(2)}, u32[]{:S(2)}) collective-permute-start(bf16[128,256]{1,0:T(8,128)(2,1)} %get-tuple-element.66.refs_0_), channel_id=1, source_target_pairs={{0,8},{8,16},{16,24},{1,9},{9,17},{17,25},{2,10},{10,18},{18,26},{... | collective-permute-start | bytes 196616 | tf_op jit(solution)/shard_map/ppermute | solution.py:735
  25.5 10.4 %collective-permute-start.3 = (bf16[4,128,256]{2,1,0:T(8,128)(2,1)S(1)}, bf16[4,128,256]{2,1,0:T(8,128)(2,1)S(1)}, u32[]{:S(2)}, u32[]{:S(2)}) collective-permute-start(bf16[4,128,256]{2,1,0:T(8,128)(2,1)S(1)} %stack.24.refs_1_), channel_id=1, source_target_pairs={{0,4},{4,0},{1,5},{5,1},{2,6},{6,2},{3,7},{7,3},{8,12},{12,8},{9,1... | collective-permute-start | bytes 786440 | tf_op jit(solution)/shard_map/ppermute | solution.py:561
  27.0 8.9 %collective-permute-start.4 = (bf16[4,128,256]{2,1,0:T(8,128)(2,1)S(1)}, bf16[4,128,256]{2,1,0:T(8,128)(2,1)S(1)}, u32[]{:S(2)}, u32[]{:S(2)}) collective-permute-start(bf16[4,128,256]{2,1,0:T(8,128)(2,1)S(1)} %stack.24.refs_1_), channel_id=1, source_target_pairs={{0,2},{2,0},{1,3},{3,1},{4,6},{6,4},{5,7},{7,5},{8,10},{10,8},{9,1... | collective-permute-start | bytes 786440 | tf_op jit(solution)/shard_map/ppermute | solution.py:561
  35.9 1.5 collective-permute-start.5
  43.0 127.0 %reduce-scatter.2.cloned.1.call-start = ((), (), s32[]{:S(2)}) async-start(), calls=%async_computation.1 | async-start | bytes 5013504 | tf_op jit(solution)/shard_map/reduce_scatter | solution.py:781
  58.8 17.8 %collective-permute-start.8 = (bf16[128,2176]{1,0:T(8,128)(2,1)}, bf16[128,2176]{1,0:T(8,128)(2,1)S(1)}, u32[]{:S(2)}, u32[]{:S(2)}) collective-permute-start(bf16[128,2176]{1,0:T(8,128)(2,1)} %get-tuple-element.82), channel_id=1, source_target_pairs={{0,1},{1,0},{4,5},{5,4},{2,3},{3,2},{6,7},{7,6},{8,9},{9,8},{12,13... | collective-permute-start | bytes 1671176 | tf_op jit(solution)/shard_map/ppermute | solution.py:567
  60.5 19.7 %collective-permute-start.9 = (bf16[128,2176]{1,0:T(8,128)(2,1)}, bf16[128,2176]{1,0:T(8,128)(2,1)}, u32[]{:S(2)}, u32[]{:S(2)}) collective-permute-start(bf16[128,2176]{1,0:T(8,128)(2,1)} %get-tuple-element.83), channel_id=1, source_target_pairs={{0,4},{1,5},{4,0},{5,1},{2,6},{3,7},{6,2},{7,3},{8,12},{9,13},{12,... | collective-permute-start | bytes 1671176 | tf_op jit(solution)/shard_map/ppermute | solution.py:567
  61.8 40.6 %collective-permute-start.14 = (bf16[128,2176]{1,0:T(8,128)(2,1)}, bf16[128,2176]{1,0:T(8,128)(2,1)}, u32[]{:S(2)}, u32[]{:S(2)}) collective-permute-start(bf16[128,2176]{1,0:T(8,128)(2,1)} %get-tuple-element.95), channel_id=1, source_target_pairs={{0,5},{1,4},{4,1},{5,0},{2,7},{3,6},{6,3},{7,2},{8,13},{9,12},{12,... | collective-permute-start | bytes 1671176 | tf_op jit(solution)/shard_map/ppermute | solution.py:567
  62.4 40.1 %copy-start.1 = (bf16[8,1024,128]{2,1,0:T(8,128)(2,1)S(1)}, bf16[8,1024,128]{2,1,0:T(8,128)(2,1)}, u32[]{:S(2)}) copy-start(bf16[8,1024,128]{2,1,0:T(8,128)(2,1)} %all-gather.5.cloned.1.call-done) | copy-start | bytes 6291460
  67.2 13.0 %collective-permute-start.6 = (bf16[4,128,256]{2,1,0:T(8,128)(2,1)}, bf16[4,128,256]{2,1,0:T(8,128)(2,1)S(1)}, u32[]{:S(2)}, u32[]{:S(2)}) collective-permute-start(bf16[4,128,256]{2,1,0:T(8,128)(2,1)} %get-tuple-element.80), channel_id=1, source_target_pairs={{0,2},{2,0},{1,3},{3,1},{4,6},{6,4},{5,7},{7,5},{8,10},{10,8},{9,1... | collective-permute-start | bytes 786440 | tf_op jit(solution)/shard_map/ppermute | solution.py:561
  67.2 13.0 %collective-permute-start.7 = (bf16[4,128,256]{2,1,0:T(8,128)(2,1)}, bf16[4,128,256]{2,1,0:T(8,128)(2,1)S(1)}, u32[]{:S(2)}, u32[]{:S(2)}) collective-permute-start(bf16[4,128,256]{2,1,0:T(8,128)(2,1)} %get-tuple-element.81), channel_id=1, source_target_pairs={{0,2},{2,0},{1,3},{3,1},{4,6},{6,4},{5,7},{7,5},{8,10},{10,8},{9,1... | collective-permute-start | bytes 786440 | tf_op jit(solution)/shard_map/ppermute | solution.py:561
  82.9 8.6 %collective-permute-start.10 = (bf16[2,128,256]{2,1,0:T(8,128)(2,1)S(1)}, bf16[2,128,256]{2,1,0:T(8,128)(2,1)S(1)}, u32[]{:S(2)}, u32[]{:S(2)}) collective-permute-start(bf16[2,128,256]{2,1,0:T(8,128)(2,1)S(1)} %get-tuple-element.88), channel_id=1, source_target_pairs={{8,0},{16,8},{24,16},{9,1},{17,9},{25,17},{10,2},{18,10},{26,18},{... | collective-permute-start | bytes 393224 | tf_op jit(solution)/shard_map/ppermute | solution.py:763
  84.2 14.2 %collective-permute-start.11 = (bf16[2,128,256]{2,1,0:T(8,128)(2,1)S(1)}, bf16[2,128,256]{2,1,0:T(8,128)(2,1)S(1)}, u32[]{:S(2)}, u32[]{:S(2)}) collective-permute-start(bf16[2,128,256]{2,1,0:T(8,128)(2,1)S(1)} %get-tuple-element.89), channel_id=1, source_target_pairs={{16,0},{24,8},{17,1},{25,9},{18,2},{26,10},{19,3},{27,11},{20,4},{... | collective-permute-start | bytes 393224 | tf_op jit(solution)/shard_map/ppermute | solution.py:763
  85.5 16.8 %collective-permute-start.12 = (bf16[2,128,256]{2,1,0:T(8,128)(2,1)S(1)}, bf16[2,128,256]{2,1,0:T(8,128)(2,1)S(1)}, u32[]{:S(2)}, u32[]{:S(2)}) collective-permute-start(bf16[2,128,256]{2,1,0:T(8,128)(2,1)S(1)} %get-tuple-element.90), channel_id=1, source_target_pairs={{24,0},{25,1},{26,2},{27,3},{28,4},{29,5},{30,6},{31,7}} | collective-permute-start | bytes 393224 | tf_op jit(solution)/shard_map/ppermute | solution.py:763
  111.8 27.3 %copy-start.16 = (s32[16]{0:T(128)S(1)}, s32[16]{0:T(128)}, u32[]{:S(2)}) copy-start(s32[16]{0:T(128)} %copy-done.14) | copy-start | bytes 196
  111.8 4.3 %collective-permute-start.13 = (bf16[128,256]{1,0:T(8,128)(2,1)S(1)}, bf16[128,256]{1,0:T(8,128)(2,1)S(1)}, u32[]{:S(2)}, u32[]{:S(2)}) collective-permute-start(bf16[128,256]{1,0:T(8,128)(2,1)S(1)} %get-tuple-element.92), channel_id=1, source_target_pairs={{0,4},{4,0},{1,5},{5,1},{2,6},{6,2},{3,7},{7,3},{8,12},{12,8},{9,1... | collective-permute-start | bytes 196616 | tf_op jit(solution)/shard_map/ppermute | solution.py:561
  120.8 12.9 %collective-permute-start.15 = (bf16[128,1664]{1,0:T(8,128)(2,1)}, bf16[128,1664]{1,0:T(8,128)(2,1)S(1)}, u32[]{:S(2)}, u32[]{:S(2)}) collective-permute-start(bf16[128,1664]{1,0:T(8,128)(2,1)} %get-tuple-element.98), channel_id=1, source_target_pairs={{0,1},{1,0},{4,5},{5,4},{2,3},{3,2},{6,7},{7,6},{8,9},{9,8},{12,13... | collective-permute-start | bytes 1277960 | tf_op jit(solution)/shard_map/ppermute | solution.py:567
  122.3 12.4 %collective-permute-start.16 = (bf16[128,1664]{1,0:T(8,128)(2,1)}, bf16[128,1664]{1,0:T(8,128)(2,1)S(1)}, u32[]{:S(2)}, u32[]{:S(2)}) collective-permute-start(bf16[128,1664]{1,0:T(8,128)(2,1)} %get-tuple-element.99), channel_id=1, source_target_pairs={{0,4},{1,5},{4,0},{5,1},{2,6},{3,7},{6,2},{7,3},{8,12},{9,13},{12,... | collective-permute-start | bytes 1277960 | tf_op jit(solution)/shard_map/ppermute | solution.py:567
  122.4 16.7 %collective-permute-start.17 = (bf16[128,1664]{1,0:T(8,128)(2,1)}, bf16[128,1664]{1,0:T(8,128)(2,1)S(1)}, u32[]{:S(2)}, u32[]{:S(2)}) collective-permute-start(bf16[128,1664]{1,0:T(8,128)(2,1)} %get-tuple-element.100), channel_id=1, source_target_pairs={{0,5},{1,4},{4,1},{5,0},{2,7},{3,6},{6,3},{7,2},{8,13},{9,12},{12,... | collective-permute-start | bytes 1277960 | tf_op jit(solution)/shard_map/ppermute | solution.py:567
  143.6 2.4 %collective-permute-start.18 = (bf16[4,128,768]{2,1,0:T(8,128)(2,1)S(1)}, bf16[4,128,768]{2,1,0:T(8,128)(2,1)S(1)}, u32[]{:S(2)}, u32[]{:S(2)}) collective-permute-start(bf16[4,128,768]{2,1,0:T(8,128)(2,1)S(1)} %get-tuple-element.103), channel_id=1, source_target_pairs={{0,2},{2,0},{1,3},{3,1},{4,6},{6,4},{5,7},{7,5},{8,10},{10,8},{9,1... | collective-permute-start | bytes 2359304 | tf_op jit(solution)/shard_map/ppermute | solution.py:561
  146.7 19.7 %collective-permute-start.19 = (bf16[2,128,768]{2,1,0:T(8,128)(2,1)S(1)}, bf16[2,128,768]{2,1,0:T(8,128)(2,1)S(1)}, u32[]{:S(2)}, u32[]{:S(2)}) collective-permute-start(bf16[2,128,768]{2,1,0:T(8,128)(2,1)S(1)} %get-tuple-element.105), channel_id=1, source_target_pairs={{0,8},{8,0},{16,24},{24,16},{1,9},{9,1},{17,25},{25,17},{2,10},{10... | collective-permute-start | bytes 1179656 | tf_op jit(solution)/shard_map/ppermute | solution.py:805
  171.7 14.7 %collective-permute-start.26 = (bf16[64,2176]{1,0:T(8,128)(2,1)S(1)}, bf16[64,2176]{1,0:T(8,128)(2,1)S(1)}, u32[]{:S(2)}, u32[]{:S(2)}) collective-permute-start(bf16[64,2176]{1,0:T(8,128)(2,1)S(1)} %get-tuple-element.111), channel_id=1, source_target_pairs={{0,5},{1,4},{4,1},{5,0},{2,7},{3,6},{6,3},{7,2},{8,13},{9,12},{12,... | collective-permute-start | bytes 835592 | tf_op jit(solution)/shard_map/ppermute | solution.py:567
  174.2 9.6 %collective-permute-start.20 = (bf16[1,128,768]{2,1,0:T(8,128)(2,1)S(1)}, bf16[1,128,768]{2,1,0:T(8,128)(2,1)S(1)}, u32[]{:S(2)}, u32[]{:S(2)}) collective-permute-start(bf16[1,128,768]{2,1,0:T(8,128)(2,1)S(1)} %get-tuple-element.107), channel_id=1, source_target_pairs={{0,16},{8,24},{16,0},{24,8},{1,17},{9,25},{17,1},{25,9},{2,18},{10... | collective-permute-start | bytes 589832 | tf_op jit(solution)/shard_map/ppermute | solution.py:805
  174.2 13.8 %collective-permute-start.25 = (bf16[64,2176]{1,0:T(8,128)(2,1)S(1)}, bf16[64,2176]{1,0:T(8,128)(2,1)S(1)}, u32[]{:S(2)}, u32[]{:S(2)}) collective-permute-start(bf16[64,2176]{1,0:T(8,128)(2,1)S(1)} %get-tuple-element.111), channel_id=1, source_target_pairs={{0,4},{1,5},{4,0},{5,1},{2,6},{3,7},{6,2},{7,3},{8,12},{9,13},{12,... | collective-permute-start | bytes 835592 | tf_op jit(solution)/shard_map/ppermute | solution.py:567
  174.8 13.2 %collective-permute-start.24 = (bf16[64,2176]{1,0:T(8,128)(2,1)S(1)}, bf16[64,2176]{1,0:T(8,128)(2,1)S(1)}, u32[]{:S(2)}, u32[]{:S(2)}) collective-permute-start(bf16[64,2176]{1,0:T(8,128)(2,1)S(1)} %get-tuple-element.108.refs_3_.refs_1_), channel_id=1, source_target_pairs={{0,1},{1,0},{4,5},{5,4},{2,3},{3,2},{6,7},{7,6},{8,9},{9,8},{12,13... | collective-permute-start | bytes 835592 | tf_op jit(solution)/shard_map/ppermute | solution.py:567
  184.4 6.6 %collective-permute-start.23 = (bf16[64,768]{1,0:T(8,128)(2,1)S(1)}, bf16[64,768]{1,0:T(8,128)(2,1)S(1)}, u32[]{:S(2)}, u32[]{:S(2)}) collective-permute-start(bf16[64,768]{1,0:T(8,128)(2,1)S(1)} %get-tuple-element.110), channel_id=1, source_target_pairs={{0,5},{1,4},{4,1},{5,0},{2,7},{3,6},{6,3},{7,2},{8,13},{9,12},{12,... | collective-permute-start | bytes 294920 | tf_op jit(solution)/shard_map/ppermute | solution.py:567
  184.8 6.4 %collective-permute-start.22 = (bf16[64,768]{1,0:T(8,128)(2,1)S(1)}, bf16[64,768]{1,0:T(8,128)(2,1)S(1)}, u32[]{:S(2)}, u32[]{:S(2)}) collective-permute-start(bf16[64,768]{1,0:T(8,128)(2,1)S(1)} %get-tuple-element.110), channel_id=1, source_target_pairs={{0,4},{1,5},{4,0},{5,1},{2,6},{3,7},{6,2},{7,3},{8,12},{9,13},{12,... | collective-permute-start | bytes 294920 | tf_op jit(solution)/shard_map/ppermute | solution.py:567
  186.5 5.7 %collective-permute-start.21 = (bf16[64,768]{1,0:T(8,128)(2,1)S(1)}, bf16[64,768]{1,0:T(8,128)(2,1)S(1)}, u32[]{:S(2)}, u32[]{:S(2)}) collective-permute-start(bf16[64,768]{1,0:T(8,128)(2,1)S(1)} %get-tuple-element.109.refs_5_.refs_1_), channel_id=1, source_target_pairs={{0,1},{1,0},{4,5},{5,4},{2,3},{3,2},{6,7},{7,6},{8,9},{9,8},{12,13... | collective-permute-start | bytes 294920 | tf_op jit(solution)/shard_map/ppermute | solution.py:567
  (20 other events, 91.4 us)
Sparse Core Ops, SparseCore 0:
  11.7 40.5 all-gather.4
  54.1 35.2 all-gather.6
  111.9 58.0 reduce-scatter.1

commit v5 on v4

--- a/solution.py
+++ b/solution.py
@@ -513,7 +513,7 @@
             pltpu.SemaphoreType.DMA((len(lefts) + moves, FOUR)),
         ],
         after,
-        14,
+        14 if nz else 60,
     )
 
 

time: 201 us -> 200 us (level)
  local copies, waits for them, and re-layouts: 15.3 us -> 9.96 us
  Pallas kernels: 49.2 us -> 51.8 us
    unnamed x44 -> x40, local copies, waits for them, and re-layouts: 14 us -> 8.7 us
    pallas_call x17, Pallas kernels: 49.2 us -> 51.8 us  [call(): pl.pallas_call(body, out_shape=tuple(outs), in_specs=list(specs) + [ANY]...]
where the time goes in v5:
time: 200 us
  waiting for transfers between devices  92.5 us (46%)
  Pallas kernels  51.8 us (26%)
  starting transfers between devices  31.2 us (16%)
  between operations  14.1 us (7%)
  local copies, waits for them, and re-layouts  9.96 us (5%)
    pallas_call x17, Pallas kernels, call(): pl.pallas_call(body, out_shape=tuple(outs), in_specs=list(specs) + [ANY]...  51.8 us
    ppermute x12, waiting for transfers between devices, plane_swap(): lax.ppermute(parts[k], PLANE, [(d, d ^ k) for d in range(FOUR)])  29.2 us
    ppermute x2, waiting for transfers between devices, shards(): came = lax.ppermute(send, 'z', [(i, i ^ 1 << step) for i in range(nz)])  28.3 us
    ppermute x7, waiting for transfers between devices, swap(): return lax.ppermute(value, axis, [(0, 1), (1, 0)])  16.9 us
    ppermute x12, starting transfers between devices, plane_swap(): lax.ppermute(parts[k], PLANE, [(d, d ^ k) for d in range(FOUR)])  14.1 us
    ppermute x3, waiting for transfers between devices, shards(): moved[k] = lax.ppermute(moved[k], 'z', [(i, i - k) for i in range(k, nz)])  13.8 us
    ppermute x3, starting transfers between devices, shards(): moved.append(lax.ppermute(kv, 'z', [(i, i + k) for i in range(nz - k)]))  10.7 us
    unnamed x40, local copies, waits for them, and re-layouts  8.7 us
  transfers between devices with their start and end apart: 30, of which 19 were waited for; matrix products, arithmetic and copies ran while one was open for 0% of the time, Pallas kernels for 19%

profile of v5, /device:TPU:0, one launch (start us, length us, event | category | flops | bytes accessed | tf_op | source)
XLA Modules:
  0.0 199.5 jit_solution(644504479859840803)
XLA Ops:
  7.2 4.4 %enter.1 = (bf16[128,512]{1,0:T(8,128)(2,1)}, bf16[128,256]{1,0:T(8,128)(2,1)}, bf16[2,1024,128]{2,1,0:T(8,128)(2,1)}, bf16[2,128,1024]{2,1,0:T(8,128)(2,1)}) custom-call(bf16[128,1024]{1,0:T(8,128)(2,1)} %bitcast.25, bf16[1024]{0:T(1024)(128)(2,1)} %refs_3_.3, bf16[1024,512]{1,0:T(8,128)(2,1)} %refs_9_.1, bf16[256,256]{1,0:T(8,128)(2,1)} %refs_8_.5, ...), custom_call_target="tpu_custom_call" | custom-call | bytes 36000 | tf_op jit(solution)/shard_map/enter/pallas_call | solution.py:71
  11.7 7.0 %collective-permute-start.2 = (bf16[128,256]{1,0:T(8,128)(2,1)}, bf16[128,256]{1,0:T(8,128)(2,1)S(1)}, u32[]{:S(2)}, u32[]{:S(2)}) collective-permute-start(bf16[128,256]{1,0:T(8,128)(2,1)} %get-tuple-element.66.refs_0_), channel_id=1, source_target_pairs={{0,24},{1,25},{2,26},{3,27},{4,28},{5,29},{6,30},{7,31}} | collective-permute-start | bytes 196616 | tf_op jit(solution)/shard_map/ppermute | solution.py:735
  19.9 2.5 %collective-permute-start = (bf16[128,256]{1,0:T(8,128)(2,1)}, bf16[128,256]{1,0:T(8,128)(2,1)S(1)}, u32[]{:S(2)}, u32[]{:S(2)}) collective-permute-start(bf16[128,256]{1,0:T(8,128)(2,1)} %get-tuple-element.66.refs_0_), channel_id=1, source_target_pairs={{0,8},{8,16},{16,24},{1,9},{9,17},{17,25},{2,10},{10,18},{18,26},{... | collective-permute-start | bytes 196616 | tf_op jit(solution)/shard_map/ppermute | solution.py:735
  23.2 1.4 collective-permute-done.refs_1_
  25.5 1.6 collective-permute-start.3
  27.1 8.9 %collective-permute-done.3.refs_2_ = bf16[4,128,256]{2,1,0:T(8,128)(2,1)S(1)} collective-permute-done((bf16[4,128,256]{2,1,0:T(8,128)(2,1)S(1)}, bf16[4,128,256]{2,1,0:T(8,128)(2,1)S(1)}, u32[]{:S(2)}, u32[]{:S(2)}) %collective-permute-start.3) | collective-permute-done | bytes 262176 | tf_op jit(solution)/shard_map/ppermute | solution.py:561
  35.9 1.5 collective-permute-done.5.refs_4_
  38.2 4.9 %attend.1 = (bf16[2048,256]{1,0:T(8,128)(2,1)}, f32[2,64,1024]{2,1,0:T(8,128)}, f32[2,1,1024]{2,1,0:T(1,128)}, bf16[1024,128]{1,0:T(8,128)(2,1)}, bf16[1024,128]...) custom-call(s32[16]{0:T(128)} %copy-done.12, bf16[4,128,256]{2,1,0:T(8,128)(2,1)} %copy-done.5, ...), custom_call_target="tpu_custom_call" | custom-call | bytes 36000 | tf_op jit(solution)/shard_map/attend/pallas_call | solution.py:71
  43.1 15.7 %feed.1 = (bf16[128,2176]{1,0:T(8,128)(2,1)}, bf16[128,2176]{1,0:T(8,128)(2,1)}, bf16[128,2176]{1,0:T(8,128)(2,1)}, bf16[128,2176]{1,0:T(8,128)(2,1)}, bf16[128,...) custom-call(s32[16]{0:T(128)} %copy-done.12, ...), custom_call_target="tpu_custom_call" | custom-call | bytes 36000 | tf_op jit(solution)/shard_map/feed/pallas_call | solution.py:71
  58.9 1.7 collective-permute-start.8
  62.4 4.6 %attend_back.1 = (bf16[128,1024]{1,0:T(8,128)(2,1)}, bf16[4,128,256]{2,1,0:T(8,128)(2,1)}, bf16[4,128,256]{2,1,0:T(8,128)(2,1)}, bf16[4,128,256]{2,1,0:T(8,128)(2,1)}, bf16[4,128,256]{2,1,0:T(8,128)(2,1)}) custom-call(s32[16]{0:T(128)} %copy-done.12, bf16[2048,256]{1,0:T(8,128)(2,1)} %get-tuple-element.72.refs_1_, ...), custom_call_target="tpu_custom_call" | custom-call | bytes 32400000 | tf_op jit(solution)/shard_map/attend_back/pallas_call | solution.py:71
  67.5 9.2 %collective-permute-done.8.refs_5_.refs_4_ = bf16[128,2176]{1,0:T(8,128)(2,1)S(1)} collective-permute-done((bf16[128,2176]{1,0:T(8,128)(2,1)}, bf16[128,2176]{1,0:T(8,128)(2,1)S(1)}, u32[]{:S(2)}, u32[]{:S(2)}) %collective-permute-start.8) | collective-permute-done | bytes 557088 | tf_op jit(solution)/shard_map/ppermute | solution.py:567
  76.7 3.5 %collective-permute-done.9.refs_6_.refs_5_ = bf16[128,2176]{1,0:T(8,128)(2,1)} collective-permute-done((bf16[128,2176]{1,0:T(8,128)(2,1)}, bf16[128,2176]{1,0:T(8,128)(2,1)}, u32[]{:S(2)}, u32[]{:S(2)}) %collective-permute-start.9) | collective-permute-done | bytes 557088 | tf_op jit(solution)/shard_map/ppermute | solution.py:567
  88.6 2.9 %collective-permute-done.10.refs_1_ = bf16[2,128,256]{2,1,0:T(8,128)(2,1)S(1)} collective-permute-done((bf16[2,128,256]{2,1,0:T(8,128)(2,1)S(1)}, bf16[2,128,256]{2,1,0:T(8,128)(2,1)S(1)}, u32[]{:S(2)}, u32[]{:S(2)}) %collective-permute-start.10) | collective-permute-done | bytes 131104 | tf_op jit(solution)/shard_map/ppermute | solution.py:763
  91.5 6.9 %collective-permute-done.11.refs_2_ = bf16[2,128,256]{2,1,0:T(8,128)(2,1)S(1)} collective-permute-done((bf16[2,128,256]{2,1,0:T(8,128)(2,1)S(1)}, bf16[2,128,256]{2,1,0:T(8,128)(2,1)S(1)}, u32[]{:S(2)}, u32[]{:S(2)}) %collective-permute-start.11) | collective-permute-done | bytes 131104 | tf_op jit(solution)/shard_map/ppermute | solution.py:763
  98.4 3.9 %collective-permute-done.12.refs_3_ = bf16[2,128,256]{2,1,0:T(8,128)(2,1)S(1)} collective-permute-done((bf16[2,128,256]{2,1,0:T(8,128)(2,1)S(1)}, bf16[2,128,256]{2,1,0:T(8,128)(2,1)S(1)}, u32[]{:S(2)}, u32[]{:S(2)}) %collective-permute-start.12) | collective-permute-done | bytes 131104 | tf_op jit(solution)/shard_map/ppermute | solution.py:763
  103.1 7.6 %weight_terms.2.refs_13_ = bf16[1024,2176]{1,0:T(8,128)(2,1)} custom-call(s32[16]{0:T(128)} %copy-done.12, bf16[4,1024,128]{2,1,0:T(8,128)(2,1)} %bitcast.30, bf16[4,2,1024,128]{3,2,1,0:T(8,128)(2,1)} %bitcast.21, bf16[128,2176]{1,0:T(8,128)(2,1)} %get-tuple-element.94.refs_3_, bf16[128,2176]{1,0:T(8,128)(2,1)} %copy-done.3, ...), custom_call_target="tpu_custom_call" | custom-call | bytes 36000 | tf_op jit(solution)/shard_map/weight_terms/pallas_call | solution.py:71
  110.8 4.3 %collective-permute-done.13.refs_12_ = bf16[128,256]{1,0:T(8,128)(2,1)S(1)} collective-permute-done((bf16[128,256]{1,0:T(8,128)(2,1)S(1)}, bf16[128,256]{1,0:T(8,128)(2,1)S(1)}, u32[]{:S(2)}, u32[]{:S(2)}) %collective-permute-start.13) | collective-permute-done | bytes 65568 | tf_op jit(solution)/shard_map/ppermute | solution.py:561
  115.7 4.1 %leave.1 = (bf16[128,1024]{1,0:T(8,128)(2,1)}, bf16[1024,128]{1,0:T(8,128)(2,1)}, bf16[128,1664]{1,0:T(8,128)(2,1)}, bf16[128,1664]{1,0:T(8,128)(2,1)}, bf16[128...) custom-call(s32[16]{0:T(128)} %copy-done.12, bf16[128,1024]{1,0:T(8,128)(2,1)} %bitcast.27, ...), custom_call_target="tpu_custom_call" | custom-call | bytes 36000 | tf_op jit(solution)/shard_map/leave/pallas_call | solution.py:71
  121.2 2.1 %collective-permute-start.17 = (bf16[128,1664]{1,0:T(8,128)(2,1)}, bf16[128,1664]{1,0:T(8,128)(2,1)S(1)}, u32[]{:S(2)}, u32[]{:S(2)}) collective-permute-start(bf16[128,1664]{1,0:T(8,128)(2,1)} %get-tuple-element.100), channel_id=1, source_target_pairs={{0,5},{1,4},{4,1},{5,0},{2,7},{3,6},{6,3},{7,2},{8,13},{9,12},{12,... | collective-permute-start | bytes 1277960 | tf_op jit(solution)/shard_map/ppermute | solution.py:567
  123.3 9.4 %collective-permute-done.15.refs_3_ = bf16[128,1664]{1,0:T(8,128)(2,1)S(1)} collective-permute-done((bf16[128,1664]{1,0:T(8,128)(2,1)}, bf16[128,1664]{1,0:T(8,128)(2,1)S(1)}, u32[]{:S(2)}, u32[]{:S(2)}) %collective-permute-start.15) | collective-permute-done | bytes 426016 | tf_op jit(solution)/shard_map/ppermute | solution.py:567
  133.4 4.4 %collective-permute-done.17.refs_5_ = bf16[128,1664]{1,0:T(8,128)(2,1)S(1)} collective-permute-done((bf16[128,1664]{1,0:T(8,128)(2,1)}, bf16[128,1664]{1,0:T(8,128)(2,1)S(1)}, u32[]{:S(2)}, u32[]{:S(2)}) %collective-permute-start.17) | collective-permute-done | bytes 426016 | tf_op jit(solution)/shard_map/ppermute | solution.py:567
  139.8 2.6 %weight_terms.3 = (bf16[4,128,768]{2,1,0:T(8,128)(2,1)S(1)}, bf16[4,128,768]{2,1,0:T(8,128)(2,1)S(1)}) custom-call(s32[16]{0:T(128)S(1)} %copy-done.14, bf16[4,2,1024,128]{3,2,1,0:T(8,128)(2,1)S(1)} %bitcast.22, bf16[128,1664]{1,0:T(8,128)(2,1)S(1)} %copy-done.8, bf16[128,1664]{1,0:T(8,128)(2,1)S(1)} %collective-permute-done.15.refs_3_, ...), custom_call_target="tpu_custom_call" | custom-call | bytes 36000 | tf_op jit(solution)/shard_map/weight_terms/pallas_call | solution.py:71
  142.5 2.3 %collective-permute-done.18.refs_2_ = bf16[4,128,768]{2,1,0:T(8,128)(2,1)S(1)} collective-permute-done((bf16[4,128,768]{2,1,0:T(8,128)(2,1)S(1)}, bf16[4,128,768]{2,1,0:T(8,128)(2,1)S(1)}, u32[]{:S(2)}, u32[]{:S(2)}) %collective-permute-start.18) | collective-permute-done | bytes 786464 | tf_op jit(solution)/shard_map/ppermute | solution.py:561
  145.6 19.8 %collective-permute-done.19.refs_2_ = bf16[2,128,768]{2,1,0:T(8,128)(2,1)S(1)} collective-permute-done((bf16[2,128,768]{2,1,0:T(8,128)(2,1)S(1)}, bf16[2,128,768]{2,1,0:T(8,128)(2,1)S(1)}, u32[]{:S(2)}, u32[]{:S(2)}) %collective-permute-start.19) | collective-permute-done | bytes 393248 | tf_op jit(solution)/shard_map/ppermute | solution.py:805
  166.0 2.9 %reduce-scatter.2.cloned.1.call-done.refs_1_ = bf16[128,2176]{1,0:T(8,128)(2,1)} async-done(((bf16[1024,2176]{1,0:T(8,128)(2,1)}), bf16[128,2176]{1,0:T(8,128)(2,1)}) %reduce-scatter.2.cloned.1.call-update) | async-done | bytes 557072 | tf_op jit(solution)/shard_map/reduce_scatter | solution.py:781
  170.6 2.4 %collective-permute-start.26 = (bf16[64,2176]{1,0:T(8,128)(2,1)S(1)}, bf16[64,2176]{1,0:T(8,128)(2,1)S(1)}, u32[]{:S(2)}, u32[]{:S(2)}) collective-permute-start(bf16[64,2176]{1,0:T(8,128)(2,1)S(1)} %get-tuple-element.111), channel_id=1, source_target_pairs={{0,5},{1,4},{4,1},{5,0},{2,7},{3,6},{6,3},{7,2},{8,13},{9,12},{12,... | collective-permute-start | bytes 835592 | tf_op jit(solution)/shard_map/ppermute | solution.py:567
  174.2 8.5 %collective-permute-done.20 = bf16[1,128,768]{2,1,0:T(8,128)(2,1)S(1)} collective-permute-done((bf16[1,128,768]{2,1,0:T(8,128)(2,1)S(1)}, bf16[1,128,768]{2,1,0:T(8,128)(2,1)S(1)}, u32[]{:S(2)}, u32[]{:S(2)}) %collective-permute-start.20) | collective-permute-done | bytes 196640 | tf_op jit(solution)/shard_map/ppermute | solution.py:805
  183.7 1.7 collective-permute-start.22
  185.4 1.5 collective-permute-start.21
  186.8 2.1 %put.2 = (f32[64,2816]{1,0:T(8,128)}, f32[64,2816]{1,0:T(8,128)}, f32[64,2816]{1,0:T(8,128)}, f32[8,128]{1,0:T(8,128)S(1)}) custom-call(s32[16]{0:T(128)S(1)} %copy-done.14, bf16[64,2176]{1,0:T(8,128)(2,1)S(1)} %get-tuple-element.108.refs_3_.refs_1_, bf16[64,2176]{1,0:T(8,128)(2,1)S(1)} %collective-permute-done.24.refs_2_, ...), custom_call_target="tpu_custom_call" | custom-call | bytes 36000 | tf_op jit(solution)/shard_map/put/pallas_call | solution.py:71
  191.1 1.4 put.3
  (90 shorter events, 28.0 us)
Async XLA Ops:
  7.2 55.2 %all-gather.5.cloned.1.call-start = ((), (), s32[]{:S(2)}) async-start(), calls=%async_computation.2 | async-start | bytes 2621440 | tf_op jit(solution)/shard_map/all_gather | solution.py:730
  11.6 91.4 %all-gather.7.cloned.1.call-start = ((), (), s32[]{:S(2)}) async-start(), calls=%async_computation.3 | async-start | bytes 1310720 | tf_op jit(solution)/shard_map/all_gather | solution.py:746
  11.7 11.5 %collective-permute-start.2 = (bf16[128,256]{1,0:T(8,128)(2,1)}, bf16[128,256]{1,0:T(8,128)(2,1)S(1)}, u32[]{:S(2)}, u32[]{:S(2)}) collective-permute-start(bf16[128,256]{1,0:T(8,128)(2,1)} %get-tuple-element.66.refs_0_), channel_id=1, source_target_pairs={{0,24},{1,25},{2,26},{3,27},{4,28},{5,29},{6,30},{7,31}} | collective-permute-start | bytes 196616 | tf_op jit(solution)/shard_map/ppermute | solution.py:735
  18.6 4.5 %collective-permute-start.1 = (bf16[128,256]{1,0:T(8,128)(2,1)}, bf16[128,256]{1,0:T(8,128)(2,1)S(1)}, u32[]{:S(2)}, u32[]{:S(2)}) collective-permute-start(bf16[128,256]{1,0:T(8,128)(2,1)} %get-tuple-element.66.refs_0_), channel_id=1, source_target_pairs={{0,16},{8,24},{1,17},{9,25},{2,18},{10,26},{3,19},{11,27},{4,20},{... | collective-permute-start | bytes 196616 | tf_op jit(solution)/shard_map/ppermute | solution.py:735
  19.9 4.7 %collective-permute-start = (bf16[128,256]{1,0:T(8,128)(2,1)}, bf16[128,256]{1,0:T(8,128)(2,1)S(1)}, u32[]{:S(2)}, u32[]{:S(2)}) collective-permute-start(bf16[128,256]{1,0:T(8,128)(2,1)} %get-tuple-element.66.refs_0_), channel_id=1, source_target_pairs={{0,8},{8,16},{16,24},{1,9},{9,17},{17,25},{2,10},{10,18},{18,26},{... | collective-permute-start | bytes 196616 | tf_op jit(solution)/shard_map/ppermute | solution.py:735
  25.5 10.4 %collective-permute-start.3 = (bf16[4,128,256]{2,1,0:T(8,128)(2,1)S(1)}, bf16[4,128,256]{2,1,0:T(8,128)(2,1)S(1)}, u32[]{:S(2)}, u32[]{:S(2)}) collective-permute-start(bf16[4,128,256]{2,1,0:T(8,128)(2,1)S(1)} %stack.24.refs_1_), channel_id=1, source_target_pairs={{0,4},{4,0},{1,5},{5,1},{2,6},{6,2},{3,7},{7,3},{8,12},{12,8},{9,1... | collective-permute-start | bytes 786440 | tf_op jit(solution)/shard_map/ppermute | solution.py:561
  27.0 8.9 %collective-permute-start.4 = (bf16[4,128,256]{2,1,0:T(8,128)(2,1)S(1)}, bf16[4,128,256]{2,1,0:T(8,128)(2,1)S(1)}, u32[]{:S(2)}, u32[]{:S(2)}) collective-permute-start(bf16[4,128,256]{2,1,0:T(8,128)(2,1)S(1)} %stack.24.refs_1_), channel_id=1, source_target_pairs={{0,2},{2,0},{1,3},{3,1},{4,6},{6,4},{5,7},{7,5},{8,10},{10,8},{9,1... | collective-permute-start | bytes 786440 | tf_op jit(solution)/shard_map/ppermute | solution.py:561
  35.9 1.5 collective-permute-start.5
  43.0 125.8 %reduce-scatter.2.cloned.1.call-start = ((), (), s32[]{:S(2)}) async-start(), calls=%async_computation.1 | async-start | bytes 5013504 | tf_op jit(solution)/shard_map/reduce_scatter | solution.py:781
  58.9 27.9 %copy-start.1 = (bf16[1024,1024]{1,0:T(8,128)(2,1)S(1)}, bf16[1024,1024]{1,0:T(8,128)(2,1)}, u32[]{:S(2)}) copy-start(bf16[1024,1024]{1,0:T(8,128)(2,1)} %refs_1_.3) | copy-start | bytes 6291460
  58.9 17.8 %collective-permute-start.8 = (bf16[128,2176]{1,0:T(8,128)(2,1)}, bf16[128,2176]{1,0:T(8,128)(2,1)S(1)}, u32[]{:S(2)}, u32[]{:S(2)}) collective-permute-start(bf16[128,2176]{1,0:T(8,128)(2,1)} %get-tuple-element.82), channel_id=1, source_target_pairs={{0,1},{1,0},{4,5},{5,4},{2,3},{3,2},{6,7},{7,6},{8,9},{9,8},{12,13... | collective-permute-start | bytes 1671176 | tf_op jit(solution)/shard_map/ppermute | solution.py:567
  60.5 19.7 %collective-permute-start.9 = (bf16[128,2176]{1,0:T(8,128)(2,1)}, bf16[128,2176]{1,0:T(8,128)(2,1)}, u32[]{:S(2)}, u32[]{:S(2)}) collective-permute-start(bf16[128,2176]{1,0:T(8,128)(2,1)} %get-tuple-element.83), channel_id=1, source_target_pairs={{0,4},{1,5},{4,0},{5,1},{2,6},{3,7},{6,2},{7,3},{8,12},{9,13},{12,... | collective-permute-start | bytes 1671176 | tf_op jit(solution)/shard_map/ppermute | solution.py:567
  61.9 41.2 %collective-permute-start.14 = (bf16[128,2176]{1,0:T(8,128)(2,1)}, bf16[128,2176]{1,0:T(8,128)(2,1)}, u32[]{:S(2)}, u32[]{:S(2)}) collective-permute-start(bf16[128,2176]{1,0:T(8,128)(2,1)} %get-tuple-element.95), channel_id=1, source_target_pairs={{0,5},{1,4},{4,1},{5,0},{2,7},{3,6},{6,3},{7,2},{8,13},{9,12},{12,... | collective-permute-start | bytes 1671176 | tf_op jit(solution)/shard_map/ppermute | solution.py:567
  67.0 13.2 %collective-permute-start.6 = (bf16[4,128,256]{2,1,0:T(8,128)(2,1)}, bf16[4,128,256]{2,1,0:T(8,128)(2,1)S(1)}, u32[]{:S(2)}, u32[]{:S(2)}) collective-permute-start(bf16[4,128,256]{2,1,0:T(8,128)(2,1)} %get-tuple-element.80), channel_id=1, source_target_pairs={{0,2},{2,0},{1,3},{3,1},{4,6},{6,4},{5,7},{7,5},{8,10},{10,8},{9,1... | collective-permute-start | bytes 786440 | tf_op jit(solution)/shard_map/ppermute | solution.py:561
  67.0 13.2 %collective-permute-start.7 = (bf16[4,128,256]{2,1,0:T(8,128)(2,1)}, bf16[4,128,256]{2,1,0:T(8,128)(2,1)S(1)}, u32[]{:S(2)}, u32[]{:S(2)}) collective-permute-start(bf16[4,128,256]{2,1,0:T(8,128)(2,1)} %get-tuple-element.81), channel_id=1, source_target_pairs={{0,2},{2,0},{1,3},{3,1},{4,6},{6,4},{5,7},{7,5},{8,10},{10,8},{9,1... | collective-permute-start | bytes 786440 | tf_op jit(solution)/shard_map/ppermute | solution.py:561
  82.9 8.6 %collective-permute-start.10 = (bf16[2,128,256]{2,1,0:T(8,128)(2,1)S(1)}, bf16[2,128,256]{2,1,0:T(8,128)(2,1)S(1)}, u32[]{:S(2)}, u32[]{:S(2)}) collective-permute-start(bf16[2,128,256]{2,1,0:T(8,128)(2,1)S(1)} %get-tuple-element.88), channel_id=1, source_target_pairs={{8,0},{16,8},{24,16},{9,1},{17,9},{25,17},{10,2},{18,10},{26,18},{... | collective-permute-start | bytes 393224 | tf_op jit(solution)/shard_map/ppermute | solution.py:763
  84.2 14.2 %collective-permute-start.11 = (bf16[2,128,256]{2,1,0:T(8,128)(2,1)S(1)}, bf16[2,128,256]{2,1,0:T(8,128)(2,1)S(1)}, u32[]{:S(2)}, u32[]{:S(2)}) collective-permute-start(bf16[2,128,256]{2,1,0:T(8,128)(2,1)S(1)} %get-tuple-element.89), channel_id=1, source_target_pairs={{16,0},{24,8},{17,1},{25,9},{18,2},{26,10},{19,3},{27,11},{20,4},{... | collective-permute-start | bytes 393224 | tf_op jit(solution)/shard_map/ppermute | solution.py:763
  85.5 16.8 %collective-permute-start.12 = (bf16[2,128,256]{2,1,0:T(8,128)(2,1)S(1)}, bf16[2,128,256]{2,1,0:T(8,128)(2,1)S(1)}, u32[]{:S(2)}, u32[]{:S(2)}) collective-permute-start(bf16[2,128,256]{2,1,0:T(8,128)(2,1)S(1)} %get-tuple-element.90), channel_id=1, source_target_pairs={{24,0},{25,1},{26,2},{27,3},{28,4},{29,5},{30,6},{31,7}} | collective-permute-start | bytes 393224 | tf_op jit(solution)/shard_map/ppermute | solution.py:763
  110.7 27.1 %copy-start = (bf16[8,1024,128]{2,1,0:T(8,128)(2,1)S(1)}, bf16[8,1024,128]{2,1,0:T(8,128)(2,1)}, u32[]{:S(2)}) copy-start(bf16[8,1024,128]{2,1,0:T(8,128)(2,1)} %all-gather.5.cloned.1.call-done) | copy-start | bytes 6291460
  110.8 4.3 %collective-permute-start.13 = (bf16[128,256]{1,0:T(8,128)(2,1)S(1)}, bf16[128,256]{1,0:T(8,128)(2,1)S(1)}, u32[]{:S(2)}, u32[]{:S(2)}) collective-permute-start(bf16[128,256]{1,0:T(8,128)(2,1)S(1)} %get-tuple-element.92), channel_id=1, source_target_pairs={{0,4},{4,0},{1,5},{5,1},{2,6},{6,2},{3,7},{7,3},{8,12},{12,8},{9,1... | collective-permute-start | bytes 196616 | tf_op jit(solution)/shard_map/ppermute | solution.py:561
  119.8 12.9 %collective-permute-start.15 = (bf16[128,1664]{1,0:T(8,128)(2,1)}, bf16[128,1664]{1,0:T(8,128)(2,1)S(1)}, u32[]{:S(2)}, u32[]{:S(2)}) collective-permute-start(bf16[128,1664]{1,0:T(8,128)(2,1)} %get-tuple-element.98), channel_id=1, source_target_pairs={{0,1},{1,0},{4,5},{5,4},{2,3},{3,2},{6,7},{7,6},{8,9},{9,8},{12,13... | collective-permute-start | bytes 1277960 | tf_op jit(solution)/shard_map/ppermute | solution.py:567
  121.1 12.3 %collective-permute-start.16 = (bf16[128,1664]{1,0:T(8,128)(2,1)}, bf16[128,1664]{1,0:T(8,128)(2,1)S(1)}, u32[]{:S(2)}, u32[]{:S(2)}) collective-permute-start(bf16[128,1664]{1,0:T(8,128)(2,1)} %get-tuple-element.99), channel_id=1, source_target_pairs={{0,4},{1,5},{4,0},{5,1},{2,6},{3,7},{6,2},{7,3},{8,12},{9,13},{12,... | collective-permute-start | bytes 1277960 | tf_op jit(solution)/shard_map/ppermute | solution.py:567
  121.2 16.6 %collective-permute-start.17 = (bf16[128,1664]{1,0:T(8,128)(2,1)}, bf16[128,1664]{1,0:T(8,128)(2,1)S(1)}, u32[]{:S(2)}, u32[]{:S(2)}) collective-permute-start(bf16[128,1664]{1,0:T(8,128)(2,1)} %get-tuple-element.100), channel_id=1, source_target_pairs={{0,5},{1,4},{4,1},{5,0},{2,7},{3,6},{6,3},{7,2},{8,13},{9,12},{12,... | collective-permute-start | bytes 1277960 | tf_op jit(solution)/shard_map/ppermute | solution.py:567
  142.4 2.4 %collective-permute-start.18 = (bf16[4,128,768]{2,1,0:T(8,128)(2,1)S(1)}, bf16[4,128,768]{2,1,0:T(8,128)(2,1)S(1)}, u32[]{:S(2)}, u32[]{:S(2)}) collective-permute-start(bf16[4,128,768]{2,1,0:T(8,128)(2,1)S(1)} %get-tuple-element.103), channel_id=1, source_target_pairs={{0,2},{2,0},{1,3},{3,1},{4,6},{6,4},{5,7},{7,5},{8,10},{10,8},{9,1... | collective-permute-start | bytes 2359304 | tf_op jit(solution)/shard_map/ppermute | solution.py:561
  145.5 19.9 %collective-permute-start.19 = (bf16[2,128,768]{2,1,0:T(8,128)(2,1)S(1)}, bf16[2,128,768]{2,1,0:T(8,128)(2,1)S(1)}, u32[]{:S(2)}, u32[]{:S(2)}) collective-permute-start(bf16[2,128,768]{2,1,0:T(8,128)(2,1)S(1)} %get-tuple-element.105), channel_id=1, source_target_pairs={{0,8},{8,0},{16,24},{24,16},{1,9},{9,1},{17,25},{25,17},{2,10},{10... | collective-permute-start | bytes 1179656 | tf_op jit(solution)/shard_map/ppermute | solution.py:805
  170.6 14.7 %collective-permute-start.26 = (bf16[64,2176]{1,0:T(8,128)(2,1)S(1)}, bf16[64,2176]{1,0:T(8,128)(2,1)S(1)}, u32[]{:S(2)}, u32[]{:S(2)}) collective-permute-start(bf16[64,2176]{1,0:T(8,128)(2,1)S(1)} %get-tuple-element.111), channel_id=1, source_target_pairs={{0,5},{1,4},{4,1},{5,0},{2,7},{3,6},{6,3},{7,2},{8,13},{9,12},{12,... | collective-permute-start | bytes 835592 | tf_op jit(solution)/shard_map/ppermute | solution.py:567
  173.1 9.6 %collective-permute-start.20 = (bf16[1,128,768]{2,1,0:T(8,128)(2,1)S(1)}, bf16[1,128,768]{2,1,0:T(8,128)(2,1)S(1)}, u32[]{:S(2)}, u32[]{:S(2)}) collective-permute-start(bf16[1,128,768]{2,1,0:T(8,128)(2,1)S(1)} %get-tuple-element.107), channel_id=1, source_target_pairs={{0,16},{8,24},{16,0},{24,8},{1,17},{9,25},{17,1},{25,9},{2,18},{10... | collective-permute-start | bytes 589832 | tf_op jit(solution)/shard_map/ppermute | solution.py:805
  173.1 13.8 %collective-permute-start.25 = (bf16[64,2176]{1,0:T(8,128)(2,1)S(1)}, bf16[64,2176]{1,0:T(8,128)(2,1)S(1)}, u32[]{:S(2)}, u32[]{:S(2)}) collective-permute-start(bf16[64,2176]{1,0:T(8,128)(2,1)S(1)} %get-tuple-element.111), channel_id=1, source_target_pairs={{0,4},{1,5},{4,0},{5,1},{2,6},{3,7},{6,2},{7,3},{8,12},{9,13},{12,... | collective-permute-start | bytes 835592 | tf_op jit(solution)/shard_map/ppermute | solution.py:567
  173.6 13.2 %collective-permute-start.24 = (bf16[64,2176]{1,0:T(8,128)(2,1)S(1)}, bf16[64,2176]{1,0:T(8,128)(2,1)S(1)}, u32[]{:S(2)}, u32[]{:S(2)}) collective-permute-start(bf16[64,2176]{1,0:T(8,128)(2,1)S(1)} %get-tuple-element.108.refs_3_.refs_1_), channel_id=1, source_target_pairs={{0,1},{1,0},{4,5},{5,4},{2,3},{3,2},{6,7},{7,6},{8,9},{9,8},{12,13... | collective-permute-start | bytes 835592 | tf_op jit(solution)/shard_map/ppermute | solution.py:567
  183.3 6.6 %collective-permute-start.23 = (bf16[64,768]{1,0:T(8,128)(2,1)S(1)}, bf16[64,768]{1,0:T(8,128)(2,1)S(1)}, u32[]{:S(2)}, u32[]{:S(2)}) collective-permute-start(bf16[64,768]{1,0:T(8,128)(2,1)S(1)} %get-tuple-element.110), channel_id=1, source_target_pairs={{0,5},{1,4},{4,1},{5,0},{2,7},{3,6},{6,3},{7,2},{8,13},{9,12},{12,... | collective-permute-start | bytes 294920 | tf_op jit(solution)/shard_map/ppermute | solution.py:567
  183.7 6.5 %collective-permute-start.22 = (bf16[64,768]{1,0:T(8,128)(2,1)S(1)}, bf16[64,768]{1,0:T(8,128)(2,1)S(1)}, u32[]{:S(2)}, u32[]{:S(2)}) collective-permute-start(bf16[64,768]{1,0:T(8,128)(2,1)S(1)} %get-tuple-element.110), channel_id=1, source_target_pairs={{0,4},{1,5},{4,0},{5,1},{2,6},{3,7},{6,2},{7,3},{8,12},{9,13},{12,... | collective-permute-start | bytes 294920 | tf_op jit(solution)/shard_map/ppermute | solution.py:567
  185.4 5.7 %collective-permute-start.21 = (bf16[64,768]{1,0:T(8,128)(2,1)S(1)}, bf16[64,768]{1,0:T(8,128)(2,1)S(1)}, u32[]{:S(2)}, u32[]{:S(2)}) collective-permute-start(bf16[64,768]{1,0:T(8,128)(2,1)S(1)} %get-tuple-element.109.refs_5_.refs_1_), channel_id=1, source_target_pairs={{0,1},{1,0},{4,5},{5,4},{2,3},{3,2},{6,7},{7,6},{8,9},{9,8},{12,13... | collective-permute-start | bytes 294920 | tf_op jit(solution)/shard_map/ppermute | solution.py:567
  (18 other events, 135.0 us)
Sparse Core Ops, SparseCore 0:
  11.7 40.5 all-gather.4
  54.2 35.2 all-gather.6
  110.9 57.9 reduce-scatter.1

commit v6 on v5

--- a/solution.py
+++ b/solution.py
@@ -513,7 +513,7 @@
             pltpu.SemaphoreType.DMA((len(lefts) + moves, FOUR)),
         ],
         after,
-        14 if nz else 60,
+        60,
     )
 
 
@@ -758,7 +758,7 @@
     )
     pieces = (keep_own, keep_far, swap(send_own, "core"), swap(send_far, "core"))
     if relative:
-        moved = list(kv_cut(sc, pieces, nz - 1, after=parts_a[1:3]))
+        moved = list(kv_cut(sc, pieces, nz - 1, after=parts_a[1:2]))
         for k in range(1, nz):
             moved[k] = lax.ppermute(moved[k], "z", [(i, i - k) for i in range(k, nz)])
         last.append(moved[0])

time: 200 us -> 200 us (level)
  waiting for transfers between devices: 92.5 us -> 87.9 us
  Pallas kernels: 51.8 us -> 54.7 us
    ppermute x2, waiting for transfers between devices: 28.3 us -> 23.3 us  [shards(): came = lax.ppermute(send, 'z', [(i, i ^ 1 << step) for i in range(nz)])]
    ppermute x3, waiting for transfers between devices: 13.8 us -> 16.9 us  [shards(): moved[k] = lax.ppermute(moved[k], 'z', [(i, i - k) for i in range(k, nz)])]
    pallas_call x17, Pallas kernels: 51.8 us -> 54.7 us  [call(): pl.pallas_call(body, out_shape=tuple(outs), in_specs=list(specs) + [ANY]...]
    reduce_scatter x1, waiting for transfers between devices: 2.88 us -> 0.59 us  [shards(): lax.psum_scatter(main, ('z', 'core'), scatter_dimension=0, tiled=True)]
    unnamed x40 -> x42, local copies, waits for them, and re-layouts: 8.7 us -> 8.85 us
  transfers between devices with their start and end apart: 30 -> 30, of which waited for: 19 -> 18; matrix products, arithmetic and copies ran while one was open for 0% -> 0% of each run, Pallas kernels for 19% -> 20%
where the time goes in v6:
time: 200 us
  waiting for transfers between devices  87.9 us (44%)
  Pallas kernels  54.7 us (27%)
  starting transfers between devices  32.6 us (16%)
  between operations  14.1 us (7%)
  local copies, waits for them, and re-layouts  10.1 us (5%)
    pallas_call x17, Pallas kernels, call(): pl.pallas_call(body, out_shape=tuple(outs), in_specs=list(specs) + [ANY]...  54.7 us
    ppermute x12, waiting for transfers between devices, plane_swap(): lax.ppermute(parts[k], PLANE, [(d, d ^ k) for d in range(FOUR)])  28.6 us
    ppermute x2, waiting for transfers between devices, shards(): came = lax.ppermute(send, 'z', [(i, i ^ 1 << step) for i in range(nz)])  23.3 us
    ppermute x7, waiting for transfers between devices, swap(): return lax.ppermute(value, axis, [(0, 1), (1, 0)])  17.1 us
    ppermute x3, waiting for transfers between devices, shards(): moved[k] = lax.ppermute(moved[k], 'z', [(i, i - k) for i in range(k, nz)])  16.9 us
    ppermute x12, starting transfers between devices, plane_swap(): lax.ppermute(parts[k], PLANE, [(d, d ^ k) for d in range(FOUR)])  14.6 us
    ppermute x3, starting transfers between devices, shards(): moved.append(lax.ppermute(kv, 'z', [(i, i + k) for i in range(nz - k)]))  10.7 us
    unnamed x42, local copies, waits for them, and re-layouts  8.85 us
  transfers between devices with their start and end apart: 30, of which 18 were waited for; matrix products, arithmetic and copies ran while one was open for 0% of the time, Pallas kernels for 20%

profile of v6, /device:TPU:0, one launch (start us, length us, event | category | flops | bytes accessed | tf_op | source)
XLA Modules:
  0.0 199.5 jit_solution(14438698318975517568)
XLA Ops:
  7.2 4.4 %enter.1 = (bf16[128,512]{1,0:T(8,128)(2,1)}, bf16[128,256]{1,0:T(8,128)(2,1)}, bf16[2,1024,128]{2,1,0:T(8,128)(2,1)}, bf16[2,128,1024]{2,1,0:T(8,128)(2,1)}) custom-call(bf16[128,1024]{1,0:T(8,128)(2,1)} %bitcast.25, bf16[1024]{0:T(1024)(128)(2,1)} %refs_3_.3, bf16[1024,512]{1,0:T(8,128)(2,1)} %refs_9_.1, bf16[256,256]{1,0:T(8,128)(2,1)} %refs_8_.5, ...), custom_call_target="tpu_custom_call" | custom-call | bytes 36000 | tf_op jit(solution)/shard_map/enter/pallas_call | solution.py:71
  11.7 7.0 %collective-permute-start.2 = (bf16[128,256]{1,0:T(8,128)(2,1)}, bf16[128,256]{1,0:T(8,128)(2,1)S(1)}, u32[]{:S(2)}, u32[]{:S(2)}) collective-permute-start(bf16[128,256]{1,0:T(8,128)(2,1)} %get-tuple-element.66.refs_0_), channel_id=1, source_target_pairs={{0,24},{1,25},{2,26},{3,27},{4,28},{5,29},{6,30},{7,31}} | collective-permute-start | bytes 196616 | tf_op jit(solution)/shard_map/ppermute | solution.py:735
  19.9 2.5 %collective-permute-start = (bf16[128,256]{1,0:T(8,128)(2,1)}, bf16[128,256]{1,0:T(8,128)(2,1)S(1)}, u32[]{:S(2)}, u32[]{:S(2)}) collective-permute-start(bf16[128,256]{1,0:T(8,128)(2,1)} %get-tuple-element.66.refs_0_), channel_id=1, source_target_pairs={{0,8},{8,16},{16,24},{1,9},{9,17},{17,25},{2,10},{10,18},{18,26},{... | collective-permute-start | bytes 196616 | tf_op jit(solution)/shard_map/ppermute | solution.py:735
  23.2 1.4 collective-permute-done.refs_1_
  25.5 1.6 collective-permute-start.3
  27.0 8.9 %collective-permute-done.3.refs_2_ = bf16[4,128,256]{2,1,0:T(8,128)(2,1)S(1)} collective-permute-done((bf16[4,128,256]{2,1,0:T(8,128)(2,1)S(1)}, bf16[4,128,256]{2,1,0:T(8,128)(2,1)S(1)}, u32[]{:S(2)}, u32[]{:S(2)}) %collective-permute-start.3) | collective-permute-done | bytes 262176 | tf_op jit(solution)/shard_map/ppermute | solution.py:561
  35.9 1.5 collective-permute-done.5.refs_4_
  38.1 4.9 %attend.1 = (bf16[2048,256]{1,0:T(8,128)(2,1)}, f32[2,64,1024]{2,1,0:T(8,128)}, f32[2,1,1024]{2,1,0:T(1,128)}, bf16[1024,128]{1,0:T(8,128)(2,1)}, bf16[1024,128]...) custom-call(s32[16]{0:T(128)} %copy-done.10, bf16[4,128,256]{2,1,0:T(8,128)(2,1)} %copy-done.5, ...), custom_call_target="tpu_custom_call" | custom-call | bytes 36000 | tf_op jit(solution)/shard_map/attend/pallas_call | solution.py:71
  43.1 15.7 %feed.1 = (bf16[128,2176]{1,0:T(8,128)(2,1)}, bf16[128,2176]{1,0:T(8,128)(2,1)}, bf16[128,2176]{1,0:T(8,128)(2,1)}, bf16[128,2176]{1,0:T(8,128)(2,1)}, bf16[128,...) custom-call(s32[16]{0:T(128)} %copy-done.10, ...), custom_call_target="tpu_custom_call" | custom-call | bytes 36000 | tf_op jit(solution)/shard_map/feed/pallas_call | solution.py:71
  58.9 1.7 collective-permute-start.8
  62.4 4.6 %attend_back.1 = (bf16[128,1024]{1,0:T(8,128)(2,1)}, bf16[4,128,256]{2,1,0:T(8,128)(2,1)}, bf16[4,128,256]{2,1,0:T(8,128)(2,1)}, bf16[4,128,256]{2,1,0:T(8,128)(2,1)}, bf16[4,128,256]{2,1,0:T(8,128)(2,1)}) custom-call(s32[16]{0:T(128)} %copy-done.10, bf16[2048,256]{1,0:T(8,128)(2,1)} %get-tuple-element.72.refs_1_, ...), custom_call_target="tpu_custom_call" | custom-call | bytes 32400000 | tf_op jit(solution)/shard_map/attend_back/pallas_call | solution.py:71
  67.6 9.1 %collective-permute-done.8.refs_5_.refs_4_ = bf16[128,2176]{1,0:T(8,128)(2,1)S(1)} collective-permute-done((bf16[128,2176]{1,0:T(8,128)(2,1)}, bf16[128,2176]{1,0:T(8,128)(2,1)S(1)}, u32[]{:S(2)}, u32[]{:S(2)}) %collective-permute-start.8) | collective-permute-done | bytes 557088 | tf_op jit(solution)/shard_map/ppermute | solution.py:567
  85.3 5.4 %collective-permute-done.9.refs_1_ = bf16[2,128,256]{2,1,0:T(8,128)(2,1)S(1)} collective-permute-done((bf16[2,128,256]{2,1,0:T(8,128)(2,1)S(1)}, bf16[2,128,256]{2,1,0:T(8,128)(2,1)S(1)}, u32[]{:S(2)}, u32[]{:S(2)}) %collective-permute-start.9) | collective-permute-done | bytes 131104 | tf_op jit(solution)/shard_map/ppermute | solution.py:763
  90.7 3.3 %collective-permute-done.10.refs_2_ = bf16[2,128,256]{2,1,0:T(8,128)(2,1)S(1)} collective-permute-done((bf16[2,128,256]{2,1,0:T(8,128)(2,1)S(1)}, bf16[2,128,256]{2,1,0:T(8,128)(2,1)S(1)}, u32[]{:S(2)}, u32[]{:S(2)}) %collective-permute-start.10) | collective-permute-done | bytes 131104 | tf_op jit(solution)/shard_map/ppermute | solution.py:763
  94.0 8.1 %collective-permute-done.11.refs_3_ = bf16[2,128,256]{2,1,0:T(8,128)(2,1)S(1)} collective-permute-done((bf16[2,128,256]{2,1,0:T(8,128)(2,1)S(1)}, bf16[2,128,256]{2,1,0:T(8,128)(2,1)S(1)}, u32[]{:S(2)}, u32[]{:S(2)}) %collective-permute-start.11) | collective-permute-done | bytes 131104 | tf_op jit(solution)/shard_map/ppermute | solution.py:763
  102.9 7.6 %weight_terms.2.refs_13_ = bf16[1024,2176]{1,0:T(8,128)(2,1)} custom-call(s32[16]{0:T(128)} %copy-done.10, bf16[4,1024,128]{2,1,0:T(8,128)(2,1)} %bitcast.30, bf16[4,2,1024,128]{3,2,1,0:T(8,128)(2,1)} %bitcast.23, bf16[128,2176]{1,0:T(8,128)(2,1)} %get-tuple-element.93.refs_3_, bf16[128,2176]{1,0:T(8,128)(2,1)} %copy-done.3, ...), custom_call_target="tpu_custom_call" | custom-call | bytes 36000 | tf_op jit(solution)/shard_map/weight_terms/pallas_call | solution.py:71
  110.7 4.2 %collective-permute-done.12.refs_12_ = bf16[128,256]{1,0:T(8,128)(2,1)S(1)} collective-permute-done((bf16[128,256]{1,0:T(8,128)(2,1)S(1)}, bf16[128,256]{1,0:T(8,128)(2,1)S(1)}, u32[]{:S(2)}, u32[]{:S(2)}) %collective-permute-start.12) | collective-permute-done | bytes 65568 | tf_op jit(solution)/shard_map/ppermute | solution.py:561
  115.6 4.1 %leave.1 = (bf16[128,1024]{1,0:T(8,128)(2,1)}, bf16[1024,128]{1,0:T(8,128)(2,1)}, bf16[128,1664]{1,0:T(8,128)(2,1)}, bf16[128,1664]{1,0:T(8,128)(2,1)}, bf16[128...) custom-call(s32[16]{0:T(128)} %copy-done.10, bf16[128,1024]{1,0:T(8,128)(2,1)} %bitcast.27, ...), custom_call_target="tpu_custom_call" | custom-call | bytes 36000 | tf_op jit(solution)/shard_map/leave/pallas_call | solution.py:71
  119.7 1.5 collective-permute-start.15
  121.3 1.9 collective-permute-start.17
  123.2 8.6 %collective-permute-done.15.refs_3_ = bf16[128,1664]{1,0:T(8,128)(2,1)S(1)} collective-permute-done((bf16[128,1664]{1,0:T(8,128)(2,1)}, bf16[128,1664]{1,0:T(8,128)(2,1)S(1)}, u32[]{:S(2)}, u32[]{:S(2)}) %collective-permute-start.15) | collective-permute-done | bytes 426016 | tf_op jit(solution)/shard_map/ppermute | solution.py:567
  131.8 2.4 %collective-permute-done.16.refs_4_ = bf16[128,1664]{1,0:T(8,128)(2,1)S(1)} collective-permute-done((bf16[128,1664]{1,0:T(8,128)(2,1)}, bf16[128,1664]{1,0:T(8,128)(2,1)S(1)}, u32[]{:S(2)}, u32[]{:S(2)}) %collective-permute-start.16) | collective-permute-done | bytes 426016 | tf_op jit(solution)/shard_map/ppermute | solution.py:567
  134.1 6.4 %collective-permute-done.17.refs_5_ = bf16[128,1664]{1,0:T(8,128)(2,1)S(1)} collective-permute-done((bf16[128,1664]{1,0:T(8,128)(2,1)}, bf16[128,1664]{1,0:T(8,128)(2,1)S(1)}, u32[]{:S(2)}, u32[]{:S(2)}) %collective-permute-start.17) | collective-permute-done | bytes 426016 | tf_op jit(solution)/shard_map/ppermute | solution.py:567
  141.3 5.5 %weight_terms.3 = (bf16[4,128,768]{2,1,0:T(8,128)(2,1)}, bf16[4,128,768]{2,1,0:T(8,128)(2,1)}) custom-call(s32[16]{0:T(128)} %copy-done.10, bf16[4,2,1024,128]{3,2,1,0:T(8,128)(2,1)} %bitcast.24, bf16[128,1664]{1,0:T(8,128)(2,1)} %get-tuple-element.97.refs_2_, bf16[128,1664]{1,0:T(8,128)(2,1)} %copy-done.14, bf16[128,1664]{1,0:T(8,128)(2,1)} %copy-done.15, ...), custom_call_target="tpu_custom_call" | custom-call | bytes 36000 | tf_op jit(solution)/shard_map/weight_terms/pallas_call | solution.py:71
  146.9 2.5 %collective-permute-done.18.refs_2_ = bf16[4,128,768]{2,1,0:T(8,128)(2,1)S(1)} collective-permute-done((bf16[4,128,768]{2,1,0:T(8,128)(2,1)}, bf16[4,128,768]{2,1,0:T(8,128)(2,1)S(1)}, u32[]{:S(2)}, u32[]{:S(2)}) %collective-permute-start.18) | collective-permute-done | bytes 786464 | tf_op jit(solution)/shard_map/ppermute | solution.py:561
  151.3 15.2 %collective-permute-done.19.refs_2_ = bf16[2,128,768]{2,1,0:T(8,128)(2,1)S(1)} collective-permute-done((bf16[2,128,768]{2,1,0:T(8,128)(2,1)S(1)}, bf16[2,128,768]{2,1,0:T(8,128)(2,1)S(1)}, u32[]{:S(2)}, u32[]{:S(2)}) %collective-permute-start.19) | collective-permute-done | bytes 393248 | tf_op jit(solution)/shard_map/ppermute | solution.py:805
  169.5 2.9 %collective-permute-start.26 = (bf16[64,2176]{1,0:T(8,128)(2,1)S(1)}, bf16[64,2176]{1,0:T(8,128)(2,1)S(1)}, u32[]{:S(2)}, u32[]{:S(2)}) collective-permute-start(bf16[64,2176]{1,0:T(8,128)(2,1)S(1)} %get-tuple-element.111), channel_id=1, source_target_pairs={{0,5},{1,4},{4,1},{5,0},{2,7},{3,6},{6,3},{7,2},{8,13},{9,12},{12,... | collective-permute-start | bytes 835592 | tf_op jit(solution)/shard_map/ppermute | solution.py:567
  174.6 8.1 %collective-permute-done.20 = bf16[1,128,768]{2,1,0:T(8,128)(2,1)S(1)} collective-permute-done((bf16[1,128,768]{2,1,0:T(8,128)(2,1)S(1)}, bf16[1,128,768]{2,1,0:T(8,128)(2,1)S(1)}, u32[]{:S(2)}, u32[]{:S(2)}) %collective-permute-start.20) | collective-permute-done | bytes 196640 | tf_op jit(solution)/shard_map/ppermute | solution.py:805
  183.7 1.7 collective-permute-start.22
  185.4 1.5 collective-permute-start.21
  186.8 2.1 %put.2 = (f32[64,2816]{1,0:T(8,128)}, f32[64,2816]{1,0:T(8,128)}, f32[64,2816]{1,0:T(8,128)}, f32[8,128]{1,0:T(8,128)S(1)}) custom-call(s32[16]{0:T(128)S(1)} %copy-done.12, bf16[64,2176]{1,0:T(8,128)(2,1)S(1)} %get-tuple-element.108.refs_3_.refs_1_, bf16[64,2176]{1,0:T(8,128)(2,1)S(1)} %collective-permute-done.24.refs_2_, ...), custom_call_target="tpu_custom_call" | custom-call | bytes 36000 | tf_op jit(solution)/shard_map/put/pallas_call | solution.py:71
  191.1 1.4 put.3
  (92 shorter events, 27.8 us)
Async XLA Ops:
  7.2 55.3 %all-gather.5.cloned.1.call-start = ((), (), s32[]{:S(2)}) async-start(), calls=%async_computation.2 | async-start | bytes 2621440 | tf_op jit(solution)/shard_map/all_gather | solution.py:730
  11.6 91.3 %all-gather.7.cloned.1.call-start = ((), (), s32[]{:S(2)}) async-start(), calls=%async_computation.3 | async-start | bytes 1310720 | tf_op jit(solution)/shard_map/all_gather | solution.py:746
  11.7 11.5 %collective-permute-start.2 = (bf16[128,256]{1,0:T(8,128)(2,1)}, bf16[128,256]{1,0:T(8,128)(2,1)S(1)}, u32[]{:S(2)}, u32[]{:S(2)}) collective-permute-start(bf16[128,256]{1,0:T(8,128)(2,1)} %get-tuple-element.66.refs_0_), channel_id=1, source_target_pairs={{0,24},{1,25},{2,26},{3,27},{4,28},{5,29},{6,30},{7,31}} | collective-permute-start | bytes 196616 | tf_op jit(solution)/shard_map/ppermute | solution.py:735
  18.6 4.5 %collective-permute-start.1 = (bf16[128,256]{1,0:T(8,128)(2,1)}, bf16[128,256]{1,0:T(8,128)(2,1)S(1)}, u32[]{:S(2)}, u32[]{:S(2)}) collective-permute-start(bf16[128,256]{1,0:T(8,128)(2,1)} %get-tuple-element.66.refs_0_), channel_id=1, source_target_pairs={{0,16},{8,24},{1,17},{9,25},{2,18},{10,26},{3,19},{11,27},{4,20},{... | collective-permute-start | bytes 196616 | tf_op jit(solution)/shard_map/ppermute | solution.py:735
  19.9 4.7 %collective-permute-start = (bf16[128,256]{1,0:T(8,128)(2,1)}, bf16[128,256]{1,0:T(8,128)(2,1)S(1)}, u32[]{:S(2)}, u32[]{:S(2)}) collective-permute-start(bf16[128,256]{1,0:T(8,128)(2,1)} %get-tuple-element.66.refs_0_), channel_id=1, source_target_pairs={{0,8},{8,16},{16,24},{1,9},{9,17},{17,25},{2,10},{10,18},{18,26},{... | collective-permute-start | bytes 196616 | tf_op jit(solution)/shard_map/ppermute | solution.py:735
  25.5 10.4 %collective-permute-start.3 = (bf16[4,128,256]{2,1,0:T(8,128)(2,1)S(1)}, bf16[4,128,256]{2,1,0:T(8,128)(2,1)S(1)}, u32[]{:S(2)}, u32[]{:S(2)}) collective-permute-start(bf16[4,128,256]{2,1,0:T(8,128)(2,1)S(1)} %stack.24.refs_1_), channel_id=1, source_target_pairs={{0,4},{4,0},{1,5},{5,1},{2,6},{6,2},{3,7},{7,3},{8,12},{12,8},{9,1... | collective-permute-start | bytes 786440 | tf_op jit(solution)/shard_map/ppermute | solution.py:561
  27.0 8.9 %collective-permute-start.4 = (bf16[4,128,256]{2,1,0:T(8,128)(2,1)S(1)}, bf16[4,128,256]{2,1,0:T(8,128)(2,1)S(1)}, u32[]{:S(2)}, u32[]{:S(2)}) collective-permute-start(bf16[4,128,256]{2,1,0:T(8,128)(2,1)S(1)} %stack.24.refs_1_), channel_id=1, source_target_pairs={{0,2},{2,0},{1,3},{3,1},{4,6},{6,4},{5,7},{7,5},{8,10},{10,8},{9,1... | collective-permute-start | bytes 786440 | tf_op jit(solution)/shard_map/ppermute | solution.py:561
  35.9 1.5 collective-permute-start.5
  43.0 124.8 %reduce-scatter.2.cloned.1.call-start = ((), (), s32[]{:S(2)}) async-start(), calls=%async_computation.1 | async-start | bytes 5013504 | tf_op jit(solution)/shard_map/reduce_scatter | solution.py:781
  58.9 17.8 %collective-permute-start.8 = (bf16[128,2176]{1,0:T(8,128)(2,1)}, bf16[128,2176]{1,0:T(8,128)(2,1)S(1)}, u32[]{:S(2)}, u32[]{:S(2)}) collective-permute-start(bf16[128,2176]{1,0:T(8,128)(2,1)} %get-tuple-element.82), channel_id=1, source_target_pairs={{0,1},{1,0},{4,5},{5,4},{2,3},{3,2},{6,7},{7,6},{8,9},{9,8},{12,13... | collective-permute-start | bytes 1671176 | tf_op jit(solution)/shard_map/ppermute | solution.py:567
  60.5 42.4 %collective-permute-start.13 = (bf16[128,2176]{1,0:T(8,128)(2,1)}, bf16[128,2176]{1,0:T(8,128)(2,1)}, u32[]{:S(2)}, u32[]{:S(2)}) collective-permute-start(bf16[128,2176]{1,0:T(8,128)(2,1)} %get-tuple-element.94), channel_id=1, source_target_pairs={{0,4},{1,5},{4,0},{5,1},{2,6},{3,7},{6,2},{7,3},{8,12},{9,13},{12,... | collective-permute-start | bytes 1671176 | tf_op jit(solution)/shard_map/ppermute | solution.py:567
  61.9 41.0 %collective-permute-start.14 = (bf16[128,2176]{1,0:T(8,128)(2,1)}, bf16[128,2176]{1,0:T(8,128)(2,1)}, u32[]{:S(2)}, u32[]{:S(2)}) collective-permute-start(bf16[128,2176]{1,0:T(8,128)(2,1)} %get-tuple-element.95), channel_id=1, source_target_pairs={{0,5},{1,4},{4,1},{5,0},{2,7},{3,6},{6,3},{7,2},{8,13},{9,12},{12,... | collective-permute-start | bytes 1671176 | tf_op jit(solution)/shard_map/ppermute | solution.py:567
  67.0 9.7 %collective-permute-start.6 = (bf16[4,128,256]{2,1,0:T(8,128)(2,1)}, bf16[4,128,256]{2,1,0:T(8,128)(2,1)S(1)}, u32[]{:S(2)}, u32[]{:S(2)}) collective-permute-start(bf16[4,128,256]{2,1,0:T(8,128)(2,1)} %get-tuple-element.80), channel_id=1, source_target_pairs={{0,2},{2,0},{1,3},{3,1},{4,6},{6,4},{5,7},{7,5},{8,10},{10,8},{9,1... | collective-permute-start | bytes 786440 | tf_op jit(solution)/shard_map/ppermute | solution.py:561
  67.1 9.7 %collective-permute-start.7 = (bf16[4,128,256]{2,1,0:T(8,128)(2,1)}, bf16[4,128,256]{2,1,0:T(8,128)(2,1)S(1)}, u32[]{:S(2)}, u32[]{:S(2)}) collective-permute-start(bf16[4,128,256]{2,1,0:T(8,128)(2,1)} %get-tuple-element.81), channel_id=1, source_target_pairs={{0,2},{2,0},{1,3},{3,1},{4,6},{6,4},{5,7},{7,5},{8,10},{10,8},{9,1... | collective-permute-start | bytes 786440 | tf_op jit(solution)/shard_map/ppermute | solution.py:561
  76.7 26.2 %copy-start.3 = (bf16[128,2176]{1,0:T(8,128)(2,1)}, bf16[128,2176]{1,0:T(8,128)(2,1)S(1)}, u32[]{:S(2)}) copy-start(bf16[128,2176]{1,0:T(8,128)(2,1)S(1)} %collective-permute-done.8.refs_5_.refs_4_) | copy-start | bytes 1671172
  79.6 11.1 %collective-permute-start.9 = (bf16[2,128,256]{2,1,0:T(8,128)(2,1)S(1)}, bf16[2,128,256]{2,1,0:T(8,128)(2,1)S(1)}, u32[]{:S(2)}, u32[]{:S(2)}) collective-permute-start(bf16[2,128,256]{2,1,0:T(8,128)(2,1)S(1)} %get-tuple-element.87), channel_id=1, source_target_pairs={{8,0},{16,8},{24,16},{9,1},{17,9},{25,17},{10,2},{18,10},{26,18},{... | collective-permute-start | bytes 393224 | tf_op jit(solution)/shard_map/ppermute | solution.py:763
  80.9 13.1 %collective-permute-start.10 = (bf16[2,128,256]{2,1,0:T(8,128)(2,1)S(1)}, bf16[2,128,256]{2,1,0:T(8,128)(2,1)S(1)}, u32[]{:S(2)}, u32[]{:S(2)}) collective-permute-start(bf16[2,128,256]{2,1,0:T(8,128)(2,1)S(1)} %get-tuple-element.88), channel_id=1, source_target_pairs={{16,0},{24,8},{17,1},{25,9},{18,2},{26,10},{19,3},{27,11},{20,4},{... | collective-permute-start | bytes 393224 | tf_op jit(solution)/shard_map/ppermute | solution.py:763
  82.2 20.0 %collective-permute-start.11 = (bf16[2,128,256]{2,1,0:T(8,128)(2,1)S(1)}, bf16[2,128,256]{2,1,0:T(8,128)(2,1)S(1)}, u32[]{:S(2)}, u32[]{:S(2)}) collective-permute-start(bf16[2,128,256]{2,1,0:T(8,128)(2,1)S(1)} %get-tuple-element.89), channel_id=1, source_target_pairs={{24,0},{25,1},{26,2},{27,3},{28,4},{29,5},{30,6},{31,7}} | collective-permute-start | bytes 393224 | tf_op jit(solution)/shard_map/ppermute | solution.py:763
  110.6 4.3 %collective-permute-start.12 = (bf16[128,256]{1,0:T(8,128)(2,1)S(1)}, bf16[128,256]{1,0:T(8,128)(2,1)S(1)}, u32[]{:S(2)}, u32[]{:S(2)}) collective-permute-start(bf16[128,256]{1,0:T(8,128)(2,1)S(1)} %get-tuple-element.91), channel_id=1, source_target_pairs={{0,4},{4,0},{1,5},{5,1},{2,6},{6,2},{3,7},{7,3},{8,12},{12,8},{9,1... | collective-permute-start | bytes 196616 | tf_op jit(solution)/shard_map/ppermute | solution.py:561
  115.6 33.8 %copy-start.12 = (s32[16]{0:T(128)S(1)}, s32[16]{0:T(128)}, u32[]{:S(2)}) copy-start(s32[16]{0:T(128)} %copy-done.10) | copy-start | bytes 196
  119.7 12.1 %collective-permute-start.15 = (bf16[128,1664]{1,0:T(8,128)(2,1)}, bf16[128,1664]{1,0:T(8,128)(2,1)S(1)}, u32[]{:S(2)}, u32[]{:S(2)}) collective-permute-start(bf16[128,1664]{1,0:T(8,128)(2,1)} %get-tuple-element.98), channel_id=1, source_target_pairs={{0,1},{1,0},{4,5},{5,4},{2,3},{3,2},{6,7},{7,6},{8,9},{9,8},{12,13... | collective-permute-start | bytes 1277960 | tf_op jit(solution)/shard_map/ppermute | solution.py:567
  121.2 13.0 %collective-permute-start.16 = (bf16[128,1664]{1,0:T(8,128)(2,1)}, bf16[128,1664]{1,0:T(8,128)(2,1)S(1)}, u32[]{:S(2)}, u32[]{:S(2)}) collective-permute-start(bf16[128,1664]{1,0:T(8,128)(2,1)} %get-tuple-element.99), channel_id=1, source_target_pairs={{0,4},{1,5},{4,0},{5,1},{2,6},{3,7},{6,2},{7,3},{8,12},{9,13},{12,... | collective-permute-start | bytes 1277960 | tf_op jit(solution)/shard_map/ppermute | solution.py:567
  121.3 19.2 %collective-permute-start.17 = (bf16[128,1664]{1,0:T(8,128)(2,1)}, bf16[128,1664]{1,0:T(8,128)(2,1)S(1)}, u32[]{:S(2)}, u32[]{:S(2)}) collective-permute-start(bf16[128,1664]{1,0:T(8,128)(2,1)} %get-tuple-element.100), channel_id=1, source_target_pairs={{0,5},{1,4},{4,1},{5,0},{2,7},{3,6},{6,3},{7,2},{8,13},{9,12},{12,... | collective-permute-start | bytes 1277960 | tf_op jit(solution)/shard_map/ppermute | solution.py:567
  146.8 2.6 %collective-permute-start.18 = (bf16[4,128,768]{2,1,0:T(8,128)(2,1)}, bf16[4,128,768]{2,1,0:T(8,128)(2,1)S(1)}, u32[]{:S(2)}, u32[]{:S(2)}) collective-permute-start(bf16[4,128,768]{2,1,0:T(8,128)(2,1)} %get-tuple-element.103), channel_id=1, source_target_pairs={{0,2},{2,0},{1,3},{3,1},{4,6},{6,4},{5,7},{7,5},{8,10},{10,8},{9,1... | collective-permute-start | bytes 2359304 | tf_op jit(solution)/shard_map/ppermute | solution.py:561
  151.2 15.3 %collective-permute-start.19 = (bf16[2,128,768]{2,1,0:T(8,128)(2,1)S(1)}, bf16[2,128,768]{2,1,0:T(8,128)(2,1)S(1)}, u32[]{:S(2)}, u32[]{:S(2)}) collective-permute-start(bf16[2,128,768]{2,1,0:T(8,128)(2,1)S(1)} %get-tuple-element.105), channel_id=1, source_target_pairs={{0,8},{8,0},{16,24},{24,16},{1,9},{9,1},{17,25},{25,17},{2,10},{10... | collective-permute-start | bytes 1179656 | tf_op jit(solution)/shard_map/ppermute | solution.py:805
  169.5 15.8 %collective-permute-start.26 = (bf16[64,2176]{1,0:T(8,128)(2,1)S(1)}, bf16[64,2176]{1,0:T(8,128)(2,1)S(1)}, u32[]{:S(2)}, u32[]{:S(2)}) collective-permute-start(bf16[64,2176]{1,0:T(8,128)(2,1)S(1)} %get-tuple-element.111), channel_id=1, source_target_pairs={{0,5},{1,4},{4,1},{5,0},{2,7},{3,6},{6,3},{7,2},{8,13},{9,12},{12,... | collective-permute-start | bytes 835592 | tf_op jit(solution)/shard_map/ppermute | solution.py:567
  172.4 10.2 %collective-permute-start.20 = (bf16[1,128,768]{2,1,0:T(8,128)(2,1)S(1)}, bf16[1,128,768]{2,1,0:T(8,128)(2,1)S(1)}, u32[]{:S(2)}, u32[]{:S(2)}) collective-permute-start(bf16[1,128,768]{2,1,0:T(8,128)(2,1)S(1)} %get-tuple-element.107), channel_id=1, source_target_pairs={{0,16},{8,24},{16,0},{24,8},{1,17},{9,25},{17,1},{25,9},{2,18},{10... | collective-permute-start | bytes 589832 | tf_op jit(solution)/shard_map/ppermute | solution.py:805
  173.5 13.4 %collective-permute-start.25 = (bf16[64,2176]{1,0:T(8,128)(2,1)S(1)}, bf16[64,2176]{1,0:T(8,128)(2,1)S(1)}, u32[]{:S(2)}, u32[]{:S(2)}) collective-permute-start(bf16[64,2176]{1,0:T(8,128)(2,1)S(1)} %get-tuple-element.111), channel_id=1, source_target_pairs={{0,4},{1,5},{4,0},{5,1},{2,6},{3,7},{6,2},{7,3},{8,12},{9,13},{12,... | collective-permute-start | bytes 835592 | tf_op jit(solution)/shard_map/ppermute | solution.py:567
  174.0 12.8 %collective-permute-start.24 = (bf16[64,2176]{1,0:T(8,128)(2,1)S(1)}, bf16[64,2176]{1,0:T(8,128)(2,1)S(1)}, u32[]{:S(2)}, u32[]{:S(2)}) collective-permute-start(bf16[64,2176]{1,0:T(8,128)(2,1)S(1)} %get-tuple-element.108.refs_3_.refs_1_), channel_id=1, source_target_pairs={{0,1},{1,0},{4,5},{5,4},{2,3},{3,2},{6,7},{7,6},{8,9},{9,8},{12,13... | collective-permute-start | bytes 835592 | tf_op jit(solution)/shard_map/ppermute | solution.py:567
  183.3 6.6 %collective-permute-start.23 = (bf16[64,768]{1,0:T(8,128)(2,1)S(1)}, bf16[64,768]{1,0:T(8,128)(2,1)S(1)}, u32[]{:S(2)}, u32[]{:S(2)}) collective-permute-start(bf16[64,768]{1,0:T(8,128)(2,1)S(1)} %get-tuple-element.110), channel_id=1, source_target_pairs={{0,5},{1,4},{4,1},{5,0},{2,7},{3,6},{6,3},{7,2},{8,13},{9,12},{12,... | collective-permute-start | bytes 294920 | tf_op jit(solution)/shard_map/ppermute | solution.py:567
  183.7 6.5 %collective-permute-start.22 = (bf16[64,768]{1,0:T(8,128)(2,1)S(1)}, bf16[64,768]{1,0:T(8,128)(2,1)S(1)}, u32[]{:S(2)}, u32[]{:S(2)}) collective-permute-start(bf16[64,768]{1,0:T(8,128)(2,1)S(1)} %get-tuple-element.110), channel_id=1, source_target_pairs={{0,4},{1,5},{4,0},{5,1},{2,6},{3,7},{6,2},{7,3},{8,12},{9,13},{12,... | collective-permute-start | bytes 294920 | tf_op jit(solution)/shard_map/ppermute | solution.py:567
  185.4 5.7 %collective-permute-start.21 = (bf16[64,768]{1,0:T(8,128)(2,1)S(1)}, bf16[64,768]{1,0:T(8,128)(2,1)S(1)}, u32[]{:S(2)}, u32[]{:S(2)}) collective-permute-start(bf16[64,768]{1,0:T(8,128)(2,1)S(1)} %get-tuple-element.109.refs_5_.refs_1_), channel_id=1, source_target_pairs={{0,1},{1,0},{4,5},{5,4},{2,3},{3,2},{6,7},{7,6},{8,9},{9,8},{12,13... | collective-permute-start | bytes 294920 | tf_op jit(solution)/shard_map/ppermute | solution.py:567
  (19 other events, 121.1 us)
Sparse Core Ops, SparseCore 0:
  11.7 40.5 all-gather.4
  54.2 35.2 all-gather.6
  110.7 57.0 reduce-scatter.1
